TPU v7x, 256 devices: a whole 4x4x8 slice. The times are simulated.
256 devices in a mesh: segment: 4 (over z_hi, core), ctx: 16 (over x, z_lo), dp: 4 (over y).
Axes of the slice: x: 4, y: 4, z: 8 (z_hi: 2, z_lo: 4; z = z_hi * 4 + z_lo), core: 2. Of those that a mesh axis runs over, the one named last changes fastest.
Arguments:
- qkv: bfloat16 [4, 4, 2560, 3, 2560], P('segment', 'dp', 'ctx'), may hold values from -24 to 24
- qk_gain: float32 [4, 2, 2560], P('segment'), may hold values from 1.5 to 2.5
- mod_weight: float32 [4, 256, 2560], P('segment'), may hold values from -0.375 to 0.375
- positions: int32 [4, 2560], P('dp', 'ctx'), may hold values from 0 to 75599
- timesteps: int32 [4, 4], P('segment', 'dp'), may hold values from 0 to 999
- cotangent: bfloat16 [4, 4, 2560, 2560], P('segment', 'dp', 'ctx'), may hold values from -6 to 6
Outputs:
- attn_out: bfloat16 [4, 4, 2560, 2560], P('segment', 'dp', 'ctx')
- gate_grad: float32 [4, 256, 2560], P('segment', ('ctx', 'dp'))
All inputs are finite; a program needn't handle non-finite values.
Results may differ from a plain program's by a relative error of at most 0.012.
Values may be sent and summed in bfloat16 or wider, within the bound.
No kernel may reach another device: no remote copies, remote signals or barrier semaphores. Data moves between devices by JAX's collectives and lax.ppermute only.
A program may use at most 128 MiB of HBM per device.

v0:
```python
import functools

import jax
import jax.numpy as jnp
import numpy as np
from jax import lax
from jax.experimental import pallas as pl
from jax.experimental.pallas import tpu as pltpu
from jax.sharding import PartitionSpec as P

HEADS = 20
HEAD_DIM = 128
FREQS = 256
GRID_ROWS = 45
GRID_COLS = 80
SIDE = 4
GROUP = HEADS // SIDE
TOK = 160
ROWS = SIDE * TOK
WIDTH = HEADS * HEAD_DIM
TILE = 320
EXP_SCALE = 1.4426950408889634 / HEAD_DIM**0.5
VMEM = pltpu.CompilerParams(vmem_limit_bytes=56 * 1024 * 1024)
SMEM_SPEC = pl.BlockSpec(memory_space=pltpu.SMEM)
VMEM_SPEC = pl.BlockSpec(memory_space=pltpu.VMEM)


def along_z(value, by):
    pairs = [(i, i // SIDE * SIDE + (i + by) % SIDE) for i in range(SIDE * SIDE)]
    return lax.ppermute(value, "ctx", pairs)


def along_x(value, by):
    pairs = [(i, (i + SIDE * by) % (SIDE * SIDE)) for i in range(SIDE * SIDE)]
    return lax.ppermute(value, "ctx", pairs)


def along_dp(value, by):
    return lax.ppermute(value, "dp", [(i, (i + by) % SIDE) for i in range(SIDE)])


def exchanged(along, blocks):
    got = list(blocks)
    for k in (2, 1, 3):
        got[k] = along(blocks[k], k)
    return got


def section_pairs(turn, by):
    count = SIDE * SIDE
    pairs = []
    for seg in range(SIDE):
        for i in range(count):
            target = (seg + turn) % SIDE * count + i // SIDE * SIDE + (i + by) % SIDE
            pairs.append((seg * count + i, target))
    return pairs


def home(value, by):
    return lax.ppermute(value, ("segment", "ctx"), section_pairs(1, by))


def away(value, by):
    return lax.ppermute(value, ("segment", "ctx"), section_pairs(SIDE - 1, by))


def rope_tables(pos):
    half = HEAD_DIM // 2
    side = HEAD_DIM // 6
    first = half - 2 * side
    frame = (pos // (GRID_ROWS * GRID_COLS)).astype(jnp.float32)
    row = (pos // GRID_COLS % GRID_ROWS).astype(jnp.float32)
    col = (pos % GRID_COLS).astype(jnp.float32)
    pair = np.arange(half)
    group = np.where(pair < first, 0, np.where(pair < first + side, 1, 2))
    offset = np.where(group == 0, 0, np.where(group == 1, first, first + side))
    pairs_in = np.where(group == 0, first, side)
    freq = (10000.0 ** (-(pair - offset) / pairs_in)).astype(np.float32)
    coord = jnp.where(
        group[None, :] == 0,
        frame[:, None],
        jnp.where(group[None, :] == 1, row[:, None], col[:, None]),
    )
    angle = coord * freq[None, :]
    cosine = jnp.concatenate([jnp.cos(angle), jnp.cos(angle)], axis=1)
    sine = jnp.concatenate([-jnp.sin(angle), jnp.sin(angle)], axis=1)
    return (cosine, sine)


def one_of(which, dims):
    return pl.BlockSpec((1, *dims), lambda i: (which, 0, 0))


def call(kernel, out_shape, flops, moved, *operands, smem=1, specs=None):
    grid = () if specs is None else (1,)
    specs = specs or [SMEM_SPEC] * smem + [VMEM_SPEC] * (len(operands) - smem)
    return pl.pallas_call(
        kernel,
        grid=grid,
        out_shape=out_shape,
        in_specs=specs,
        out_specs=jax.tree.map(lambda _: VMEM_SPEC, out_shape),
        compiler_params=VMEM,
        cost_estimate=pl.CostEstimate(flops=0, bytes_accessed=0, transcendentals=0),
    )(*operands)


def group_columns(index):
    wide = GROUP * HEAD_DIM
    return pl.ds(pl.multiple_of(lax.rem(index, SIDE) * wide, HEAD_DIM), wide)


def after(value, first):
    return lax.optimization_barrier((value, first))[0]


def column(index):
    return pl.ds(pl.multiple_of(index * HEAD_DIM, HEAD_DIM), HEAD_DIM)


def prep_kernel(z_ref, qkv_ref, gain_ref, cos_ref, sin_ref, main_ref, *shared):
    z = z_ref[0]
    cosine = cos_ref[...]
    sine = sin_ref[...]
    for part in range(3):
        if part < 2:
            total = jnp.zeros((TOK, HEAD_DIM), jnp.float32)
            for head in range(HEADS):
                x = qkv_ref[part, :, head * HEAD_DIM : (head + 1) * HEAD_DIM].astype(jnp.float32)
                total = total + x * x
            mean_sq = jnp.sum(total, axis=1, keepdims=True) / WIDTH
            inverse = lax.rsqrt(mean_sq + 1e-06)

        def head_of(cols):
            x = qkv_ref[part, :, cols]
            if part == 2:
                return x
            y = x.astype(jnp.float32) * inverse * gain_ref[part : part + 1, cols]
            turned = pltpu.roll(y, HEAD_DIM // 2, 1)
            return (y * cosine + turned * sine).astype(jnp.bfloat16)

        for step in range(SIDE):
            shared[step][part] = head_of(column(lax.rem(z + step, SIDE) * GROUP + GROUP - 1))
        for to_x in range(SIDE):
            for to_z in range(SIDE):
                at = (to_z * GROUP + to_x) * HEAD_DIM
                main_ref[to_x * SIDE + to_z, part] = head_of(slice(at, at + HEAD_DIM))


def cut_cotangent_kernel(z_ref, cot_ref, *outs):
    z = z_ref[0]
    for step in range(SIDE):
        outs[step][...] = cot_ref[:, group_columns(z + step)]


def attend(q, keys, values):
    nt = (((1,), (1,)), ((), ()))
    scores = [lax.dot_general(q, k, nt, preferred_element_type=jnp.float32) for k in keys]
    peak = functools.reduce(jnp.maximum, [jnp.max(s, axis=1, keepdims=True) for s in scores])
    expo = [jnp.exp2((s - peak) * EXP_SCALE) for s in scores]
    total = sum(jnp.sum(e, axis=1, keepdims=True) for e in expo)
    accum = sum(
        jnp.dot(e.astype(jnp.bfloat16), v, preferred_element_type=jnp.float32)
        for e, v in zip(expo, values, strict=True)
    )
    return (accum / total).astype(jnp.bfloat16)


def shared_kernel(q0, q1, q2, q3, s0, s1, s2, s3, out_ref):
    blocks = (s0, s1, s2, s3)
    for pair in ((q0, q1), (q2, q3)):
        at = 0 if pair[0] is q0 else TILE
        q = jnp.concatenate([p[0] for p in pair])
        out_ref[at : at + TILE] = attend(q, [b[0] for b in blocks], [b[1] for b in blocks])


def main_kernel(back, x_ref, r_ref, *outs):
    x = x_ref[0]

    def four(part, first):
        return r_ref[pl.ds(first * SIDE, SIDE), part].reshape(ROWS, HEAD_DIM)

    keys = [four(1, m) for m in range(SIDE)]
    values = [four(2, m) for m in range(SIDE)]
    for step, out_ref in zip(back, outs, strict=True):
        first = lax.rem(x + SIDE - step, SIDE) * SIDE
        for i in range(ROWS // TILE):
            half = SIDE // 2
            q = r_ref[pl.ds(first + i * half, half), 0].reshape(TILE, HEAD_DIM)
            out_ref[i * TILE : (i + 1) * TILE] = attend(q, keys, values)


def rows_of(z, source, step):
    first = lax.rem(z + SIDE - step, SIDE) if source < SIDE else step
    return pl.ds(pl.multiple_of(first * TOK, 32), TOK)


def join_kernel(place_ref, *refs):
    x, z = place_ref[0], place_ref[1]
    outs = refs[GROUP:]
    for source in range(GROUP):
        place = lax.rem(x + source, SIDE) if source < SIDE else SIDE
        for step in range(SIDE):
            outs[step][:, column(place)] = refs[source][rows_of(z, source, step)]


def channels_kernel(place_ref, time_ref, *refs):
    x, z = place_ref[0], place_ref[1]
    cots = refs[GROUP : GROUP + SIDE]
    out_ref, chan_ref = refs[GROUP + SIDE :]
    chan_ref[...] = jnp.zeros_like(chan_ref)
    for source in range(GROUP):
        place = lax.rem(x + source, SIDE) if source < SIDE else SIDE
        total = jnp.zeros((TOK, HEAD_DIM), jnp.float32)
        for step in range(SIDE):
            attn = refs[source][rows_of(z, source, step)].astype(jnp.float32)
            total = total + attn * cots[step][:, column(place)].astype(jnp.float32)
        chan_ref[pl.ds(place, 1)] = jnp.sum(total, axis=0, keepdims=True)
    chan_ref[GROUP : GROUP + 1] = time_ref[2:3, :HEAD_DIM]
    for i in range(out_ref.shape[0]):
        out_ref[i] = chan_ref[...]


def finish_kernel(z_ref, a0, a1, a2, a3, gate_ref, out_ref):
    z = z_ref[0]
    for step, a in enumerate((a0, a1, a2, a3)):
        cols = group_columns(z + step)
        out_ref[:, cols] = (a[...].astype(jnp.float32) * gate_ref[:, cols]).astype(jnp.bfloat16)


def grad_kernel(index_ref, freq_ref, before_ref, chan_ref, out_ref):
    is_cosine = index_ref[0] < FREQS // 2
    factors = []
    for d in range(SIDE):
        angle = chan_ref[d, GROUP : GROUP + 1] * freq_ref[...]
        factors.append(jnp.where(is_cosine, jnp.cos(angle), jnp.sin(angle)))
    for z in range(SIDE):
        chans = [sum(chan_ref[(x * SIDE + z) * SIDE + d] for x in range(SIDE)) for d in range(SIDE)]
        for head in range(GROUP):
            total = sum(f * c[head : head + 1] for f, c in zip(factors, chans, strict=True))
            at = (z * GROUP + head) * HEAD_DIM
            cols = slice(at, at + HEAD_DIM)
            out_ref[:, cols] = before_ref[:, cols] + total


def shape(dims, dtype=jnp.bfloat16):
    return jax.ShapeDtypeStruct(dims, dtype)


def frequencies():
    count = FREQS // 2
    return (10000.0 ** (-np.arange(count) / count)).astype(np.float32)


def embed(step):
    angle = step.astype(jnp.float32) * frequencies()
    return jnp.concatenate([jnp.cos(angle), jnp.sin(angle)])


def local(qkv, qk_gain, mod_weight, positions, timesteps, cotangent):
    ctx = lax.axis_index("ctx").astype(jnp.int32)
    x = (ctx // SIDE)[None]
    z = (ctx % SIDE)[None]
    steps = (1, 2, 3)
    place = jnp.concatenate([x, z])
    count = SIDE * SIDE
    block = shape((3, TOK, HEAD_DIM))
    single = shape((ROWS, HEAD_DIM))
    flat = shape((TOK, GROUP * HEAD_DIM))

    step = timesteps[0, 0]
    when = jnp.full((1, WIDTH), step.astype(jnp.float32))
    gains = jnp.concatenate([qk_gain[0], when])
    gains = lax.ppermute(gains, "segment", [((i + 1) % SIDE, i) for i in range(SIDE)])
    parts = qkv[0, 0].transpose(1, 0, 2)
    cots = call(cut_cotangent_kernel, [flat] * SIDE, 0, 1_600_000, z, cotangent[0, 0])
    cots_z = [None] * SIDE
    for k in (2, 1, 3, 0):
        cots_z[k] = away(cots[k], k)
    cosine, sine = rope_tables(positions[0])
    main, *shared = call(
        prep_kernel,
        [shape((count, 3, TOK, HEAD_DIM))] + [block] * SIDE,
        10_000_000,
        5_000_000,
        z,
        parts,
        gains,
        cosine,
        sine,
    )
    shared_z = exchanged(along_z, shared)
    main = lax.all_to_all(after(main, cots_z), "ctx", 0, 0)
    pair = jnp.concatenate([b[1:] for b in shared_z], axis=1)
    pairs = [pair] + [along_x(pair, k) for k in steps]
    gate = jnp.dot(embed(step), mod_weight[0], precision=lax.Precision.HIGHEST)[None]
    rows = FREQS // (SIDE * SIDE * SIDE)
    index = (ctx * SIDE + lax.axis_index("dp").astype(jnp.int32)) * rows
    freq = lax.dynamic_slice_in_dim(np.tile(frequencies(), 2), index, rows)
    freq = jnp.broadcast_to(freq[:, None], (rows, HEAD_DIM))
    shared_out = call(
        shared_kernel, single, 840_000_000, 1_600_000, *shared_z, *pairs, smem=0
    )
    main, gate, freq, shared_out = lax.optimization_barrier((main, gate, freq, shared_out))
    back = [None] * SIDE
    back[2], back[1], back[3] = call(
        functools.partial(main_kernel, (2, 1, 3)), [single] * 3, 2_500_000_000, 2_500_000, x, main
    )
    (back[0],) = call(
        functools.partial(main_kernel, (0,)), [single], 840_000_000, 2_000_000, x, main
    )
    back = [back[0]] + [along_x(back[m], SIDE - m) for m in steps]
    joined = call(join_kernel, [flat] * SIDE, 0, 1_600_000, place, *back, shared_out)
    at_home = [None] * SIDE
    for k in (2, 1, 3, 0):
        at_home[k] = home(joined[k], (SIDE - k) % SIDE)

    def gradient(_, before):
        attn, before = lax.optimization_barrier(([*back, shared_out], before))
        chans = pl.pallas_call(
            channels_kernel,
            out_shape=shape((SIDE * count, 8, HEAD_DIM), jnp.float32),
            in_specs=[SMEM_SPEC] + [VMEM_SPEC] * (1 + GROUP + SIDE),
            out_specs=VMEM_SPEC,
            scratch_shapes=[pltpu.VMEM((8, HEAD_DIM), jnp.float32)],
            compiler_params=VMEM,
            cost_estimate=pl.CostEstimate(flops=0, bytes_accessed=0, transcendentals=0),
        )(place, gains, *attn, *cots_z)
        chans = lax.all_to_all(chans, ("ctx", "dp"), 0, 0)
        return call(grad_kernel, zeros, 0, 200_000, index[None], freq, before, chans)

    zeros = shape((rows, WIDTH), jnp.float32)
    turns = jnp.where(step < 1000, 1, 2)
    grad = lax.fori_loop(0, turns, gradient, jnp.zeros((rows, WIDTH), jnp.float32))
    grad = lax.ppermute(grad, "segment", [(i, (i + 1) % SIDE) for i in range(SIDE)])

    attn_out = call(
        finish_kernel, shape((TOK, WIDTH)), 500_000, 1_700_000, z, *at_home, gate
    )
    return (attn_out[None, None], grad[None])


def solution(mesh):
    return jax.shard_map(
        local,
        mesh=mesh,
        in_specs=(
            P("segment", "dp", "ctx", None, None),
            P("segment", None, None),
            P("segment", None, None),
            P("dp", "ctx"),
            P("segment", "dp"),
            P("segment", "dp", "ctx", None),
        ),
        out_specs=(P("segment", "dp", "ctx", None), P("segment", ("ctx", "dp"), None)),
        check_vma=False,
    )
```

profile of v0, /device:TPU:8, one launch (start us, length us, event | category | flops | bytes accessed | tf_op | source)
XLA Modules:
  0.0 184.2 jit_solution(17192626652956264830)
XLA Ops:
  2.2 6.7 %collective-permute-start = (f32[3,2560]{1,0:T(4,128)S(1)}, f32[3,2560]{1,0:T(4,128)}, u32[]{:S(2)}, u32[]{:S(2)}) collective-permute-start(f32[3,2560]{1,0:T(4,128)S(1)} %concatenate.19), channel_id=1, source_target_pairs={{64,0},{128,64},{192,128},{0,192},{65,1},{129,65},{193,129},{1,193... | collective-permute-start | bytes 92168 | tf_op jit(solution)/shard_map/ppermute | solution.py:274
  8.9 2.1 %shard_map.123 = (bf16[160,640]{1,0:T(8,128)(2,1)}, bf16[160,640]{1,0:T(8,128)(2,1)}, bf16[160,640]{1,0:T(8,128)(2,1)}, bf16[160,640]{1,0:T(8,128)(2,1)}) custom-call(s32[1]{0:T(128)} %bitcast.1.z_ref, bf16[160,2560]{1,0:T(8,128)(2,1)} %bitcast.24), custom_call_target="tpu_custom_call" | custom-call | tf_op jit(solution)/shard_map/pallas_call | solution.py:97
  11.7 1.3 collective-permute-start.3
  12.9 3.5 %collective-permute-start.4 = (bf16[160,640]{1,0:T(8,128)(2,1)}, bf16[160,640]{1,0:T(8,128)(2,1)}, u32[]{:S(2)}, u32[]{:S(2)}) collective-permute-start(bf16[160,640]{1,0:T(8,128)(2,1)} %get-tuple-element.116), channel_id=1, source_target_pairs={{0,204},{4,192},{8,196},{12,200},{16,220},{20,208},{24,212},{28,21... | collective-permute-start | bytes 614408 | tf_op jit(solution)/shard_map/ppermute | solution.py:64
  19.7 4.6 %shard_map.122 = (bf16[16,3,160,128]{3,2,1,0:T(8,128)(2,1)}, bf16[3,160,128]{2,1,0:T(8,128)(2,1)}, bf16[3,160,128]{2,1,0:T(8,128)(2,1)}, bf16[3,160,128]{2,1,0:T(8,128)(2,1)}, bf16[3,160,128]{2,1,0:T(8,128)(2,1)}) custom-call(s32[1]{0:T(128)} %bitcast.1.z_ref, bf16[3,160,2560]{2,1,0:T(8,128)(2,1)} %bitcast.22, f32[3,2560]{1,0:T(4,128)} %collective-permute-done.gain_ref, ...), custom_call_target="tpu_custom_call" | custom-call | tf_op jit(solution)/shard_map/pallas_call | solution.py:97
  25.6 3.0 %collective-permute-done.3 = bf16[160,640]{1,0:T(8,128)(2,1)} collective-permute-done((bf16[160,640]{1,0:T(8,128)(2,1)}, bf16[160,640]{1,0:T(8,128)(2,1)}, u32[]{:S(2)}, u32[]{:S(2)}) %collective-permute-start.3) | collective-permute-done | bytes 204832 | tf_op jit(solution)/shard_map/ppermute | solution.py:64
  29.3 9.2 %all-to-all-start.1 = ((bf16[16,3,160,128]{3,2,1,0:T(8,128)(2,1)}), bf16[16,3,160,128]{3,2,1,0:T(8,128)(2,1)}, u32[]{:S(2)}, u32[]{:S(2)}) async-start(bf16[16,3,160,128]{3,2,1,0:T(8,128)(2,1)} %get-tuple-element.117), calls=%async_computation.1 | async-start | bytes 3932160 | tf_op jit(solution)/shard_map/all_to_all | solution.py:293
  38.6 2.0 %collective-permute-start.5 = (bf16[3,160,128]{2,1,0:T(8,128)(2,1)S(1)}, bf16[3,160,128]{2,1,0:T(8,128)(2,1)S(1)}, u32[]{:S(2)}, u32[]{:S(2)}) collective-permute-start(bf16[3,160,128]{2,1,0:T(8,128)(2,1)S(1)} %copy-done.10), channel_id=1, source_target_pairs={{0,4},{4,8},{8,12},{12,0},{16,20},{20,24},{24,28},{28,16},{32,36},... | collective-permute-start | bytes 368648 | tf_op jit(solution)/shard_map/ppermute | solution.py:30
  40.5 2.4 %collective-permute-start.6 = (bf16[3,160,128]{2,1,0:T(8,128)(2,1)S(1)}, bf16[3,160,128]{2,1,0:T(8,128)(2,1)S(1)}, u32[]{:S(2)}, u32[]{:S(2)}) collective-permute-start(bf16[3,160,128]{2,1,0:T(8,128)(2,1)S(1)} %copy-done.9), channel_id=1, source_target_pairs={{0,8},{4,12},{8,0},{12,4},{16,24},{20,28},{24,16},{28,20},{32,40},... | collective-permute-start | bytes 368648 | tf_op jit(solution)/shard_map/ppermute | solution.py:30
  42.9 1.5 collective-permute-start.7
  44.4 34.0 %collective-permute-done.5.q1 = bf16[3,160,128]{2,1,0:T(8,128)(2,1)S(1)} collective-permute-done((bf16[3,160,128]{2,1,0:T(8,128)(2,1)S(1)}, bf16[3,160,128]{2,1,0:T(8,128)(2,1)S(1)}, u32[]{:S(2)}, u32[]{:S(2)}) %collective-permute-start.5) | collective-permute-done | bytes 122912 | tf_op jit(solution)/shard_map/ppermute | solution.py:30
  78.4 13.7 %collective-permute-done.6.q2 = bf16[3,160,128]{2,1,0:T(8,128)(2,1)S(1)} collective-permute-done((bf16[3,160,128]{2,1,0:T(8,128)(2,1)S(1)}, bf16[3,160,128]{2,1,0:T(8,128)(2,1)S(1)}, u32[]{:S(2)}, u32[]{:S(2)}) %collective-permute-start.6) | collective-permute-done | bytes 122912 | tf_op jit(solution)/shard_map/ppermute | solution.py:30
  92.8 2.8 %collective-permute-start.10 = (bf16[2,640,128]{2,1,0:T(8,128)(2,1)S(1)}, bf16[2,640,128]{2,1,0:T(8,128)(2,1)}, u32[]{:S(2)}, u32[]{:S(2)}) collective-permute-start(bf16[2,640,128]{2,1,0:T(8,128)(2,1)S(1)} %pad_maximum_fusion.s0), channel_id=1, source_target_pairs={{0,48},{4,52},{8,56},{12,60},{16,0},{20,4},{24,8},{28,12},{32,16},... | collective-permute-start | bytes 983048 | tf_op jit(solution)/shard_map/ppermute | solution.py:35
  95.6 2.3 %collective-permute-start.9 = (bf16[2,640,128]{2,1,0:T(8,128)(2,1)S(1)}, bf16[2,640,128]{2,1,0:T(8,128)(2,1)}, u32[]{:S(2)}, u32[]{:S(2)}) collective-permute-start(bf16[2,640,128]{2,1,0:T(8,128)(2,1)S(1)} %pad_maximum_fusion.s0), channel_id=1, source_target_pairs={{0,32},{4,36},{8,40},{12,44},{16,48},{20,52},{24,56},{28,60},{32,0... | collective-permute-start | bytes 983048 | tf_op jit(solution)/shard_map/ppermute | solution.py:35
  98.0 1.9 %fusion.gate_ref = f32[1,2560]{1,0:T(1,128)} fusion(f32[256,1]{0,1:T(1,128)S(1)} %bitcast.27, f32[1,256,2560]{2,1,0:T(8,128)S(1)} %copy-done), kind=kOutput, calls=%fused_computation | convolution fusion | flops 7864320 | bytes 2632704 | tf_op jit(solution)/shard_map/dot_general | solution.py:296
  99.9 7.8 %collective-permute-done.10.s3 = bf16[2,640,128]{2,1,0:T(8,128)(2,1)} collective-permute-done((bf16[2,640,128]{2,1,0:T(8,128)(2,1)S(1)}, bf16[2,640,128]{2,1,0:T(8,128)(2,1)}, u32[]{:S(2)}, u32[]{:S(2)}) %collective-permute-start.10) | collective-permute-done | bytes 327712 | tf_op jit(solution)/shard_map/ppermute | solution.py:35
  107.8 3.5 %collective-permute-done.8.s1 = bf16[2,640,128]{2,1,0:T(8,128)(2,1)} collective-permute-done((bf16[2,640,128]{2,1,0:T(8,128)(2,1)S(1)}, bf16[2,640,128]{2,1,0:T(8,128)(2,1)}, u32[]{:S(2)}, u32[]{:S(2)}) %collective-permute-start.8) | collective-permute-done | bytes 327712 | tf_op jit(solution)/shard_map/ppermute | solution.py:35
  111.3 4.1 %shard_map.124.refs_4_ = bf16[640,128]{1,0:T(8,128)(2,1)S(1)} custom-call(bf16[3,160,128]{2,1,0:T(8,128)(2,1)} %get-tuple-element.118.q0, bf16[3,160,128]{2,1,0:T(8,128)(2,1)} %copy-done.4, bf16[3,160,128]{2,1,0:T(8,128)(2,1)} %copy-done.5, bf16[3,160,128]{2,1,0:T(8,128)(2,1)} %copy-done.6, bf16[2,640,128]{2,1,0:T(8,128)(2,1)} %copy-done.2, ...), custom_call_target="tpu_custom_call" | custom-call | tf_op jit(solution)/shard_map/pallas_call | solution.py:97
  115.4 9.5 %shard_map.126 = (bf16[640,128]{1,0:T(8,128)(2,1)}, bf16[640,128]{1,0:T(8,128)(2,1)}, bf16[640,128]{1,0:T(8,128)(2,1)}) custom-call(s32[1]{0:T(128)} %bitcast.2.x_ref, bf16[16,3,160,128]{3,2,1,0:T(8,128)(2,1)} %all-to-all-done.1.r_ref), custom_call_target="tpu_custom_call" | custom-call | tf_op jit(solution)/shard_map/pallas_call | solution.py:97
  125.7 1.2 collective-permute-start.13
  127.0 4.1 %shard_map.125.refs_0_ = bf16[640,128]{1,0:T(8,128)(2,1)S(1)} custom-call(s32[1]{0:T(128)} %bitcast.2.x_ref, bf16[16,3,160,128]{3,2,1,0:T(8,128)(2,1)} %all-to-all-done.1.r_ref), custom_call_target="tpu_custom_call" | custom-call | tf_op jit(solution)/shard_map/pallas_call | solution.py:97
  132.3 1.8 collective-permute-done.13.refs_3_
  134.1 2.0 %shard_map.127 = (bf16[160,640]{1,0:T(8,128)(2,1)}, bf16[160,640]{1,0:T(8,128)(2,1)}, bf16[160,640]{1,0:T(8,128)(2,1)}, bf16[160,640]{1,0:T(8,128)(2,1)}) custom-call(s32[2]{0:T(128)S(1)} %pad_add_fusion.place_ref, bf16[640,128]{1,0:T(8,128)(2,1)S(1)} %shard_map.125.refs_0_, bf16[640,128]{1,0:T(8,128)(2,1)S(1)} %collective-permute-done.11.refs_1_, ...), custom_call_target="tpu_custom_call" | custom-call | tf_op jit(solution)/shard_map/pallas_call | solution.py:97
  136.0 8.8 %collective-permute-start.15 = (bf16[160,640]{1,0:T(8,128)(2,1)}, bf16[160,640]{1,0:T(8,128)(2,1)}, u32[]{:S(2)}, u32[]{:S(2)}) collective-permute-start(bf16[160,640]{1,0:T(8,128)(2,1)} %get-tuple-element.128), channel_id=1, source_target_pairs={{0,76},{4,64},{8,68},{12,72},{16,92},{20,80},{24,84},{28,88},{32,1... | collective-permute-start | bytes 614408 | tf_op jit(solution)/shard_map/ppermute | solution.py:60
  145.5 28.2 %while.10 = (s32[]{:T(128)}, f32[4,2560]{1,0:T(4,128)}, s32[]{:T(128)}, s32[]{:T(128)}, bf16[640,128]{1,0:T(8,128)(2,1)S(1)}, /*index=5*/bf16[640,128]{1,0:T(8,1...) while((s32[]{:T(128)}, f32[4,2560]{1,0:T(4,128)}, ...), condition=%wide.region_1.2_spmd, body=%wide.region_0.1_spmd.sunk | while | flops 2 | bytes 1917145 | solution.py:334
  145.5 2.3 %body.2 = f32[64,8,128]{2,1,0:T(8,128)} custom-call(s32[2]{0:T(128)S(1)} %get-tuple-element.334.place_ref, f32[3,2560]{1,0:T(4,128)} %get-tuple-element.335.time_ref, bf16[640,128]{1,0:T(8,128)(2,1)S(1)} %get-tuple-element.286.refs_0_, bf16[640,128]{1,0:T(8,128)(2,1)S(1)} %get-tuple-element.287.refs_1_, bf16[640,128]{1,0:T(8,128)(2,1)S(1)} %get-tuple-element.288.refs_2_, ...), custom_call_target="tpu_custom_call" | custom-call | tf_op jit(solution)/shard_map/while/body/pallas_call | solution.py:320
  147.8 9.6 %all-to-all-start = ((f32[64,8,128]{2,1,0:T(8,128)}), f32[64,8,128]{2,1,0:T(8,128)S(1)}, u32[]{:S(2)}, u32[]{:S(2)}) async-start(f32[64,8,128]{2,1,0:T(8,128)} %body.2), calls=%async_computation | async-start | bytes 524288 | tf_op jit(solution)/shard_map/while/body/all_to_all | solution.py:329
  157.4 1.4 copy.24.before_ref
  158.8 12.6 %all-to-all-done.chan_ref = f32[64,8,128]{2,1,0:T(8,128)S(1)} async-done(((f32[64,8,128]{2,1,0:T(8,128)}), f32[64,8,128]{2,1,0:T(8,128)S(1)}, u32[]{:S(2)}, u32[]{:S(2)}) %all-to-all-start) | async-done | bytes 262176 | tf_op jit(solution)/shard_map/while/body/all_to_all | solution.py:329
  172.1 1.7 body.3
  173.7 7.5 %collective-permute-done.18 = f32[4,2560]{1,0:T(4,128)S(1)} collective-permute-done((f32[4,2560]{1,0:T(4,128)}, f32[4,2560]{1,0:T(4,128)S(1)}, u32[]{:S(2)}, u32[]{:S(2)}) %collective-permute-start.18) | collective-permute-done | bytes 40992 | tf_op jit(solution)/shard_map/ppermute | solution.py:335
  181.3 2.3 %shard_map.128 = bf16[160,2560]{1,0:T(8,128)(2,1)} custom-call(s32[1]{0:T(128)} %bitcast.1.z_ref, bf16[160,640]{1,0:T(8,128)(2,1)} %collective-permute-done.14.a0, bf16[160,640]{1,0:T(8,128)(2,1)} %collective-permute-done.15.a1, bf16[160,640]{1,0:T(8,128)(2,1)} %collective-permute-done.16.a2, bf16[160,640]{1,0:T(8,128)(2,1)} %collective-permute-done.17.a3, ...), custom_call_target="tpu_custom_call" | custom-call | tf_op jit(solution)/shard_map/pallas_call | solution.py:97
  (64 shorter events, 11.7 us)
Async XLA Ops:
  0.6 97.4 %copy-start = (f32[1,256,2560]{2,1,0:T(8,128)S(1)}, f32[1,256,2560]{2,1,0:T(8,128)}, u32[]{:S(2)}) copy-start(f32[1,256,2560]{2,1,0:T(8,128)} %param.15) | copy-start | bytes 7864324
  2.2 17.6 %collective-permute-start = (f32[3,2560]{1,0:T(4,128)S(1)}, f32[3,2560]{1,0:T(4,128)}, u32[]{:S(2)}, u32[]{:S(2)}) collective-permute-start(f32[3,2560]{1,0:T(4,128)S(1)} %concatenate.19), channel_id=1, source_target_pairs={{64,0},{128,64},{192,128},{0,192},{65,1},{129,65},{193,129},{1,193... | collective-permute-start | bytes 92168 | tf_op jit(solution)/shard_map/ppermute | solution.py:274
  11.0 13.4 %collective-permute-start.1 = (bf16[160,640]{1,0:T(8,128)(2,1)}, bf16[160,640]{1,0:T(8,128)(2,1)}, u32[]{:S(2)}, u32[]{:S(2)}) collective-permute-start(bf16[160,640]{1,0:T(8,128)(2,1)} %get-tuple-element.113), channel_id=1, source_target_pairs={{0,192},{4,196},{8,200},{12,204},{16,208},{20,212},{24,216},{28,22... | collective-permute-start | bytes 614408 | tf_op jit(solution)/shard_map/ppermute | solution.py:64
  11.7 13.9 %collective-permute-start.2 = (bf16[160,640]{1,0:T(8,128)(2,1)}, bf16[160,640]{1,0:T(8,128)(2,1)}, u32[]{:S(2)}, u32[]{:S(2)}) collective-permute-start(bf16[160,640]{1,0:T(8,128)(2,1)} %get-tuple-element.114), channel_id=1, source_target_pairs={{0,196},{4,200},{8,204},{12,192},{16,212},{20,216},{24,220},{28,20... | collective-permute-start | bytes 614408 | tf_op jit(solution)/shard_map/ppermute | solution.py:64
  11.7 16.9 %collective-permute-start.3 = (bf16[160,640]{1,0:T(8,128)(2,1)}, bf16[160,640]{1,0:T(8,128)(2,1)}, u32[]{:S(2)}, u32[]{:S(2)}) collective-permute-start(bf16[160,640]{1,0:T(8,128)(2,1)} %get-tuple-element.115), channel_id=1, source_target_pairs={{0,200},{4,204},{8,192},{12,196},{16,216},{20,220},{24,208},{28,21... | collective-permute-start | bytes 614408 | tf_op jit(solution)/shard_map/ppermute | solution.py:64
  12.9 16.4 %collective-permute-start.4 = (bf16[160,640]{1,0:T(8,128)(2,1)}, bf16[160,640]{1,0:T(8,128)(2,1)}, u32[]{:S(2)}, u32[]{:S(2)}) collective-permute-start(bf16[160,640]{1,0:T(8,128)(2,1)} %get-tuple-element.116), channel_id=1, source_target_pairs={{0,204},{4,192},{8,196},{12,200},{16,220},{20,208},{24,212},{28,21... | collective-permute-start | bytes 614408 | tf_op jit(solution)/shard_map/ppermute | solution.py:64
  24.3 14.2 %copy-start.10 = (bf16[3,160,128]{2,1,0:T(8,128)(2,1)S(1)}, bf16[3,160,128]{2,1,0:T(8,128)(2,1)}, u32[]{:S(2)}) copy-start(bf16[3,160,128]{2,1,0:T(8,128)(2,1)} %get-tuple-element.119) | copy-start | bytes 368644
  24.3 16.2 %copy-start.9 = (bf16[3,160,128]{2,1,0:T(8,128)(2,1)S(1)}, bf16[3,160,128]{2,1,0:T(8,128)(2,1)}, u32[]{:S(2)}) copy-start(bf16[3,160,128]{2,1,0:T(8,128)(2,1)} %get-tuple-element.120) | copy-start | bytes 368644
  24.3 18.5 %copy-start.8 = (bf16[3,160,128]{2,1,0:T(8,128)(2,1)S(1)}, bf16[3,160,128]{2,1,0:T(8,128)(2,1)}, u32[]{:S(2)}) copy-start(bf16[3,160,128]{2,1,0:T(8,128)(2,1)} %get-tuple-element.121) | copy-start | bytes 368644
  24.4 20.0 %copy-start.7 = (f32[128]{0:T(128)S(1)}, f32[128]{0:T(128)}, u32[]{:S(2)}) copy-start(f32[128]{0:T(128)} %constant.95.clone) | copy-start | bytes 1540
  24.4 20.1 %copy-start.3 = (bf16[3,160,128]{2,1,0:T(8,128)(2,1)S(1)}, bf16[3,160,128]{2,1,0:T(8,128)(2,1)}, u32[]{:S(2)}) copy-start(bf16[3,160,128]{2,1,0:T(8,128)(2,1)} %get-tuple-element.118.q0) | copy-start | bytes 368644
  29.3 68.6 %copy-start.11 = (f32[256]{0:T(256)S(1)}, f32[256]{0:T(256)}, u32[]{:S(2)}) copy-start(f32[256]{0:T(256)} %constant.96.clone) | copy-start | bytes 3076
  29.3 86.0 %all-to-all-start.1 = ((bf16[16,3,160,128]{3,2,1,0:T(8,128)(2,1)}), bf16[16,3,160,128]{3,2,1,0:T(8,128)(2,1)}, u32[]{:S(2)}, u32[]{:S(2)}) async-start(bf16[16,3,160,128]{3,2,1,0:T(8,128)(2,1)} %get-tuple-element.117), calls=%async_computation.1 | async-start | bytes 3932160 | tf_op jit(solution)/shard_map/all_to_all | solution.py:293
  38.6 39.8 %collective-permute-start.5 = (bf16[3,160,128]{2,1,0:T(8,128)(2,1)S(1)}, bf16[3,160,128]{2,1,0:T(8,128)(2,1)S(1)}, u32[]{:S(2)}, u32[]{:S(2)}) collective-permute-start(bf16[3,160,128]{2,1,0:T(8,128)(2,1)S(1)} %copy-done.10), channel_id=1, source_target_pairs={{0,4},{4,8},{8,12},{12,0},{16,20},{20,24},{24,28},{28,16},{32,36},... | collective-permute-start | bytes 368648 | tf_op jit(solution)/shard_map/ppermute | solution.py:30
  40.5 51.6 %collective-permute-start.6 = (bf16[3,160,128]{2,1,0:T(8,128)(2,1)S(1)}, bf16[3,160,128]{2,1,0:T(8,128)(2,1)S(1)}, u32[]{:S(2)}, u32[]{:S(2)}) collective-permute-start(bf16[3,160,128]{2,1,0:T(8,128)(2,1)S(1)} %copy-done.9), channel_id=1, source_target_pairs={{0,8},{4,12},{8,0},{12,4},{16,24},{20,28},{24,16},{28,20},{32,40},... | collective-permute-start | bytes 368648 | tf_op jit(solution)/shard_map/ppermute | solution.py:30
  42.9 49.2 %collective-permute-start.7 = (bf16[3,160,128]{2,1,0:T(8,128)(2,1)S(1)}, bf16[3,160,128]{2,1,0:T(8,128)(2,1)S(1)}, u32[]{:S(2)}, u32[]{:S(2)}) collective-permute-start(bf16[3,160,128]{2,1,0:T(8,128)(2,1)S(1)} %copy-done.8), channel_id=1, source_target_pairs={{0,12},{4,0},{8,4},{12,8},{16,28},{20,16},{24,20},{28,24},{32,44},... | collective-permute-start | bytes 368648 | tf_op jit(solution)/shard_map/ppermute | solution.py:30
  78.4 32.8 %copy-start.4 = (bf16[3,160,128]{2,1,0:T(8,128)(2,1)}, bf16[3,160,128]{2,1,0:T(8,128)(2,1)S(1)}, u32[]{:S(2)}) copy-start(bf16[3,160,128]{2,1,0:T(8,128)(2,1)S(1)} %collective-permute-done.5.q1) | copy-start | bytes 368644
  92.1 19.2 %copy-start.5 = (bf16[3,160,128]{2,1,0:T(8,128)(2,1)}, bf16[3,160,128]{2,1,0:T(8,128)(2,1)S(1)}, u32[]{:S(2)}) copy-start(bf16[3,160,128]{2,1,0:T(8,128)(2,1)S(1)} %collective-permute-done.6.q2) | copy-start | bytes 368644
  92.8 18.4 %copy-start.2 = (bf16[2,640,128]{2,1,0:T(8,128)(2,1)}, bf16[2,640,128]{2,1,0:T(8,128)(2,1)S(1)}, u32[]{:S(2)}) copy-start(bf16[2,640,128]{2,1,0:T(8,128)(2,1)S(1)} %pad_maximum_fusion.s0) | copy-start | bytes 983044
  92.8 14.9 %collective-permute-start.10 = (bf16[2,640,128]{2,1,0:T(8,128)(2,1)S(1)}, bf16[2,640,128]{2,1,0:T(8,128)(2,1)}, u32[]{:S(2)}, u32[]{:S(2)}) collective-permute-start(bf16[2,640,128]{2,1,0:T(8,128)(2,1)S(1)} %pad_maximum_fusion.s0), channel_id=1, source_target_pairs={{0,48},{4,52},{8,56},{12,60},{16,0},{20,4},{24,8},{28,12},{32,16},... | collective-permute-start | bytes 983048 | tf_op jit(solution)/shard_map/ppermute | solution.py:35
  95.6 15.7 %collective-permute-start.8 = (bf16[2,640,128]{2,1,0:T(8,128)(2,1)S(1)}, bf16[2,640,128]{2,1,0:T(8,128)(2,1)}, u32[]{:S(2)}, u32[]{:S(2)}) collective-permute-start(bf16[2,640,128]{2,1,0:T(8,128)(2,1)S(1)} %pad_maximum_fusion.s0), channel_id=1, source_target_pairs={{0,16},{4,20},{8,24},{12,28},{16,32},{20,36},{24,40},{28,44},{32,4... | collective-permute-start | bytes 983048 | tf_op jit(solution)/shard_map/ppermute | solution.py:35
  95.6 15.7 %collective-permute-start.9 = (bf16[2,640,128]{2,1,0:T(8,128)(2,1)S(1)}, bf16[2,640,128]{2,1,0:T(8,128)(2,1)}, u32[]{:S(2)}, u32[]{:S(2)}) collective-permute-start(bf16[2,640,128]{2,1,0:T(8,128)(2,1)S(1)} %pad_maximum_fusion.s0), channel_id=1, source_target_pairs={{0,32},{4,36},{8,40},{12,44},{16,48},{20,52},{24,56},{28,60},{32,0... | collective-permute-start | bytes 983048 | tf_op jit(solution)/shard_map/ppermute | solution.py:35
  124.9 6.2 %collective-permute-start.11 = (bf16[640,128]{1,0:T(8,128)(2,1)}, bf16[640,128]{1,0:T(8,128)(2,1)S(1)}, u32[]{:S(2)}, u32[]{:S(2)}) collective-permute-start(bf16[640,128]{1,0:T(8,128)(2,1)} %get-tuple-element.123), channel_id=1, source_target_pairs={{0,48},{4,52},{8,56},{12,60},{16,0},{20,4},{24,8},{28,12},{32,16},... | collective-permute-start | bytes 491528 | tf_op jit(solution)/shard_map/ppermute | solution.py:35
  125.2 7.1 %collective-permute-start.12 = (bf16[640,128]{1,0:T(8,128)(2,1)}, bf16[640,128]{1,0:T(8,128)(2,1)S(1)}, u32[]{:S(2)}, u32[]{:S(2)}) collective-permute-start(bf16[640,128]{1,0:T(8,128)(2,1)} %get-tuple-element.124), channel_id=1, source_target_pairs={{0,32},{4,36},{8,40},{12,44},{16,48},{20,52},{24,56},{28,60},{32,0... | collective-permute-start | bytes 491528 | tf_op jit(solution)/shard_map/ppermute | solution.py:35
  125.7 8.4 %collective-permute-start.13 = (bf16[640,128]{1,0:T(8,128)(2,1)}, bf16[640,128]{1,0:T(8,128)(2,1)}, u32[]{:S(2)}, u32[]{:S(2)}) collective-permute-start(bf16[640,128]{1,0:T(8,128)(2,1)} %get-tuple-element.125), channel_id=1, source_target_pairs={{0,16},{4,20},{8,24},{12,28},{16,32},{20,36},{24,40},{28,44},{32,4... | collective-permute-start | bytes 491528 | tf_op jit(solution)/shard_map/ppermute | solution.py:35
  136.0 45.3 %collective-permute-start.14 = (bf16[160,640]{1,0:T(8,128)(2,1)}, bf16[160,640]{1,0:T(8,128)(2,1)}, u32[]{:S(2)}, u32[]{:S(2)}) collective-permute-start(bf16[160,640]{1,0:T(8,128)(2,1)} %get-tuple-element.127), channel_id=1, source_target_pairs={{0,64},{4,68},{8,72},{12,76},{16,80},{20,84},{24,88},{28,92},{32,9... | collective-permute-start | bytes 614408 | tf_op jit(solution)/shard_map/ppermute | solution.py:60
  136.0 45.3 %collective-permute-start.15 = (bf16[160,640]{1,0:T(8,128)(2,1)}, bf16[160,640]{1,0:T(8,128)(2,1)}, u32[]{:S(2)}, u32[]{:S(2)}) collective-permute-start(bf16[160,640]{1,0:T(8,128)(2,1)} %get-tuple-element.128), channel_id=1, source_target_pairs={{0,76},{4,64},{8,68},{12,72},{16,92},{20,80},{24,84},{28,88},{32,1... | collective-permute-start | bytes 614408 | tf_op jit(solution)/shard_map/ppermute | solution.py:60
  144.9 36.4 %collective-permute-start.16 = (bf16[160,640]{1,0:T(8,128)(2,1)}, bf16[160,640]{1,0:T(8,128)(2,1)}, u32[]{:S(2)}, u32[]{:S(2)}) collective-permute-start(bf16[160,640]{1,0:T(8,128)(2,1)} %get-tuple-element.129), channel_id=1, source_target_pairs={{0,72},{4,76},{8,64},{12,68},{16,88},{20,92},{24,80},{28,84},{32,1... | collective-permute-start | bytes 614408 | tf_op jit(solution)/shard_map/ppermute | solution.py:60
  144.9 36.4 %collective-permute-start.17 = (bf16[160,640]{1,0:T(8,128)(2,1)}, bf16[160,640]{1,0:T(8,128)(2,1)}, u32[]{:S(2)}, u32[]{:S(2)}) collective-permute-start(bf16[160,640]{1,0:T(8,128)(2,1)} %get-tuple-element.130), channel_id=1, source_target_pairs={{0,68},{4,72},{8,76},{12,64},{16,84},{20,88},{24,92},{28,80},{32,1... | collective-permute-start | bytes 614408 | tf_op jit(solution)/shard_map/ppermute | solution.py:60
  147.8 23.6 %all-to-all-start = ((f32[64,8,128]{2,1,0:T(8,128)}), f32[64,8,128]{2,1,0:T(8,128)S(1)}, u32[]{:S(2)}, u32[]{:S(2)}) async-start(f32[64,8,128]{2,1,0:T(8,128)} %body.2), calls=%async_computation | async-start | bytes 524288 | tf_op jit(solution)/shard_map/while/body/all_to_all | solution.py:329
  171.3 0.7 copy-start.1
  173.7 7.5 %collective-permute-start.18 = (f32[4,2560]{1,0:T(4,128)}, f32[4,2560]{1,0:T(4,128)S(1)}, u32[]{:S(2)}, u32[]{:S(2)}) collective-permute-start(f32[4,2560]{1,0:T(4,128)} %get-tuple-element.133), channel_id=1, source_target_pairs={{0,64},{64,128},{128,192},{192,0},{1,65},{65,129},{129,193},{193,1... | collective-permute-start | bytes 122888 | tf_op jit(solution)/shard_map/ppermute | solution.py:335
  (1 other events, 0.7 us)
where the time goes:
time: 185 us; the launch traced here: 184 us
  waiting for transfers between devices  86.9 us (47%)
  starting transfers between devices  52.7 us (28%)
  Pallas kernels  32.6 us (18%)
  local copies, waits for them, and re-layouts  4.97 us (3%)
  other arithmetic  3.45 us (2%)
  matrix products  1.94 us (1%)
    ppermute x3, waiting for transfers between devices, along_z(): return lax.ppermute(value, 'ctx', pairs)  47.6 us
    pallas_call x8, Pallas kernels, call(): pl.pallas_call(kernel, grid=grid, out_shape=out_shape, in_specs=specs, ou...  30.3 us
    ppermute x6, waiting for transfers between devices, along_x(): return lax.ppermute(value, 'ctx', pairs)  14.3 us
    all_to_all x1, waiting for transfers between devices, gradient(): chans = lax.all_to_all(chans, ('ctx', 'dp'), 0, 0)  12.6 us
    all_to_all x1, starting transfers between devices, gradient(): chans = lax.all_to_all(chans, ('ctx', 'dp'), 0, 0)  9.58 us
    all_to_all x1, starting transfers between devices, local(): main = lax.all_to_all(after(main, cots_z), 'ctx', 0, 0)  9.23 us
    ppermute x4, starting transfers between devices, home(): return lax.ppermute(value, ('segment', 'ctx'), section_pairs(1, by))  8.83 us
    ppermute x1, waiting for transfers between devices, local(): lax.ppermute(grad, 'segment', [(i, (i + 1) % SIDE) for i in range(SIDE)])  7.54 us
  transfers between devices with their start and end apart: 21, of which 11 were waited for; matrix products, arithmetic and copies ran while one was open for 4% of the time, Pallas kernels for 10%

commit v1 on v0

--- a/solution.py
+++ b/solution.py
@@ -240,7 +240,7 @@
             total = sum(f * c[head : head + 1] for f, c in zip(factors, chans, strict=True))
             at = (z * GROUP + head) * HEAD_DIM
             cols = slice(at, at + HEAD_DIM)
-            out_ref[:, cols] = before_ref[:, cols] + total
+            out_ref[:, cols] = before_ref[...] + total
 
 
 def shape(dims, dtype=jnp.bfloat16):
@@ -275,7 +275,7 @@
     parts = qkv[0, 0].transpose(1, 0, 2)
     cots = call(cut_cotangent_kernel, [flat] * SIDE, 0, 1_600_000, z, cotangent[0, 0])
     cots_z = [None] * SIDE
-    for k in (2, 1, 3, 0):
+    for k in (2, 1):
         cots_z[k] = away(cots[k], k)
     cosine, sine = rope_tables(positions[0])
     main, *shared = call(
@@ -290,7 +290,7 @@
         sine,
     )
     shared_z = exchanged(along_z, shared)
-    main = lax.all_to_all(after(main, cots_z), "ctx", 0, 0)
+    main = lax.all_to_all(after(main, shared_z), "ctx", 0, 0)
     pair = jnp.concatenate([b[1:] for b in shared_z], axis=1)
     pairs = [pair] + [along_x(pair, k) for k in steps]
     gate = jnp.dot(embed(step), mod_weight[0], precision=lax.Precision.HIGHEST)[None]
@@ -301,7 +301,7 @@
     shared_out = call(
         shared_kernel, single, 840_000_000, 1_600_000, *shared_z, *pairs, smem=0
     )
-    main, gate, freq, shared_out = lax.optimization_barrier((main, gate, freq, shared_out))
+    main, gate, freq = lax.optimization_barrier((main, gate, freq))
     back = [None] * SIDE
     back[2], back[1], back[3] = call(
         functools.partial(main_kernel, (2, 1, 3)), [single] * 3, 2_500_000_000, 2_500_000, x, main
@@ -309,14 +309,18 @@
     (back[0],) = call(
         functools.partial(main_kernel, (0,)), [single], 840_000_000, 2_000_000, x, main
     )
+    for k in (3, 0):
+        cots_z[k] = away(after(cots[k], back[2]), k)
     back = [back[0]] + [along_x(back[m], SIDE - m) for m in steps]
-    joined = call(join_kernel, [flat] * SIDE, 0, 1_600_000, place, *back, shared_out)
+    joined = call(
+        join_kernel, [flat] * SIDE, 0, 1_600_000, place, *back, after(shared_out, cots_z[1:3])
+    )
     at_home = [None] * SIDE
     for k in (2, 1, 3, 0):
         at_home[k] = home(joined[k], (SIDE - k) % SIDE)
 
-    def gradient(_, before):
-        attn, before = lax.optimization_barrier(([*back, shared_out], before))
+    def gradient(_, state):
+        attn, before = lax.optimization_barrier(([*back, shared_out], state[1]))
         chans = pl.pallas_call(
             channels_kernel,
             out_shape=shape((SIDE * count, 8, HEAD_DIM), jnp.float32),
@@ -327,11 +331,13 @@
             cost_estimate=pl.CostEstimate(flops=0, bytes_accessed=0, transcendentals=0),
         )(place, gains, *attn, *cots_z)
         chans = lax.all_to_all(chans, ("ctx", "dp"), 0, 0)
-        return call(grad_kernel, zeros, 0, 200_000, index[None], freq, before, chans)
+        grad = call(grad_kernel, zeros, 0, 200_000, index[None], freq, before, chans)
+        return (grad, before)
 
     zeros = shape((rows, WIDTH), jnp.float32)
     turns = jnp.where(step < 1000, 1, 2)
-    grad = lax.fori_loop(0, turns, gradient, jnp.zeros((rows, WIDTH), jnp.float32))
+    start = (jnp.zeros((rows, WIDTH), jnp.float32), jnp.zeros((rows, HEAD_DIM), jnp.float32))
+    grad, _ = lax.fori_loop(0, turns, gradient, start)
     grad = lax.ppermute(grad, "segment", [(i, (i + 1) % SIDE) for i in range(SIDE)])
 
     attn_out = call(

time: 185 us -> 162 us (0.88)
  waiting for transfers between devices: 86.9 us -> 69.3 us
  starting transfers between devices: 52.7 us -> 48.8 us
    all_to_all x1, waiting for transfers between devices: 0.01 us -> 41.1 us  [local(): main = lax.all_to_all(after(main, shared_z), 'ctx', 0, 0)]
    ppermute x3, waiting for transfers between devices: 47.6 us -> 7.4 us  [along_z(): return lax.ppermute(value, 'ctx', pairs)]
    ppermute x6, waiting for transfers between devices: 14.3 us -> 0.02 us  [along_x(): return lax.ppermute(value, 'ctx', pairs)]
    ppermute x4, waiting for transfers between devices: 4.93 us -> 0.01 us  [away(): return lax.ppermute(value, ('segment', 'ctx'), section_pairs(SIDE - 1, by))]
    ppermute x4, starting transfers between devices: 8.83 us -> 4.53 us  [home(): return lax.ppermute(value, ('segment', 'ctx'), section_pairs(1, by))]
  transfers between devices with their start and end apart: 21 -> 21, of which waited for: 11 -> 5; matrix products, arithmetic and copies ran while one was open for 4% -> 4% of each run, Pallas kernels for 10% -> 16%
where the time goes in v1:
time: 162 us; the launch traced here: 161 us
  waiting for transfers between devices  69.3 us (43%)
  starting transfers between devices  48.8 us (30%)
  Pallas kernels  32.5 us (20%)
  local copies, waits for them, and re-layouts  3.62 us (2%)
  other arithmetic  3.45 us (2%)
  matrix products  1.94 us (1%)
  between operations  1.62 us (1%)
    all_to_all x1, waiting for transfers between devices, local(): main = lax.all_to_all(after(main, shared_z), 'ctx', 0, 0)  41.1 us
    pallas_call x8, Pallas kernels, call(): pl.pallas_call(kernel, grid=grid, out_shape=out_shape, in_specs=specs, ou...  30.3 us
    all_to_all x1, waiting for transfers between devices, gradient(): chans = lax.all_to_all(chans, ('ctx', 'dp'), 0, 0)  13 us
    all_to_all x1, starting transfers between devices, gradient(): chans = lax.all_to_all(chans, ('ctx', 'dp'), 0, 0)  11.4 us
    ppermute x6, starting transfers between devices, along_x(): return lax.ppermute(value, 'ctx', pairs)  8.69 us
    ppermute x1, waiting for transfers between devices, local(): lax.ppermute(grad, 'segment', [(i, (i + 1) % SIDE) for i in range(SIDE)])  7.75 us
    all_to_all x1, starting transfers between devices, local(): main = lax.all_to_all(after(main, shared_z), 'ctx', 0, 0)  7.46 us
    ppermute x3, waiting for transfers between devices, along_z(): return lax.ppermute(value, 'ctx', pairs)  7.4 us
  transfers between devices with their start and end apart: 21, of which 5 were waited for; matrix products, arithmetic and copies ran while one was open for 4% of the time, Pallas kernels for 16%

profile of v1, /device:TPU:8, one launch (start us, length us, event | category | flops | bytes accessed | tf_op | source)
XLA Modules:
  0.0 161.3 jit_solution(9251722967983442421)
XLA Ops:
  2.2 6.7 %collective-permute-start = (f32[3,2560]{1,0:T(4,128)S(1)}, f32[3,2560]{1,0:T(4,128)}, u32[]{:S(2)}, u32[]{:S(2)}) collective-permute-start(f32[3,2560]{1,0:T(4,128)S(1)} %concatenate.19), channel_id=1, source_target_pairs={{64,0},{128,64},{192,128},{0,192},{65,1},{129,65},{193,129},{1,193... | collective-permute-start | bytes 92168 | tf_op jit(solution)/shard_map/ppermute | solution.py:274
  10.3 1.1 fusion.4
  12.2 4.5 %shard_map.122 = (bf16[16,3,160,128]{3,2,1,0:T(8,128)(2,1)}, bf16[3,160,128]{2,1,0:T(8,128)(2,1)}, bf16[3,160,128]{2,1,0:T(8,128)(2,1)}, bf16[3,160,128]{2,1,0:T(8,128)(2,1)}, bf16[3,160,128]{2,1,0:T(8,128)(2,1)}) custom-call(s32[1]{0:T(128)} %bitcast.1.z_ref, bf16[3,160,2560]{2,1,0:T(8,128)(2,1)} %bitcast.22, f32[3,2560]{1,0:T(4,128)} %collective-permute-done.gain_ref, ...), custom_call_target="tpu_custom_call" | custom-call | tf_op jit(solution)/shard_map/pallas_call | solution.py:97
  16.7 1.1 collective-permute-start.1
  17.8 1.5 collective-permute-start.2
  19.3 1.9 %collective-permute-start.3 = (bf16[3,160,128]{2,1,0:T(8,128)(2,1)}, bf16[3,160,128]{2,1,0:T(8,128)(2,1)S(1)}, u32[]{:S(2)}, u32[]{:S(2)}) collective-permute-start(bf16[3,160,128]{2,1,0:T(8,128)(2,1)} %get-tuple-element.122), channel_id=1, source_target_pairs={{0,12},{4,0},{8,4},{12,8},{16,28},{20,16},{24,20},{28,24},{32,44},... | collective-permute-start | bytes 368648 | tf_op jit(solution)/shard_map/ppermute | solution.py:30
  21.2 4.0 %collective-permute-done.1.q1 = bf16[3,160,128]{2,1,0:T(8,128)(2,1)S(1)} collective-permute-done((bf16[3,160,128]{2,1,0:T(8,128)(2,1)}, bf16[3,160,128]{2,1,0:T(8,128)(2,1)S(1)}, u32[]{:S(2)}, u32[]{:S(2)}) %collective-permute-start.1) | collective-permute-done | bytes 122912 | tf_op jit(solution)/shard_map/ppermute | solution.py:30
  25.2 3.4 %collective-permute-done.2.q2 = bf16[3,160,128]{2,1,0:T(8,128)(2,1)S(1)} collective-permute-done((bf16[3,160,128]{2,1,0:T(8,128)(2,1)}, bf16[3,160,128]{2,1,0:T(8,128)(2,1)S(1)}, u32[]{:S(2)}, u32[]{:S(2)}) %collective-permute-start.2) | collective-permute-done | bytes 122912 | tf_op jit(solution)/shard_map/ppermute | solution.py:30
  28.6 7.5 %all-to-all-start.1 = ((bf16[16,3,160,128]{3,2,1,0:T(8,128)(2,1)}), bf16[16,3,160,128]{3,2,1,0:T(8,128)(2,1)}, u32[]{:S(2)}, u32[]{:S(2)}) async-start(bf16[16,3,160,128]{3,2,1,0:T(8,128)(2,1)} %get-tuple-element.123), calls=%async_computation.1 | async-start | bytes 3932160 | tf_op jit(solution)/shard_map/all_to_all | solution.py:293
  36.1 2.1 %shard_map.126 = (bf16[160,640]{1,0:T(8,128)(2,1)}, bf16[160,640]{1,0:T(8,128)(2,1)}, bf16[160,640]{1,0:T(8,128)(2,1)}, bf16[160,640]{1,0:T(8,128)(2,1)}) custom-call(s32[1]{0:T(128)} %bitcast.1.z_ref, bf16[160,2560]{1,0:T(8,128)(2,1)} %bitcast.24), custom_call_target="tpu_custom_call" | custom-call | tf_op jit(solution)/shard_map/pallas_call | solution.py:97
  38.2 2.2 %collective-permute-start.10 = (bf16[160,640]{1,0:T(8,128)(2,1)}, bf16[160,640]{1,0:T(8,128)(2,1)}, u32[]{:S(2)}, u32[]{:S(2)}) collective-permute-start(bf16[160,640]{1,0:T(8,128)(2,1)} %get-tuple-element.128), channel_id=1, source_target_pairs={{0,196},{4,200},{8,204},{12,192},{16,212},{20,216},{24,220},{28,20... | collective-permute-start | bytes 614408 | tf_op jit(solution)/shard_map/ppermute | solution.py:64
  40.4 1.2 collective-permute-start.11
  41.9 1.5 collective-permute-start.7
  43.4 2.7 %collective-permute-start.8 = (bf16[2,640,128]{2,1,0:T(8,128)(2,1)S(1)}, bf16[2,640,128]{2,1,0:T(8,128)(2,1)}, u32[]{:S(2)}, u32[]{:S(2)}) collective-permute-start(bf16[2,640,128]{2,1,0:T(8,128)(2,1)S(1)} %pad_maximum_fusion.s0), channel_id=1, source_target_pairs={{0,32},{4,36},{8,40},{12,44},{16,48},{20,52},{24,56},{28,60},{32,0... | collective-permute-start | bytes 983048 | tf_op jit(solution)/shard_map/ppermute | solution.py:35
  46.1 1.5 collective-permute-start.9
  47.5 1.9 %fusion.gate_ref = f32[1,2560]{1,0:T(1,128)} fusion(f32[256,1]{0,1:T(1,128)S(1)} %bitcast.27, f32[1,256,2560]{2,1,0:T(8,128)S(1)} %copy-done), kind=kOutput, calls=%fused_computation | convolution fusion | flops 7864320 | bytes 2632704 | tf_op jit(solution)/shard_map/dot_general | solution.py:296
  49.5 41.1 %all-to-all-done.1.r_ref = bf16[16,3,160,128]{3,2,1,0:T(8,128)(2,1)} async-done(((bf16[16,3,160,128]{3,2,1,0:T(8,128)(2,1)}), bf16[16,3,160,128]{3,2,1,0:T(8,128)(2,1)}, u32[]{:S(2)}, u32[]{:S(2)}) %all-to-all-start.1) | async-done | bytes 1966112 | tf_op jit(solution)/shard_map/all_to_all | solution.py:293
  90.7 9.5 %shard_map.124 = (bf16[640,128]{1,0:T(8,128)(2,1)}, bf16[640,128]{1,0:T(8,128)(2,1)}, bf16[640,128]{1,0:T(8,128)(2,1)}) custom-call(s32[1]{0:T(128)} %bitcast.2.x_ref, bf16[16,3,160,128]{3,2,1,0:T(8,128)(2,1)} %all-to-all-done.1.r_ref), custom_call_target="tpu_custom_call" | custom-call | tf_op jit(solution)/shard_map/pallas_call | solution.py:97
  100.1 2.2 %collective-permute-start.16 = (bf16[160,640]{1,0:T(8,128)(2,1)}, bf16[160,640]{1,0:T(8,128)(2,1)}, u32[]{:S(2)}, u32[]{:S(2)}) collective-permute-start(bf16[160,640]{1,0:T(8,128)(2,1)} %get-tuple-element.137), channel_id=1, source_target_pairs={{0,192},{4,196},{8,200},{12,204},{16,208},{20,212},{24,216},{28,22... | collective-permute-start | bytes 614408 | tf_op jit(solution)/shard_map/ppermute | solution.py:64
  104.0 1.4 collective-permute-start.4
  106.2 4.1 %shard_map.125.refs_4_ = bf16[640,128]{1,0:T(8,128)(2,1)S(1)} custom-call(bf16[3,160,128]{2,1,0:T(8,128)(2,1)} %get-tuple-element.119.q0, bf16[3,160,128]{2,1,0:T(8,128)(2,1)} %copy-done.4, bf16[3,160,128]{2,1,0:T(8,128)(2,1)} %copy-done.5, bf16[3,160,128]{2,1,0:T(8,128)(2,1)} %copy-done.6, bf16[2,640,128]{2,1,0:T(8,128)(2,1)} %copy-done.2, ...), custom_call_target="tpu_custom_call" | custom-call | tf_op jit(solution)/shard_map/pallas_call | solution.py:97
  110.2 4.1 %shard_map.123.refs_0_ = bf16[640,128]{1,0:T(8,128)(2,1)S(1)} custom-call(s32[1]{0:T(128)} %bitcast.2.x_ref, bf16[16,3,160,128]{3,2,1,0:T(8,128)(2,1)} %all-to-all-done.1.r_ref), custom_call_target="tpu_custom_call" | custom-call | tf_op jit(solution)/shard_map/pallas_call | solution.py:97
  114.4 2.0 %shard_map.127 = (bf16[160,640]{1,0:T(8,128)(2,1)}, bf16[160,640]{1,0:T(8,128)(2,1)}, bf16[160,640]{1,0:T(8,128)(2,1)}, bf16[160,640]{1,0:T(8,128)(2,1)}) custom-call(s32[2]{0:T(128)S(1)} %pad_add_fusion.place_ref, bf16[640,128]{1,0:T(8,128)(2,1)S(1)} %shard_map.123.refs_0_, bf16[640,128]{1,0:T(8,128)(2,1)S(1)} %collective-permute-done.4.refs_1_, ...), custom_call_target="tpu_custom_call" | custom-call | tf_op jit(solution)/shard_map/pallas_call | solution.py:97
  116.4 2.2 %collective-permute-start.13 = (bf16[160,640]{1,0:T(8,128)(2,1)}, bf16[160,640]{1,0:T(8,128)(2,1)}, u32[]{:S(2)}, u32[]{:S(2)}) collective-permute-start(bf16[160,640]{1,0:T(8,128)(2,1)} %get-tuple-element.132), channel_id=1, source_target_pairs={{0,76},{4,64},{8,68},{12,72},{16,92},{20,80},{24,84},{28,88},{32,1... | collective-permute-start | bytes 614408 | tf_op jit(solution)/shard_map/ppermute | solution.py:60
  119.6 1.3 collective-permute-start.15
  121.6 29.0 %while.12 = (s32[]{:T(128)}, f32[4,2560]{1,0:T(4,128)}, f32[4,128]{1,0:T(4,128)S(1)}, s32[]{:T(128)}, s32[]{:T(128)}, /*index=5*/bf16[640,128]{1,0:T(8,128)(2,1)...) while((s32[]{:T(128)}, f32[4,2560]{1,0:T(4,128)}, ...), condition=%wide.region_1.2_spmd, body=%wide.region_0.1_spmd.sunk | while | flops 2 | bytes 1835233 | solution.py:340
  121.6 2.3 %body.2 = f32[64,8,128]{2,1,0:T(8,128)} custom-call(s32[2]{0:T(128)S(1)} %get-tuple-element.351.place_ref, f32[3,2560]{1,0:T(4,128)} %get-tuple-element.352.time_ref, bf16[640,128]{1,0:T(8,128)(2,1)S(1)} %get-tuple-element.300.refs_0_, bf16[640,128]{1,0:T(8,128)(2,1)S(1)} %get-tuple-element.301.refs_1_, bf16[640,128]{1,0:T(8,128)(2,1)S(1)} %get-tuple-element.302.refs_2_, ...), custom_call_target="tpu_custom_call" | custom-call | tf_op jit(solution)/shard_map/while/body/pallas_call | solution.py:324
  123.9 11.4 %all-to-all-start = ((f32[64,8,128]{2,1,0:T(8,128)}), f32[64,8,128]{2,1,0:T(8,128)S(1)}, u32[]{:S(2)}, u32[]{:S(2)}) async-start(f32[64,8,128]{2,1,0:T(8,128)} %body.2), calls=%async_computation | async-start | bytes 524288 | tf_op jit(solution)/shard_map/while/body/all_to_all | solution.py:333
  135.2 13.0 %all-to-all-done.chan_ref = f32[64,8,128]{2,1,0:T(8,128)S(1)} async-done(((f32[64,8,128]{2,1,0:T(8,128)}), f32[64,8,128]{2,1,0:T(8,128)S(1)}, u32[]{:S(2)}, u32[]{:S(2)}) %all-to-all-start) | async-done | bytes 262176 | tf_op jit(solution)/shard_map/while/body/all_to_all | solution.py:333
  148.9 1.7 %body.3 = f32[4,2560]{1,0:T(4,128)} custom-call(s32[1]{0:T(128)} %bitcast.21.index_ref, f32[4,128]{1,0:T(4,128)S(1)} %get-tuple-element.357.freq_ref, f32[4,128]{1,0:T(4,128)S(1)} %get-tuple-element.343.before_ref, f32[64,8,128]{2,1,0:T(8,128)} %copy-done.1), custom_call_target="tpu_custom_call" | custom-call | tf_op jit(solution)/shard_map/while/body/pallas_call | solution.py:97
  150.6 7.7 %collective-permute-done.18 = f32[4,2560]{1,0:T(4,128)S(1)} collective-permute-done((f32[4,2560]{1,0:T(4,128)}, f32[4,2560]{1,0:T(4,128)S(1)}, u32[]{:S(2)}, u32[]{:S(2)}) %collective-permute-start.18) | collective-permute-done | bytes 40992 | tf_op jit(solution)/shard_map/ppermute | solution.py:341
  158.4 2.3 %shard_map.128 = bf16[160,2560]{1,0:T(8,128)(2,1)} custom-call(s32[1]{0:T(128)} %bitcast.1.z_ref, bf16[160,640]{1,0:T(8,128)(2,1)} %collective-permute-done.12.a0, bf16[160,640]{1,0:T(8,128)(2,1)} %collective-permute-done.13.a1, bf16[160,640]{1,0:T(8,128)(2,1)} %collective-permute-done.14.a2, bf16[160,640]{1,0:T(8,128)(2,1)} %collective-permute-done.15.a3, ...), custom_call_target="tpu_custom_call" | custom-call | tf_op jit(solution)/shard_map/pallas_call | solution.py:97
  (60 shorter events, 8.6 us)
Async XLA Ops:
  0.6 46.9 %copy-start = (f32[1,256,2560]{2,1,0:T(8,128)S(1)}, f32[1,256,2560]{2,1,0:T(8,128)}, u32[]{:S(2)}) copy-start(f32[1,256,2560]{2,1,0:T(8,128)} %param.15) | copy-start | bytes 7864324
  2.2 10.0 %collective-permute-start = (f32[3,2560]{1,0:T(4,128)S(1)}, f32[3,2560]{1,0:T(4,128)}, u32[]{:S(2)}, u32[]{:S(2)}) collective-permute-start(f32[3,2560]{1,0:T(4,128)S(1)} %concatenate.19), channel_id=1, source_target_pairs={{64,0},{128,64},{192,128},{0,192},{65,1},{129,65},{193,129},{1,193... | collective-permute-start | bytes 92168 | tf_op jit(solution)/shard_map/ppermute | solution.py:274
  16.7 24.9 %copy-start.9 = (f32[256]{0:T(256)S(1)}, f32[256]{0:T(256)}, u32[]{:S(2)}) copy-start(f32[256]{0:T(256)} %constant.97.clone) | copy-start | bytes 3076
  16.7 24.9 %copy-start.8 = (f32[128]{0:T(128)S(1)}, f32[128]{0:T(128)}, u32[]{:S(2)}) copy-start(f32[128]{0:T(128)} %constant.96.clone) | copy-start | bytes 1540
  16.7 25.0 %copy-start.3 = (bf16[3,160,128]{2,1,0:T(8,128)(2,1)S(1)}, bf16[3,160,128]{2,1,0:T(8,128)(2,1)}, u32[]{:S(2)}) copy-start(bf16[3,160,128]{2,1,0:T(8,128)(2,1)} %get-tuple-element.119.q0) | copy-start | bytes 368644
  16.7 8.4 %collective-permute-start.1 = (bf16[3,160,128]{2,1,0:T(8,128)(2,1)}, bf16[3,160,128]{2,1,0:T(8,128)(2,1)S(1)}, u32[]{:S(2)}, u32[]{:S(2)}) collective-permute-start(bf16[3,160,128]{2,1,0:T(8,128)(2,1)} %get-tuple-element.120), channel_id=1, source_target_pairs={{0,4},{4,8},{8,12},{12,0},{16,20},{20,24},{24,28},{28,16},{32,36},... | collective-permute-start | bytes 368648 | tf_op jit(solution)/shard_map/ppermute | solution.py:30
  17.8 10.8 %collective-permute-start.2 = (bf16[3,160,128]{2,1,0:T(8,128)(2,1)}, bf16[3,160,128]{2,1,0:T(8,128)(2,1)S(1)}, u32[]{:S(2)}, u32[]{:S(2)}) collective-permute-start(bf16[3,160,128]{2,1,0:T(8,128)(2,1)} %get-tuple-element.121), channel_id=1, source_target_pairs={{0,8},{4,12},{8,0},{12,4},{16,24},{20,28},{24,16},{28,20},{32,40},... | collective-permute-start | bytes 368648 | tf_op jit(solution)/shard_map/ppermute | solution.py:30
  19.3 9.3 %collective-permute-start.3 = (bf16[3,160,128]{2,1,0:T(8,128)(2,1)}, bf16[3,160,128]{2,1,0:T(8,128)(2,1)S(1)}, u32[]{:S(2)}, u32[]{:S(2)}) collective-permute-start(bf16[3,160,128]{2,1,0:T(8,128)(2,1)} %get-tuple-element.122), channel_id=1, source_target_pairs={{0,12},{4,0},{8,4},{12,8},{16,28},{20,16},{24,20},{28,24},{32,44},... | collective-permute-start | bytes 368648 | tf_op jit(solution)/shard_map/ppermute | solution.py:30
  25.2 16.6 %copy-start.4 = (bf16[3,160,128]{2,1,0:T(8,128)(2,1)}, bf16[3,160,128]{2,1,0:T(8,128)(2,1)S(1)}, u32[]{:S(2)}) copy-start(bf16[3,160,128]{2,1,0:T(8,128)(2,1)S(1)} %collective-permute-done.1.q1) | copy-start | bytes 368644
  28.6 13.2 %copy-start.5 = (bf16[3,160,128]{2,1,0:T(8,128)(2,1)}, bf16[3,160,128]{2,1,0:T(8,128)(2,1)S(1)}, u32[]{:S(2)}) copy-start(bf16[3,160,128]{2,1,0:T(8,128)(2,1)S(1)} %collective-permute-done.2.q2) | copy-start | bytes 368644
  28.6 13.2 %copy-start.6 = (bf16[3,160,128]{2,1,0:T(8,128)(2,1)}, bf16[3,160,128]{2,1,0:T(8,128)(2,1)S(1)}, u32[]{:S(2)}) copy-start(bf16[3,160,128]{2,1,0:T(8,128)(2,1)S(1)} %collective-permute-done.3.q3) | copy-start | bytes 368644
  28.6 62.0 %all-to-all-start.1 = ((bf16[16,3,160,128]{3,2,1,0:T(8,128)(2,1)}), bf16[16,3,160,128]{3,2,1,0:T(8,128)(2,1)}, u32[]{:S(2)}, u32[]{:S(2)}) async-start(bf16[16,3,160,128]{3,2,1,0:T(8,128)(2,1)} %get-tuple-element.123), calls=%async_computation.1 | async-start | bytes 3932160 | tf_op jit(solution)/shard_map/all_to_all | solution.py:293
  38.2 62.0 %collective-permute-start.10 = (bf16[160,640]{1,0:T(8,128)(2,1)}, bf16[160,640]{1,0:T(8,128)(2,1)}, u32[]{:S(2)}, u32[]{:S(2)}) collective-permute-start(bf16[160,640]{1,0:T(8,128)(2,1)} %get-tuple-element.128), channel_id=1, source_target_pairs={{0,196},{4,200},{8,204},{12,192},{16,212},{20,216},{24,220},{28,20... | collective-permute-start | bytes 614408 | tf_op jit(solution)/shard_map/ppermute | solution.py:64
  40.4 61.9 %collective-permute-start.11 = (bf16[160,640]{1,0:T(8,128)(2,1)}, bf16[160,640]{1,0:T(8,128)(2,1)}, u32[]{:S(2)}, u32[]{:S(2)}) collective-permute-start(bf16[160,640]{1,0:T(8,128)(2,1)} %get-tuple-element.129), channel_id=1, source_target_pairs={{0,200},{4,204},{8,192},{12,196},{16,216},{20,220},{24,208},{28,21... | collective-permute-start | bytes 614408 | tf_op jit(solution)/shard_map/ppermute | solution.py:64
  41.8 64.3 %copy-start.2 = (bf16[2,640,128]{2,1,0:T(8,128)(2,1)}, bf16[2,640,128]{2,1,0:T(8,128)(2,1)S(1)}, u32[]{:S(2)}) copy-start(bf16[2,640,128]{2,1,0:T(8,128)(2,1)S(1)} %pad_maximum_fusion.s0) | copy-start | bytes 983044
  41.9 61.5 %collective-permute-start.7 = (bf16[2,640,128]{2,1,0:T(8,128)(2,1)S(1)}, bf16[2,640,128]{2,1,0:T(8,128)(2,1)S(1)}, u32[]{:S(2)}, u32[]{:S(2)}) collective-permute-start(bf16[2,640,128]{2,1,0:T(8,128)(2,1)S(1)} %pad_maximum_fusion.s0), channel_id=1, source_target_pairs={{0,16},{4,20},{8,24},{12,28},{16,32},{20,36},{24,40},{28,44},{32,4... | collective-permute-start | bytes 983048 | tf_op jit(solution)/shard_map/ppermute | solution.py:35
  43.4 62.0 %collective-permute-start.8 = (bf16[2,640,128]{2,1,0:T(8,128)(2,1)S(1)}, bf16[2,640,128]{2,1,0:T(8,128)(2,1)}, u32[]{:S(2)}, u32[]{:S(2)}) collective-permute-start(bf16[2,640,128]{2,1,0:T(8,128)(2,1)S(1)} %pad_maximum_fusion.s0), channel_id=1, source_target_pairs={{0,32},{4,36},{8,40},{12,44},{16,48},{20,52},{24,56},{28,60},{32,0... | collective-permute-start | bytes 983048 | tf_op jit(solution)/shard_map/ppermute | solution.py:35
  46.1 60.0 %collective-permute-start.9 = (bf16[2,640,128]{2,1,0:T(8,128)(2,1)S(1)}, bf16[2,640,128]{2,1,0:T(8,128)(2,1)}, u32[]{:S(2)}, u32[]{:S(2)}) collective-permute-start(bf16[2,640,128]{2,1,0:T(8,128)(2,1)S(1)} %pad_maximum_fusion.s0), channel_id=1, source_target_pairs={{0,48},{4,52},{8,56},{12,60},{16,0},{20,4},{24,8},{28,12},{32,16},... | collective-permute-start | bytes 983048 | tf_op jit(solution)/shard_map/ppermute | solution.py:35
  100.1 19.4 %collective-permute-start.16 = (bf16[160,640]{1,0:T(8,128)(2,1)}, bf16[160,640]{1,0:T(8,128)(2,1)}, u32[]{:S(2)}, u32[]{:S(2)}) collective-permute-start(bf16[160,640]{1,0:T(8,128)(2,1)} %get-tuple-element.137), channel_id=1, source_target_pairs={{0,192},{4,196},{8,200},{12,204},{16,208},{20,212},{24,216},{28,22... | collective-permute-start | bytes 614408 | tf_op jit(solution)/shard_map/ppermute | solution.py:64
  102.3 12.0 %collective-permute-start.5 = (bf16[640,128]{1,0:T(8,128)(2,1)}, bf16[640,128]{1,0:T(8,128)(2,1)S(1)}, u32[]{:S(2)}, u32[]{:S(2)}) collective-permute-start(bf16[640,128]{1,0:T(8,128)(2,1)} %get-tuple-element.126), channel_id=1, source_target_pairs={{0,32},{4,36},{8,40},{12,44},{16,48},{20,52},{24,56},{28,60},{32,0... | collective-permute-start | bytes 491528 | tf_op jit(solution)/shard_map/ppermute | solution.py:35
  103.3 0.7 copy-start.7
  104.0 10.3 %collective-permute-start.4 = (bf16[640,128]{1,0:T(8,128)(2,1)}, bf16[640,128]{1,0:T(8,128)(2,1)S(1)}, u32[]{:S(2)}, u32[]{:S(2)}) collective-permute-start(bf16[640,128]{1,0:T(8,128)(2,1)} %get-tuple-element.125), channel_id=1, source_target_pairs={{0,48},{4,52},{8,56},{12,60},{16,0},{20,4},{24,8},{28,12},{32,16},... | collective-permute-start | bytes 491528 | tf_op jit(solution)/shard_map/ppermute | solution.py:35
  105.4 8.9 %collective-permute-start.6 = (bf16[640,128]{1,0:T(8,128)(2,1)}, bf16[640,128]{1,0:T(8,128)(2,1)}, u32[]{:S(2)}, u32[]{:S(2)}) collective-permute-start(bf16[640,128]{1,0:T(8,128)(2,1)} %get-tuple-element.127), channel_id=1, source_target_pairs={{0,16},{4,20},{8,24},{12,28},{16,32},{20,36},{24,40},{28,44},{32,4... | collective-permute-start | bytes 491528 | tf_op jit(solution)/shard_map/ppermute | solution.py:35
  106.1 14.9 %collective-permute-start.17 = (bf16[160,640]{1,0:T(8,128)(2,1)}, bf16[160,640]{1,0:T(8,128)(2,1)}, u32[]{:S(2)}, u32[]{:S(2)}) collective-permute-start(bf16[160,640]{1,0:T(8,128)(2,1)} %get-tuple-element.139), channel_id=1, source_target_pairs={{0,204},{4,192},{8,196},{12,200},{16,220},{20,208},{24,212},{28,21... | collective-permute-start | bytes 614408 | tf_op jit(solution)/shard_map/ppermute | solution.py:64
  116.4 42.0 %collective-permute-start.12 = (bf16[160,640]{1,0:T(8,128)(2,1)}, bf16[160,640]{1,0:T(8,128)(2,1)}, u32[]{:S(2)}, u32[]{:S(2)}) collective-permute-start(bf16[160,640]{1,0:T(8,128)(2,1)} %get-tuple-element.131), channel_id=1, source_target_pairs={{0,64},{4,68},{8,72},{12,76},{16,80},{20,84},{24,88},{28,92},{32,9... | collective-permute-start | bytes 614408 | tf_op jit(solution)/shard_map/ppermute | solution.py:60
  116.4 42.0 %collective-permute-start.13 = (bf16[160,640]{1,0:T(8,128)(2,1)}, bf16[160,640]{1,0:T(8,128)(2,1)}, u32[]{:S(2)}, u32[]{:S(2)}) collective-permute-start(bf16[160,640]{1,0:T(8,128)(2,1)} %get-tuple-element.132), channel_id=1, source_target_pairs={{0,76},{4,64},{8,68},{12,72},{16,92},{20,80},{24,84},{28,88},{32,1... | collective-permute-start | bytes 614408 | tf_op jit(solution)/shard_map/ppermute | solution.py:60
  118.6 39.8 %collective-permute-start.14 = (bf16[160,640]{1,0:T(8,128)(2,1)}, bf16[160,640]{1,0:T(8,128)(2,1)}, u32[]{:S(2)}, u32[]{:S(2)}) collective-permute-start(bf16[160,640]{1,0:T(8,128)(2,1)} %get-tuple-element.133), channel_id=1, source_target_pairs={{0,72},{4,76},{8,64},{12,68},{16,88},{20,92},{24,80},{28,84},{32,1... | collective-permute-start | bytes 614408 | tf_op jit(solution)/shard_map/ppermute | solution.py:60
  119.6 38.8 %collective-permute-start.15 = (bf16[160,640]{1,0:T(8,128)(2,1)}, bf16[160,640]{1,0:T(8,128)(2,1)}, u32[]{:S(2)}, u32[]{:S(2)}) collective-permute-start(bf16[160,640]{1,0:T(8,128)(2,1)} %get-tuple-element.134), channel_id=1, source_target_pairs={{0,68},{4,72},{8,76},{12,64},{16,84},{20,88},{24,92},{28,80},{32,1... | collective-permute-start | bytes 614408 | tf_op jit(solution)/shard_map/ppermute | solution.py:60
  123.9 24.4 %all-to-all-start = ((f32[64,8,128]{2,1,0:T(8,128)}), f32[64,8,128]{2,1,0:T(8,128)S(1)}, u32[]{:S(2)}, u32[]{:S(2)}) async-start(f32[64,8,128]{2,1,0:T(8,128)} %body.2), calls=%async_computation | async-start | bytes 524288 | tf_op jit(solution)/shard_map/while/body/all_to_all | solution.py:333
  148.2 0.7 copy-start.1
  150.6 7.8 %collective-permute-start.18 = (f32[4,2560]{1,0:T(4,128)}, f32[4,2560]{1,0:T(4,128)S(1)}, u32[]{:S(2)}, u32[]{:S(2)}) collective-permute-start(f32[4,2560]{1,0:T(4,128)} %get-tuple-element.141), channel_id=1, source_target_pairs={{0,64},{64,128},{128,192},{192,0},{1,65},{65,129},{129,193},{193,1... | collective-permute-start | bytes 122888 | tf_op jit(solution)/shard_map/ppermute | solution.py:341

commit v2 on v1

--- a/solution.py
+++ b/solution.py
@@ -46,22 +46,14 @@
     return got
 
 
-def section_pairs(turn, by):
+def onward(value, back):
     count = SIDE * SIDE
     pairs = []
     for seg in range(SIDE):
         for i in range(count):
-            target = (seg + turn) % SIDE * count + i // SIDE * SIDE + (i + by) % SIDE
+            target = (seg + 1) % SIDE * count + (i - back * SIDE) % count
             pairs.append((seg * count + i, target))
-    return pairs
-
-
-def home(value, by):
-    return lax.ppermute(value, ("segment", "ctx"), section_pairs(1, by))
-
-
-def away(value, by):
-    return lax.ppermute(value, ("segment", "ctx"), section_pairs(SIDE - 1, by))
+    return lax.ppermute(value, ("segment", "ctx"), pairs)
 
 
 def rope_tables(pos):
@@ -144,7 +136,15 @@
         for to_x in range(SIDE):
             for to_z in range(SIDE):
                 at = (to_z * GROUP + to_x) * HEAD_DIM
-                main_ref[to_x * SIDE + to_z, part] = head_of(slice(at, at + HEAD_DIM))
+                if part < 2:
+                    main_ref[to_x * SIDE + to_z, part] = head_of(slice(at, at + HEAD_DIM))
+
+
+def cut_values_kernel(v_ref, out_ref):
+    for to_x in range(SIDE):
+        for to_z in range(SIDE):
+            at = (to_z * GROUP + to_x) * HEAD_DIM
+            out_ref[to_x * SIDE + to_z] = v_ref[0, :, at : at + HEAD_DIM]
 
 
 def cut_cotangent_kernel(z_ref, cot_ref, *outs):
@@ -174,14 +174,12 @@
         out_ref[at : at + TILE] = attend(q, [b[0] for b in blocks], [b[1] for b in blocks])
 
 
-def main_kernel(back, x_ref, r_ref, *outs):
+def main_kernel(back, x_ref, r_ref, v_ref, *outs):
     x = x_ref[0]
 
-    def four(part, first):
-        return r_ref[pl.ds(first * SIDE, SIDE), part].reshape(ROWS, HEAD_DIM)
-
-    keys = [four(1, m) for m in range(SIDE)]
-    values = [four(2, m) for m in range(SIDE)]
+    fours = [pl.ds(m * SIDE, SIDE) for m in range(SIDE)]
+    keys = [r_ref[four, 1].reshape(ROWS, HEAD_DIM) for four in fours]
+    values = [v_ref[four].reshape(ROWS, HEAD_DIM) for four in fours]
     for step, out_ref in zip(back, outs, strict=True):
         first = lax.rem(x + SIDE - step, SIDE) * SIDE
         for i in range(ROWS // TILE):
@@ -216,7 +214,7 @@
             attn = refs[source][rows_of(z, source, step)].astype(jnp.float32)
             total = total + attn * cots[step][:, column(place)].astype(jnp.float32)
         chan_ref[pl.ds(place, 1)] = jnp.sum(total, axis=0, keepdims=True)
-    chan_ref[GROUP : GROUP + 1] = time_ref[2:3, :HEAD_DIM]
+    chan_ref[GROUP : GROUP + 1] = time_ref[...]
     for i in range(out_ref.shape[0]):
         out_ref[i] = chan_ref[...]
 
@@ -269,18 +267,24 @@
     flat = shape((TOK, GROUP * HEAD_DIM))
 
     step = timesteps[0, 0]
-    when = jnp.full((1, WIDTH), step.astype(jnp.float32))
-    gains = jnp.concatenate([qk_gain[0], when])
-    gains = lax.ppermute(gains, "segment", [((i + 1) % SIDE, i) for i in range(SIDE)])
+    when = jnp.full((1, HEAD_DIM), step.astype(jnp.float32))
+    gains = lax.ppermute(qk_gain[0], "segment", [((i + 1) % SIDE, i) for i in range(SIDE)])
     parts = qkv[0, 0].transpose(1, 0, 2)
     cots = call(cut_cotangent_kernel, [flat] * SIDE, 0, 1_600_000, z, cotangent[0, 0])
-    cots_z = [None] * SIDE
-    for k in (2, 1):
-        cots_z[k] = away(cots[k], k)
+    cots_z = [cots[0], along_z(cots[1], 1), along_z(cots[2], 2), None]
+    values = call(
+        cut_values_kernel,
+        shape((count, TOK, HEAD_DIM)),
+        0,
+        1_600_000,
+        parts,
+        specs=[one_of(2, (TOK, WIDTH))],
+    )
+    values = lax.all_to_all(values, "ctx", 0, 0)
     cosine, sine = rope_tables(positions[0])
     main, *shared = call(
         prep_kernel,
-        [shape((count, 3, TOK, HEAD_DIM))] + [block] * SIDE,
+        [shape((count, 2, TOK, HEAD_DIM))] + [block] * SIDE,
         10_000_000,
         5_000_000,
         z,
@@ -290,7 +294,7 @@
         sine,
     )
     shared_z = exchanged(along_z, shared)
-    main = lax.all_to_all(after(main, shared_z), "ctx", 0, 0)
+    main = lax.all_to_all(after(main, (values, shared_z)), "ctx", 0, 0)
     pair = jnp.concatenate([b[1:] for b in shared_z], axis=1)
     pairs = [pair] + [along_x(pair, k) for k in steps]
     gate = jnp.dot(embed(step), mod_weight[0], precision=lax.Precision.HIGHEST)[None]
@@ -298,26 +302,25 @@
     index = (ctx * SIDE + lax.axis_index("dp").astype(jnp.int32)) * rows
     freq = lax.dynamic_slice_in_dim(np.tile(frequencies(), 2), index, rows)
     freq = jnp.broadcast_to(freq[:, None], (rows, HEAD_DIM))
-    shared_out = call(
-        shared_kernel, single, 840_000_000, 1_600_000, *shared_z, *pairs, smem=0
-    )
     main, gate, freq = lax.optimization_barrier((main, gate, freq))
     back = [None] * SIDE
     back[2], back[1], back[3] = call(
-        functools.partial(main_kernel, (2, 1, 3)), [single] * 3, 2_500_000_000, 2_500_000, x, main
+        functools.partial(main_kernel, (2, 1, 3)), [single] * 3, 2_500_000_000, 2_500_000, x, main, values
     )
     (back[0],) = call(
-        functools.partial(main_kernel, (0,)), [single], 840_000_000, 2_000_000, x, main
-    )
-    for k in (3, 0):
-        cots_z[k] = away(after(cots[k], back[2]), k)
-    back = [back[0]] + [along_x(back[m], SIDE - m) for m in steps]
+        functools.partial(main_kernel, (0,)), [single], 840_000_000, 2_000_000, x, main, values
+    )
+    shared_out = call(
+        shared_kernel, single, 840_000_000, 1_600_000, *after(shared_z, back[2]), *pairs, smem=0
+    )
+    cots_z[3] = along_z(after(cots[3], back[2]), 3)
+    for m in (2, 1, 3, 0):
+        back[m] = onward(back[m], m)
+    shared_out = onward(shared_out, 0)
     joined = call(
-        join_kernel, [flat] * SIDE, 0, 1_600_000, place, *back, after(shared_out, cots_z[1:3])
-    )
-    at_home = [None] * SIDE
-    for k in (2, 1, 3, 0):
-        at_home[k] = home(joined[k], (SIDE - k) % SIDE)
+        join_kernel, [flat] * SIDE, 0, 1_600_000, place, *back, after(shared_out, cots_z[1:])
+    )
+    at_home = [joined[0]] + [along_z(joined[k], SIDE - k) for k in steps]
 
     def gradient(_, state):
         attn, before = lax.optimization_barrier(([*back, shared_out], state[1]))
@@ -329,7 +332,7 @@
             scratch_shapes=[pltpu.VMEM((8, HEAD_DIM), jnp.float32)],
             compiler_params=VMEM,
             cost_estimate=pl.CostEstimate(flops=0, bytes_accessed=0, transcendentals=0),
-        )(place, gains, *attn, *cots_z)
+        )(place, when, *attn, *cots_z)
         chans = lax.all_to_all(chans, ("ctx", "dp"), 0, 0)
         grad = call(grad_kernel, zeros, 0, 200_000, index[None], freq, before, chans)
         return (grad, before)
@@ -338,10 +341,9 @@
     turns = jnp.where(step < 1000, 1, 2)
     start = (jnp.zeros((rows, WIDTH), jnp.float32), jnp.zeros((rows, HEAD_DIM), jnp.float32))
     grad, _ = lax.fori_loop(0, turns, gradient, start)
-    grad = lax.ppermute(grad, "segment", [(i, (i + 1) % SIDE) for i in range(SIDE)])
 
     attn_out = call(
-        finish_kernel, shape((TOK, WIDTH)), 500_000, 1_700_000, z, *at_home, gate
+        finish_kernel, shape((TOK, WIDTH)), 500_000, 1_700_000, z, *after(at_home, grad), gate
     )
     return (attn_out[None, None], grad[None])
 

time: 162 us -> 168 us (1.037)
  starting transfers between devices: 48.8 us -> 54.4 us
  Pallas kernels: 32.5 us -> 35.8 us
  waiting for transfers between devices: 69.3 us -> 66.5 us
    all_to_all x1 -> x2, waiting for transfers between devices: 41.1 us -> 25.3 us  [the longest x1 25.2 us: local(): main = lax.all_to_all(after(main, (values, shared_z)), 'ctx', 0, 0)]
    ppermute x10 -> x6, waiting for transfers between devices: 7.77 us -> 22.8 us  [the longest x5 17.1 us: onward(): return lax.ppermute(value, ('segment', 'ctx'), pairs)]
    all_to_all x1 -> x2, starting transfers between devices: 7.46 us -> 15.2 us  [the longest x1 8.47 us: local(): values = lax.all_to_all(values, 'ctx', 0, 0)]
    ppermute x3 -> x9, starting transfers between devices: 4.47 us -> 10.6 us  [along_z(): return lax.ppermute(value, 'ctx', pairs)]
    ppermute x10 -> x6, starting transfers between devices: 16.8 us -> 13.2 us  [the longest x5 9.47 us: onward(): return lax.ppermute(value, ('segment', 'ctx'), pairs)]
    pallas_call x8 -> x9, Pallas kernels: 30.3 us -> 33.5 us  [call(): pl.pallas_call(kernel, grid=grid, out_shape=out_shape, in_specs=specs, ou...]
    ppermute x6 -> x3, starting transfers between devices: 8.69 us -> 5.6 us  [along_x(): return lax.ppermute(value, 'ctx', pairs)]
    all_to_all x1, waiting for transfers between devices: 13 us -> 10.6 us  [gradient(): chans = lax.all_to_all(chans, ('ctx', 'dp'), 0, 0)]
  transfers between devices with their start and end apart: 21 -> 21, of which waited for: 5 -> 9; matrix products, arithmetic and copies ran while one was open for 4% -> 4% of each run, Pallas kernels for 16% -> 18%
where the time goes in v2:
time: 168 us; the launch traced here: 167 us
  waiting for transfers between devices  66.5 us (40%)
  starting transfers between devices  54.4 us (32%)
  Pallas kernels  35.8 us (21%)
  local copies, waits for them, and re-layouts  5.11 us (3%)
  other arithmetic  2.15 us (1%)
  matrix products  1.94 us (1%)
    pallas_call x9, Pallas kernels, call(): pl.pallas_call(kernel, grid=grid, out_shape=out_shape, in_specs=specs, ou...  33.5 us
    all_to_all x1, waiting for transfers between devices, local(): main = lax.all_to_all(after(main, (values, shared_z)), 'ctx', 0, 0)  25.2 us
    ppermute x5, waiting for transfers between devices, onward(): return lax.ppermute(value, ('segment', 'ctx'), pairs)  17.1 us
    all_to_all x1, waiting for transfers between devices, gradient(): chans = lax.all_to_all(chans, ('ctx', 'dp'), 0, 0)  10.6 us
    ppermute x9, starting transfers between devices, along_z(): return lax.ppermute(value, 'ctx', pairs)  10.6 us
    all_to_all x1, starting transfers between devices, gradient(): chans = lax.all_to_all(chans, ('ctx', 'dp'), 0, 0)  9.72 us
    ppermute x5, starting transfers between devices, onward(): return lax.ppermute(value, ('segment', 'ctx'), pairs)  9.47 us
    all_to_all x1, starting transfers between devices, local(): values = lax.all_to_all(values, 'ctx', 0, 0)  8.47 us
  transfers between devices with their start and end apart: 21, of which 9 were waited for; matrix products, arithmetic and copies ran while one was open for 4% of the time, Pallas kernels for 18%

profile of v2, /device:TPU:8, one launch (start us, length us, event | category | flops | bytes accessed | tf_op | source)
XLA Modules:
  0.0 167.3 jit_solution(4189349180997702910)
XLA Ops:
  0.7 2.2 %shard_map.123 = bf16[16,160,128]{2,1,0:T(8,128)(2,1)} custom-call(bf16[3,160,2560]{2,1,0:T(8,128)(2,1)} %bitcast.22), custom_call_target="tpu_custom_call" | custom-call | tf_op jit(solution)/shard_map/pallas_call | solution.py:89
  3.0 8.5 %all-to-all-start.1 = ((bf16[16,160,128]{2,1,0:T(8,128)(2,1)}), bf16[16,160,128]{2,1,0:T(8,128)(2,1)S(1)}, u32[]{:S(2)}, u32[]{:S(2)}) async-start(bf16[16,160,128]{2,1,0:T(8,128)(2,1)} %shard_map.123), calls=%async_computation.1 | async-start | bytes 1310720 | tf_op jit(solution)/shard_map/all_to_all | solution.py:283
  11.4 3.7 %collective-permute-start = (f32[2,2560]{1,0:T(2,128)S(1)}, f32[2,2560]{1,0:T(2,128)S(1)}, u32[]{:S(2)}, u32[]{:S(2)}) collective-permute-start(f32[2,2560]{1,0:T(2,128)S(1)} %bitcast.31), channel_id=1, source_target_pairs={{64,0},{128,64},{192,128},{0,192},{65,1},{129,65},{193,129},{1,193... | collective-permute-start | bytes 61448 | tf_op jit(solution)/shard_map/ppermute | solution.py:271
  16.5 5.8 %collective-permute-done.gain_ref = f32[2,2560]{1,0:T(2,128)S(1)} collective-permute-done((f32[2,2560]{1,0:T(2,128)S(1)}, f32[2,2560]{1,0:T(2,128)S(1)}, u32[]{:S(2)}, u32[]{:S(2)}) %collective-permute-start) | collective-permute-done | bytes 20512 | tf_op jit(solution)/shard_map/ppermute | solution.py:271
  22.8 4.3 %shard_map.122 = (bf16[16,2,160,128]{3,2,1,0:T(8,128)(2,1)}, bf16[3,160,128]{2,1,0:T(8,128)(2,1)}, bf16[3,160,128]{2,1,0:T(8,128)(2,1)}, bf16[3,160,128]{2,1,0:T(8,128)(2,1)}, bf16[3,160,128]{2,1,0:T(8,128)(2,1)}) custom-call(s32[1]{0:T(128)} %bitcast.z_ref, bf16[3,160,2560]{2,1,0:T(8,128)(2,1)} %bitcast.23, f32[2,2560]{1,0:T(2,128)} %copy-done.6, ...), custom_call_target="tpu_custom_call" | custom-call | tf_op jit(solution)/shard_map/pallas_call | solution.py:89
  27.2 4.4 %collective-permute-start.2 = (bf16[3,160,128]{2,1,0:T(8,128)(2,1)}, bf16[3,160,128]{2,1,0:T(8,128)(2,1)S(1)}, u32[]{:S(2)}, u32[]{:S(2)}) collective-permute-start(bf16[3,160,128]{2,1,0:T(8,128)(2,1)} %get-tuple-element.128), channel_id=1, source_target_pairs={{0,8},{4,12},{8,0},{12,4},{16,24},{20,28},{24,16},{28,20},{32,40},... | collective-permute-start | bytes 368648 | tf_op jit(solution)/shard_map/ppermute | solution.py:30
  31.5 2.6 %collective-permute-done.1.q1 = bf16[3,160,128]{2,1,0:T(8,128)(2,1)S(1)} collective-permute-done((bf16[3,160,128]{2,1,0:T(8,128)(2,1)}, bf16[3,160,128]{2,1,0:T(8,128)(2,1)S(1)}, u32[]{:S(2)}, u32[]{:S(2)}) %collective-permute-start.1) | collective-permute-done | bytes 122912 | tf_op jit(solution)/shard_map/ppermute | solution.py:30
  34.1 2.7 %collective-permute-done.2.q2 = bf16[3,160,128]{2,1,0:T(8,128)(2,1)S(1)} collective-permute-done((bf16[3,160,128]{2,1,0:T(8,128)(2,1)}, bf16[3,160,128]{2,1,0:T(8,128)(2,1)S(1)}, u32[]{:S(2)}, u32[]{:S(2)}) %collective-permute-start.2) | collective-permute-done | bytes 122912 | tf_op jit(solution)/shard_map/ppermute | solution.py:30
  37.4 2.5 %collective-permute-done.3.q3 = bf16[3,160,128]{2,1,0:T(8,128)(2,1)} collective-permute-done((bf16[3,160,128]{2,1,0:T(8,128)(2,1)}, bf16[3,160,128]{2,1,0:T(8,128)(2,1)}, u32[]{:S(2)}, u32[]{:S(2)}) %collective-permute-start.3) | collective-permute-done | bytes 122912 | tf_op jit(solution)/shard_map/ppermute | solution.py:30
  39.9 6.7 %all-to-all-start.2 = ((bf16[16,2,160,128]{3,2,1,0:T(8,128)(2,1)}), bf16[16,2,160,128]{3,2,1,0:T(8,128)(2,1)}, u32[]{:S(2)}, u32[]{:S(2)}) async-start(bf16[16,2,160,128]{3,2,1,0:T(8,128)(2,1)} %get-tuple-element.130), calls=%async_computation.2 | async-start | bytes 2621440 | tf_op jit(solution)/shard_map/all_to_all | solution.py:297
  46.7 2.2 %shard_map.127 = (bf16[160,640]{1,0:T(8,128)(2,1)}, bf16[160,640]{1,0:T(8,128)(2,1)}, bf16[160,640]{1,0:T(8,128)(2,1)}, bf16[160,640]{1,0:T(8,128)(2,1)}) custom-call(s32[1]{0:T(128)} %bitcast.z_ref, bf16[160,2560]{1,0:T(8,128)(2,1)} %bitcast.25), custom_call_target="tpu_custom_call" | custom-call | tf_op jit(solution)/shard_map/pallas_call | solution.py:89
  48.8 1.9 %collective-permute-start.12 = (bf16[160,640]{1,0:T(8,128)(2,1)}, bf16[160,640]{1,0:T(8,128)(2,1)}, u32[]{:S(2)}, u32[]{:S(2)}) collective-permute-start(bf16[160,640]{1,0:T(8,128)(2,1)} %get-tuple-element.139), channel_id=1, source_target_pairs={{0,4},{4,8},{8,12},{12,0},{16,20},{20,24},{24,28},{28,16},{32,36},... | collective-permute-start | bytes 614408 | tf_op jit(solution)/shard_map/ppermute | solution.py:30
  50.7 2.4 %collective-permute-start.13 = (bf16[160,640]{1,0:T(8,128)(2,1)}, bf16[160,640]{1,0:T(8,128)(2,1)}, u32[]{:S(2)}, u32[]{:S(2)}) collective-permute-start(bf16[160,640]{1,0:T(8,128)(2,1)} %get-tuple-element.140), channel_id=1, source_target_pairs={{0,8},{4,12},{8,0},{12,4},{16,24},{20,28},{24,16},{28,20},{32,40},... | collective-permute-start | bytes 614408 | tf_op jit(solution)/shard_map/ppermute | solution.py:30
  56.3 1.5 collective-permute-start.8
  57.8 2.7 %collective-permute-start.9 = (bf16[2,640,128]{2,1,0:T(8,128)(2,1)}, bf16[2,640,128]{2,1,0:T(8,128)(2,1)}, u32[]{:S(2)}, u32[]{:S(2)}) collective-permute-start(bf16[2,640,128]{2,1,0:T(8,128)(2,1)} %pad_maximum_fusion.s0), channel_id=1, source_target_pairs={{0,32},{4,36},{8,40},{12,44},{16,48},{20,52},{24,56},{28,60},{32,0... | collective-permute-start | bytes 983048 | tf_op jit(solution)/shard_map/ppermute | solution.py:35
  62.0 1.9 %fusion.2.gate_ref = f32[1,2560]{1,0:T(1,128)} fusion(f32[256,1]{0,1:T(1,128)S(1)} %bitcast.27, f32[1,256,2560]{2,1,0:T(8,128)S(1)} %copy-done), kind=kOutput, calls=%fused_computation.1 | convolution fusion | flops 7864320 | bytes 2632704 | tf_op jit(solution)/shard_map/dot_general | solution.py:300
  64.0 25.2 %all-to-all-done.2.r_ref = bf16[16,2,160,128]{3,2,1,0:T(8,128)(2,1)} async-done(((bf16[16,2,160,128]{3,2,1,0:T(8,128)(2,1)}), bf16[16,2,160,128]{3,2,1,0:T(8,128)(2,1)}, u32[]{:S(2)}, u32[]{:S(2)}) %all-to-all-start.2) | async-done | bytes 1310752 | tf_op jit(solution)/shard_map/all_to_all | solution.py:297
  89.3 9.4 %shard_map.125 = (bf16[640,128]{1,0:T(8,128)(2,1)}, bf16[640,128]{1,0:T(8,128)(2,1)}, bf16[640,128]{1,0:T(8,128)(2,1)}) custom-call(s32[1]{0:T(128)} %bitcast.1.x_ref, bf16[16,2,160,128]{3,2,1,0:T(8,128)(2,1)} %all-to-all-done.2.r_ref, bf16[16,160,128]{2,1,0:T(8,128)(2,1)} %copy-done.2), custom_call_target="tpu_custom_call" | custom-call | tf_op jit(solution)/shard_map/pallas_call | solution.py:89
  98.7 4.8 %shard_map.126 = bf16[640,128]{1,0:T(8,128)(2,1)} custom-call(bf16[3,160,128]{2,1,0:T(8,128)(2,1)} %get-tuple-element.135.q0, bf16[3,160,128]{2,1,0:T(8,128)(2,1)} %copy-done.4, bf16[3,160,128]{2,1,0:T(8,128)(2,1)} %copy-done.5, bf16[3,160,128]{2,1,0:T(8,128)(2,1)} %collective-permute-done.3.q3, bf16[2,640,128]{2,1,0:T(8,128)(2,1)} %pad_maximum_fusion.s0, ...), custom_call_target="tpu_custom_call" | custom-call | tf_op jit(solution)/shard_map/pallas_call | solution.py:89
  103.5 1.9 %collective-permute-start.11 = (bf16[640,128]{1,0:T(8,128)(2,1)}, bf16[640,128]{1,0:T(8,128)(2,1)S(1)}, u32[]{:S(2)}, u32[]{:S(2)}) collective-permute-start(bf16[640,128]{1,0:T(8,128)(2,1)} %shard_map.126), channel_id=1, source_target_pairs={{0,64},{4,68},{8,72},{12,76},{16,80},{20,84},{24,88},{28,92},{32,9... | collective-permute-start | bytes 491528 | tf_op jit(solution)/shard_map/ppermute | solution.py:56
  105.4 5.7 %collective-permute-start.6 = (bf16[640,128]{1,0:T(8,128)(2,1)}, bf16[640,128]{1,0:T(8,128)(2,1)S(1)}, u32[]{:S(2)}, u32[]{:S(2)}) collective-permute-start(bf16[640,128]{1,0:T(8,128)(2,1)} %get-tuple-element.133), channel_id=1, source_target_pairs={{0,96},{4,100},{8,104},{12,108},{16,112},{20,116},{24,120},{28,124... | collective-permute-start | bytes 491528 | tf_op jit(solution)/shard_map/ppermute | solution.py:56
  111.1 4.7 %shard_map.124 = bf16[640,128]{1,0:T(8,128)(2,1)} custom-call(s32[1]{0:T(128)} %bitcast.1.x_ref, bf16[16,2,160,128]{3,2,1,0:T(8,128)(2,1)} %all-to-all-done.2.r_ref, bf16[16,160,128]{2,1,0:T(8,128)(2,1)} %copy-done.2), custom_call_target="tpu_custom_call" | custom-call | tf_op jit(solution)/shard_map/pallas_call | solution.py:89
  117.8 6.9 %collective-permute-done.4.refs_0_ = bf16[640,128]{1,0:T(8,128)(2,1)S(1)} collective-permute-done((bf16[640,128]{1,0:T(8,128)(2,1)}, bf16[640,128]{1,0:T(8,128)(2,1)S(1)}, u32[]{:S(2)}, u32[]{:S(2)}) %collective-permute-start.4) | collective-permute-done | bytes 163872 | tf_op jit(solution)/shard_map/ppermute | solution.py:56
  124.7 6.1 %collective-permute-done.5.refs_1_ = bf16[640,128]{1,0:T(8,128)(2,1)S(1)} collective-permute-done((bf16[640,128]{1,0:T(8,128)(2,1)S(1)}, bf16[640,128]{1,0:T(8,128)(2,1)S(1)}, u32[]{:S(2)}, u32[]{:S(2)}) %collective-permute-start.5) | collective-permute-done | bytes 163872 | tf_op jit(solution)/shard_map/ppermute | solution.py:56
  130.8 4.0 %collective-permute-done.7.refs_3_ = bf16[640,128]{1,0:T(8,128)(2,1)} collective-permute-done((bf16[640,128]{1,0:T(8,128)(2,1)S(1)}, bf16[640,128]{1,0:T(8,128)(2,1)}, u32[]{:S(2)}, u32[]{:S(2)}) %collective-permute-start.7) | collective-permute-done | bytes 163872 | tf_op jit(solution)/shard_map/ppermute | solution.py:56
  134.9 2.0 %shard_map.128 = (bf16[160,640]{1,0:T(8,128)(2,1)}, bf16[160,640]{1,0:T(8,128)(2,1)}, bf16[160,640]{1,0:T(8,128)(2,1)}, bf16[160,640]{1,0:T(8,128)(2,1)}) custom-call(s32[2]{0:T(128)S(1)} %pad_add_fusion.place_ref, bf16[640,128]{1,0:T(8,128)(2,1)S(1)} %collective-permute-done.4.refs_0_, bf16[640,128]{1,0:T(8,128)(2,1)S(1)} %collective-permute-done.5.refs_1_, ...), custom_call_target="tpu_custom_call" | custom-call | tf_op jit(solution)/shard_map/pallas_call | solution.py:89
  139.5 25.5 %while.13 = (s32[]{:T(128)}, f32[4,2560]{1,0:T(4,128)}, f32[4,128]{1,0:T(4,128)S(1)}, s32[]{:T(128)}, s32[]{:T(128)}, /*index=5*/bf16[640,128]{1,0:T(8,128)(2,1)...) while((s32[]{:T(128)}, f32[4,2560]{1,0:T(4,128)}, ...), condition=%wide.region_1.2_spmd.clone, body=%wide.region_0.1_spmd.clone.sunk | while | flops 2 | bytes 1835749 | solution.py:343
  140.0 2.3 %body.2 = f32[64,8,128]{2,1,0:T(8,128)} custom-call(s32[2]{0:T(128)S(1)} %get-tuple-element.408.place_ref, f32[1,128]{1,0:T(1,128)} %broadcast_in_dim.122.time_ref, bf16[640,128]{1,0:T(8,128)(2,1)S(1)} %get-tuple-element.357.refs_0_, bf16[640,128]{1,0:T(8,128)(2,1)S(1)} %get-tuple-element.358.refs_1_, bf16[640,128]{1,0:T(8,128)(2,1)S(1)} %get-tuple-element.359.refs_2_, ...), custom_call_target="tpu_custom_call" | custom-call | tf_op jit(solution)/shard_map/while/body/pallas_call | solution.py:327
  142.3 9.7 %all-to-all-start = ((f32[64,8,128]{2,1,0:T(8,128)}), f32[64,8,128]{2,1,0:T(8,128)S(1)}, u32[]{:S(2)}, u32[]{:S(2)}) async-start(f32[64,8,128]{2,1,0:T(8,128)} %body.2), calls=%async_computation | async-start | bytes 524288 | tf_op jit(solution)/shard_map/while/body/all_to_all | solution.py:336
  152.1 10.6 %all-to-all-done.chan_ref = f32[64,8,128]{2,1,0:T(8,128)S(1)} async-done(((f32[64,8,128]{2,1,0:T(8,128)}), f32[64,8,128]{2,1,0:T(8,128)S(1)}, u32[]{:S(2)}, u32[]{:S(2)}) %all-to-all-start) | async-done | bytes 262176 | tf_op jit(solution)/shard_map/while/body/all_to_all | solution.py:336
  163.4 1.7 body.3
  165.1 2.3 %shard_map.129 = bf16[160,2560]{1,0:T(8,128)(2,1)} custom-call(s32[1]{0:T(128)} %bitcast.z_ref, bf16[160,640]{1,0:T(8,128)(2,1)} %get-tuple-element.151.a0, bf16[160,640]{1,0:T(8,128)(2,1)} %collective-permute-done.15.a1, bf16[160,640]{1,0:T(8,128)(2,1)} %collective-permute-done.16.a2, bf16[160,640]{1,0:T(8,128)(2,1)} %collective-permute-done.17.a3, ...), custom_call_target="tpu_custom_call" | custom-call | tf_op jit(solution)/shard_map/pallas_call | solution.py:89
  (74 shorter events, 12.6 us)
Async XLA Ops:
  0.6 61.3 %copy-start = (f32[1,256,2560]{2,1,0:T(8,128)S(1)}, f32[1,256,2560]{2,1,0:T(8,128)}, u32[]{:S(2)}) copy-start(f32[1,256,2560]{2,1,0:T(8,128)} %param.15) | copy-start | bytes 7864324
  0.6 14.6 %copy-start.8 = (f32[64]{0:T(128)S(1)}, f32[64]{0:T(128)}, u32[]{:S(2)}) copy-start(f32[64]{0:T(128)} %constant.106) | copy-start | bytes 772
  0.7 14.6 %copy-start.9 = (pred[64]{0:T(512)(128)(4,1)S(1)}, pred[64]{0:T(512)(128)(4,1)}, u32[]{:S(2)}) copy-start(pred[64]{0:T(512)(128)(4,1)} %constant.105) | copy-start | bytes 196
  3.0 36.9 %all-to-all-start.1 = ((bf16[16,160,128]{2,1,0:T(8,128)(2,1)}), bf16[16,160,128]{2,1,0:T(8,128)(2,1)S(1)}, u32[]{:S(2)}, u32[]{:S(2)}) async-start(bf16[16,160,128]{2,1,0:T(8,128)(2,1)} %shard_map.123), calls=%async_computation.1 | async-start | bytes 1310720 | tf_op jit(solution)/shard_map/all_to_all | solution.py:283
  11.4 10.8 %collective-permute-start = (f32[2,2560]{1,0:T(2,128)S(1)}, f32[2,2560]{1,0:T(2,128)S(1)}, u32[]{:S(2)}, u32[]{:S(2)}) collective-permute-start(f32[2,2560]{1,0:T(2,128)S(1)} %bitcast.31), channel_id=1, source_target_pairs={{64,0},{128,64},{192,128},{0,192},{65,1},{129,65},{193,129},{1,193... | collective-permute-start | bytes 61448 | tf_op jit(solution)/shard_map/ppermute | solution.py:271
  22.8 30.9 %copy-start.11 = (f32[128]{0:T(128)S(1)}, f32[128]{0:T(128)}, u32[]{:S(2)}) copy-start(f32[128]{0:T(128)} %constant.96.clone) | copy-start | bytes 1540
  27.1 26.6 %copy-start.3 = (bf16[3,160,128]{2,1,0:T(8,128)(2,1)S(1)}, bf16[3,160,128]{2,1,0:T(8,128)(2,1)}, u32[]{:S(2)}) copy-start(bf16[3,160,128]{2,1,0:T(8,128)(2,1)} %get-tuple-element.135.q0) | copy-start | bytes 368644
  27.2 7.0 %collective-permute-start.1 = (bf16[3,160,128]{2,1,0:T(8,128)(2,1)}, bf16[3,160,128]{2,1,0:T(8,128)(2,1)S(1)}, u32[]{:S(2)}, u32[]{:S(2)}) collective-permute-start(bf16[3,160,128]{2,1,0:T(8,128)(2,1)} %get-tuple-element.127), channel_id=1, source_target_pairs={{0,4},{4,8},{8,12},{12,0},{16,20},{20,24},{24,28},{28,16},{32,36},... | collective-permute-start | bytes 368648 | tf_op jit(solution)/shard_map/ppermute | solution.py:30
  27.2 9.6 %collective-permute-start.2 = (bf16[3,160,128]{2,1,0:T(8,128)(2,1)}, bf16[3,160,128]{2,1,0:T(8,128)(2,1)S(1)}, u32[]{:S(2)}, u32[]{:S(2)}) collective-permute-start(bf16[3,160,128]{2,1,0:T(8,128)(2,1)} %get-tuple-element.128), channel_id=1, source_target_pairs={{0,8},{4,12},{8,0},{12,4},{16,24},{20,28},{24,16},{28,20},{32,40},... | collective-permute-start | bytes 368648 | tf_op jit(solution)/shard_map/ppermute | solution.py:30
  31.5 8.4 %collective-permute-start.3 = (bf16[3,160,128]{2,1,0:T(8,128)(2,1)}, bf16[3,160,128]{2,1,0:T(8,128)(2,1)}, u32[]{:S(2)}, u32[]{:S(2)}) collective-permute-start(bf16[3,160,128]{2,1,0:T(8,128)(2,1)} %get-tuple-element.129), channel_id=1, source_target_pairs={{0,12},{4,0},{8,4},{12,8},{16,28},{20,16},{24,20},{28,24},{32,44},... | collective-permute-start | bytes 368648 | tf_op jit(solution)/shard_map/ppermute | solution.py:30
  34.1 29.8 %copy-start.4 = (bf16[3,160,128]{2,1,0:T(8,128)(2,1)}, bf16[3,160,128]{2,1,0:T(8,128)(2,1)S(1)}, u32[]{:S(2)}) copy-start(bf16[3,160,128]{2,1,0:T(8,128)(2,1)S(1)} %collective-permute-done.1.q1) | copy-start | bytes 368644
  39.9 24.0 %copy-start.2 = (bf16[16,160,128]{2,1,0:T(8,128)(2,1)}, bf16[16,160,128]{2,1,0:T(8,128)(2,1)S(1)}, u32[]{:S(2)}) copy-start(bf16[16,160,128]{2,1,0:T(8,128)(2,1)S(1)} %all-to-all-done.1.v_ref) | copy-start | bytes 1966084
  39.9 49.3 %all-to-all-start.2 = ((bf16[16,2,160,128]{3,2,1,0:T(8,128)(2,1)}), bf16[16,2,160,128]{3,2,1,0:T(8,128)(2,1)}, u32[]{:S(2)}, u32[]{:S(2)}) async-start(bf16[16,2,160,128]{3,2,1,0:T(8,128)(2,1)} %get-tuple-element.130), calls=%async_computation.2 | async-start | bytes 2621440 | tf_op jit(solution)/shard_map/all_to_all | solution.py:297
  46.6 17.3 %copy-start.16 = (f32[256]{0:T(256)S(1)}, f32[256]{0:T(256)}, u32[]{:S(2)}) copy-start(f32[256]{0:T(256)} %constant.97.clone) | copy-start | bytes 3076
  48.8 67.1 %collective-permute-start.12 = (bf16[160,640]{1,0:T(8,128)(2,1)}, bf16[160,640]{1,0:T(8,128)(2,1)}, u32[]{:S(2)}, u32[]{:S(2)}) collective-permute-start(bf16[160,640]{1,0:T(8,128)(2,1)} %get-tuple-element.139), channel_id=1, source_target_pairs={{0,4},{4,8},{8,12},{12,0},{16,20},{20,24},{24,28},{28,16},{32,36},... | collective-permute-start | bytes 614408 | tf_op jit(solution)/shard_map/ppermute | solution.py:30
  50.7 65.4 %collective-permute-start.13 = (bf16[160,640]{1,0:T(8,128)(2,1)}, bf16[160,640]{1,0:T(8,128)(2,1)}, u32[]{:S(2)}, u32[]{:S(2)}) collective-permute-start(bf16[160,640]{1,0:T(8,128)(2,1)} %get-tuple-element.140), channel_id=1, source_target_pairs={{0,8},{4,12},{8,0},{12,4},{16,24},{20,28},{24,16},{28,20},{32,40},... | collective-permute-start | bytes 614408 | tf_op jit(solution)/shard_map/ppermute | solution.py:30
  56.3 42.4 %collective-permute-start.8 = (bf16[2,640,128]{2,1,0:T(8,128)(2,1)}, bf16[2,640,128]{2,1,0:T(8,128)(2,1)}, u32[]{:S(2)}, u32[]{:S(2)}) collective-permute-start(bf16[2,640,128]{2,1,0:T(8,128)(2,1)} %pad_maximum_fusion.s0), channel_id=1, source_target_pairs={{0,16},{4,20},{8,24},{12,28},{16,32},{20,36},{24,40},{28,44},{32,4... | collective-permute-start | bytes 983048 | tf_op jit(solution)/shard_map/ppermute | solution.py:35
  57.8 40.9 %collective-permute-start.9 = (bf16[2,640,128]{2,1,0:T(8,128)(2,1)}, bf16[2,640,128]{2,1,0:T(8,128)(2,1)}, u32[]{:S(2)}, u32[]{:S(2)}) collective-permute-start(bf16[2,640,128]{2,1,0:T(8,128)(2,1)} %pad_maximum_fusion.s0), channel_id=1, source_target_pairs={{0,32},{4,36},{8,40},{12,44},{16,48},{20,52},{24,56},{28,60},{32,0... | collective-permute-start | bytes 983048 | tf_op jit(solution)/shard_map/ppermute | solution.py:35
  60.5 38.3 %collective-permute-start.10 = (bf16[2,640,128]{2,1,0:T(8,128)(2,1)}, bf16[2,640,128]{2,1,0:T(8,128)(2,1)}, u32[]{:S(2)}, u32[]{:S(2)}) collective-permute-start(bf16[2,640,128]{2,1,0:T(8,128)(2,1)} %pad_maximum_fusion.s0), channel_id=1, source_target_pairs={{0,48},{4,52},{8,56},{12,60},{16,0},{20,4},{24,8},{28,12},{32,16},... | collective-permute-start | bytes 983048 | tf_op jit(solution)/shard_map/ppermute | solution.py:35
  63.9 41.5 %copy-start.12 = (bf16[160,640]{1,0:T(8,128)(2,1)S(1)}, bf16[160,640]{1,0:T(8,128)(2,1)}, u32[]{:S(2)}) copy-start(bf16[160,640]{1,0:T(8,128)(2,1)} %get-tuple-element.142) | copy-start | bytes 614404
  98.7 17.4 %copy-start.14 = (bf16[640,128]{1,0:T(8,128)(2,1)S(1)}, bf16[640,128]{1,0:T(8,128)(2,1)}, u32[]{:S(2)}) copy-start(bf16[640,128]{1,0:T(8,128)(2,1)} %get-tuple-element.132) | copy-start | bytes 491524
  98.7 18.3 %copy-start.13 = (bf16[640,128]{1,0:T(8,128)(2,1)S(1)}, bf16[640,128]{1,0:T(8,128)(2,1)}, u32[]{:S(2)}) copy-start(bf16[640,128]{1,0:T(8,128)(2,1)} %get-tuple-element.134) | copy-start | bytes 491524
  103.5 13.5 %collective-permute-start.11 = (bf16[640,128]{1,0:T(8,128)(2,1)}, bf16[640,128]{1,0:T(8,128)(2,1)S(1)}, u32[]{:S(2)}, u32[]{:S(2)}) collective-permute-start(bf16[640,128]{1,0:T(8,128)(2,1)} %shard_map.126), channel_id=1, source_target_pairs={{0,64},{4,68},{8,72},{12,76},{16,80},{20,84},{24,88},{28,92},{32,9... | collective-permute-start | bytes 491528 | tf_op jit(solution)/shard_map/ppermute | solution.py:56
  105.4 12.4 %collective-permute-start.14 = (bf16[160,640]{1,0:T(8,128)(2,1)S(1)}, bf16[160,640]{1,0:T(8,128)(2,1)}, u32[]{:S(2)}, u32[]{:S(2)}) collective-permute-start(bf16[160,640]{1,0:T(8,128)(2,1)S(1)} %copy-done.12), channel_id=1, source_target_pairs={{0,12},{4,0},{8,4},{12,8},{16,28},{20,16},{24,20},{28,24},{32,44},... | collective-permute-start | bytes 614408 | tf_op jit(solution)/shard_map/ppermute | solution.py:30
  105.4 25.4 %collective-permute-start.6 = (bf16[640,128]{1,0:T(8,128)(2,1)}, bf16[640,128]{1,0:T(8,128)(2,1)S(1)}, u32[]{:S(2)}, u32[]{:S(2)}) collective-permute-start(bf16[640,128]{1,0:T(8,128)(2,1)} %get-tuple-element.133), channel_id=1, source_target_pairs={{0,96},{4,100},{8,104},{12,108},{16,112},{20,116},{24,120},{28,124... | collective-permute-start | bytes 491528 | tf_op jit(solution)/shard_map/ppermute | solution.py:56
  115.9 8.9 %collective-permute-start.4 = (bf16[640,128]{1,0:T(8,128)(2,1)}, bf16[640,128]{1,0:T(8,128)(2,1)S(1)}, u32[]{:S(2)}, u32[]{:S(2)}) collective-permute-start(bf16[640,128]{1,0:T(8,128)(2,1)} %shard_map.124), channel_id=1, source_target_pairs={{0,64},{4,68},{8,72},{12,76},{16,80},{20,84},{24,88},{28,92},{32,9... | collective-permute-start | bytes 491528 | tf_op jit(solution)/shard_map/ppermute | solution.py:56
  116.1 14.7 %collective-permute-start.5 = (bf16[640,128]{1,0:T(8,128)(2,1)S(1)}, bf16[640,128]{1,0:T(8,128)(2,1)S(1)}, u32[]{:S(2)}, u32[]{:S(2)}) collective-permute-start(bf16[640,128]{1,0:T(8,128)(2,1)S(1)} %copy-done.14), channel_id=1, source_target_pairs={{0,112},{4,116},{8,120},{12,124},{16,64},{20,68},{24,72},{28,76},{... | collective-permute-start | bytes 491528 | tf_op jit(solution)/shard_map/ppermute | solution.py:56
  117.0 17.9 %collective-permute-start.7 = (bf16[640,128]{1,0:T(8,128)(2,1)S(1)}, bf16[640,128]{1,0:T(8,128)(2,1)}, u32[]{:S(2)}, u32[]{:S(2)}) collective-permute-start(bf16[640,128]{1,0:T(8,128)(2,1)S(1)} %copy-done.13), channel_id=1, source_target_pairs={{0,80},{4,84},{8,88},{12,92},{16,96},{20,100},{24,104},{28,108},{3... | collective-permute-start | bytes 491528 | tf_op jit(solution)/shard_map/ppermute | solution.py:56
  136.9 28.2 %collective-permute-start.15 = (bf16[160,640]{1,0:T(8,128)(2,1)}, bf16[160,640]{1,0:T(8,128)(2,1)}, u32[]{:S(2)}, u32[]{:S(2)}) collective-permute-start(bf16[160,640]{1,0:T(8,128)(2,1)} %get-tuple-element.145), channel_id=1, source_target_pairs={{0,12},{4,0},{8,4},{12,8},{16,28},{20,16},{24,20},{28,24},{32,44},... | collective-permute-start | bytes 614408 | tf_op jit(solution)/shard_map/ppermute | solution.py:30
  138.0 27.0 %collective-permute-start.16 = (bf16[160,640]{1,0:T(8,128)(2,1)}, bf16[160,640]{1,0:T(8,128)(2,1)}, u32[]{:S(2)}, u32[]{:S(2)}) collective-permute-start(bf16[160,640]{1,0:T(8,128)(2,1)} %get-tuple-element.146), channel_id=1, source_target_pairs={{0,8},{4,12},{8,0},{12,4},{16,24},{20,28},{24,16},{28,20},{32,40},... | collective-permute-start | bytes 614408 | tf_op jit(solution)/shard_map/ppermute | solution.py:30
  138.7 26.4 %collective-permute-start.17 = (bf16[160,640]{1,0:T(8,128)(2,1)}, bf16[160,640]{1,0:T(8,128)(2,1)}, u32[]{:S(2)}, u32[]{:S(2)}) collective-permute-start(bf16[160,640]{1,0:T(8,128)(2,1)} %get-tuple-element.147), channel_id=1, source_target_pairs={{0,4},{4,8},{8,12},{12,0},{16,20},{20,24},{24,28},{28,16},{32,36},... | collective-permute-start | bytes 614408 | tf_op jit(solution)/shard_map/ppermute | solution.py:30
  142.3 20.4 %all-to-all-start = ((f32[64,8,128]{2,1,0:T(8,128)}), f32[64,8,128]{2,1,0:T(8,128)S(1)}, u32[]{:S(2)}, u32[]{:S(2)}) async-start(f32[64,8,128]{2,1,0:T(8,128)} %body.2), calls=%async_computation | async-start | bytes 524288 | tf_op jit(solution)/shard_map/while/body/all_to_all | solution.py:336
  (6 other events, 41.8 us)

commit v3 on v2

--- a/solution.py
+++ b/solution.py
@@ -270,8 +270,7 @@
     when = jnp.full((1, HEAD_DIM), step.astype(jnp.float32))
     gains = lax.ppermute(qk_gain[0], "segment", [((i + 1) % SIDE, i) for i in range(SIDE)])
     parts = qkv[0, 0].transpose(1, 0, 2)
-    cots = call(cut_cotangent_kernel, [flat] * SIDE, 0, 1_600_000, z, cotangent[0, 0])
-    cots_z = [cots[0], along_z(cots[1], 1), along_z(cots[2], 2), None]
+    cosine, sine = rope_tables(positions[0])
     values = call(
         cut_values_kernel,
         shape((count, TOK, HEAD_DIM)),
@@ -280,8 +279,7 @@
         parts,
         specs=[one_of(2, (TOK, WIDTH))],
     )
-    values = lax.all_to_all(values, "ctx", 0, 0)
-    cosine, sine = rope_tables(positions[0])
+    values = lax.all_to_all(after(values, (gains, cosine, sine)), "ctx", 0, 0)
     main, *shared = call(
         prep_kernel,
         [shape((count, 2, TOK, HEAD_DIM))] + [block] * SIDE,
@@ -293,8 +291,10 @@
         cosine,
         sine,
     )
+    cots = call(cut_cotangent_kernel, [flat] * SIDE, 0, 1_600_000, z, after(cotangent[0, 0], shared))
+    cots_z = exchanged(along_z, cots)
     shared_z = exchanged(along_z, shared)
-    main = lax.all_to_all(after(main, (values, shared_z)), "ctx", 0, 0)
+    main = lax.all_to_all(after(main, (values, shared_z, cots_z[3])), "ctx", 0, 0)
     pair = jnp.concatenate([b[1:] for b in shared_z], axis=1)
     pairs = [pair] + [along_x(pair, k) for k in steps]
     gate = jnp.dot(embed(step), mod_weight[0], precision=lax.Precision.HIGHEST)[None]
@@ -304,21 +304,23 @@
     freq = jnp.broadcast_to(freq[:, None], (rows, HEAD_DIM))
     main, gate, freq = lax.optimization_barrier((main, gate, freq))
     back = [None] * SIDE
-    back[2], back[1], back[3] = call(
-        functools.partial(main_kernel, (2, 1, 3)), [single] * 3, 2_500_000_000, 2_500_000, x, main, values
-    )
-    (back[0],) = call(
-        functools.partial(main_kernel, (0,)), [single], 840_000_000, 2_000_000, x, main, values
+    back[2], back[1], back[3], back[0] = call(
+        functools.partial(main_kernel, (2, 1, 3, 0)),
+        [single] * SIDE,
+        3_400_000_000,
+        2_500_000,
+        x,
+        main,
+        values,
     )
     shared_out = call(
-        shared_kernel, single, 840_000_000, 1_600_000, *after(shared_z, back[2]), *pairs, smem=0
-    )
-    cots_z[3] = along_z(after(cots[3], back[2]), 3)
+        shared_kernel, single, 840_000_000, 1_600_000, *after(shared_z, (back[2], cots_z[1], cots_z[2])), *pairs, smem=0
+    )
     for m in (2, 1, 3, 0):
         back[m] = onward(back[m], m)
     shared_out = onward(shared_out, 0)
     joined = call(
-        join_kernel, [flat] * SIDE, 0, 1_600_000, place, *back, after(shared_out, cots_z[1:])
+        join_kernel, [flat] * SIDE, 0, 1_600_000, place, *back, shared_out
     )
     at_home = [joined[0]] + [along_z(joined[k], SIDE - k) for k in steps]
 

time: 168 us -> 168 us (level)
  Pallas kernels: 35.8 us -> 33.2 us
  starting transfers between devices: 54.4 us -> 56.6 us
  other arithmetic: 2.15 us -> 4.19 us
  waiting for transfers between devices: 66.5 us -> 64.7 us
    ppermute x9, waiting for transfers between devices: 7.73 us -> 14.7 us  [along_z(): return lax.ppermute(value, 'ctx', pairs)]
    ppermute x1, waiting for transfers between devices: 5.76 us -> 0.01 us  [local(): lax.ppermute(qk_gain[0], 'segment', [((i + 1) % SIDE, i) for i in range(S...]
    ppermute x5, waiting for transfers between devices: 17.1 us -> 12.2 us  [onward(): return lax.ppermute(value, ('segment', 'ctx'), pairs)]
    ppermute x9, starting transfers between devices: 10.6 us -> 14.6 us  [along_z(): return lax.ppermute(value, 'ctx', pairs)]
    ppermute x1, starting transfers between devices: 3.73 us -> 6.71 us  [local(): lax.ppermute(qk_gain[0], 'segment', [((i + 1) % SIDE, i) for i in range(S...]
    all_to_all x2, starting transfers between devices: 15.2 us -> 12.4 us  [the longest x1 6.67 us: local(): lax.all_to_all(after(main, (values, shared_z, cots_z[3])), 'ctx', 0, 0)]
    pallas_call x9 -> x8, Pallas kernels: 33.5 us -> 30.9 us  [call(): pl.pallas_call(kernel, grid=grid, out_shape=out_shape, in_specs=specs, ou...]
    all_to_all x2, waiting for transfers between devices: 25.3 us -> 27.1 us  [the longest x1 27.1 us: local(): lax.all_to_all(after(main, (values, shared_z, cots_z[3])), 'ctx', 0, 0)]
  transfers between devices with their start and end apart: 21 -> 21, of which waited for: 9 -> 8; matrix products, arithmetic and copies ran while one was open for 4% -> 6% of each run, Pallas kernels for 18% -> 17%
where the time goes in v3:
time: 168 us; the launch traced here: 167 us
  waiting for transfers between devices  64.7 us (39%)
  starting transfers between devices  56.6 us (34%)
  Pallas kernels  33.2 us (20%)
  local copies, waits for them, and re-layouts  5.11 us (3%)
  other arithmetic  4.19 us (2%)
  matrix products  1.94 us (1%)
    pallas_call x8, Pallas kernels, call(): pl.pallas_call(kernel, grid=grid, out_shape=out_shape, in_specs=specs, ou...  30.9 us
    all_to_all x1, waiting for transfers between devices, local(): lax.all_to_all(after(main, (values, shared_z, cots_z[3])), 'ctx', 0, 0)  27.1 us
    ppermute x9, waiting for transfers between devices, along_z(): return lax.ppermute(value, 'ctx', pairs)  14.7 us
    ppermute x9, starting transfers between devices, along_z(): return lax.ppermute(value, 'ctx', pairs)  14.6 us
    ppermute x5, waiting for transfers between devices, onward(): return lax.ppermute(value, ('segment', 'ctx'), pairs)  12.2 us
    all_to_all x1, waiting for transfers between devices, gradient(): chans = lax.all_to_all(chans, ('ctx', 'dp'), 0, 0)  10.6 us
    all_to_all x1, starting transfers between devices, gradient(): chans = lax.all_to_all(chans, ('ctx', 'dp'), 0, 0)  9.01 us
    ppermute x5, starting transfers between devices, onward(): return lax.ppermute(value, ('segment', 'ctx'), pairs)  7.83 us
  transfers between devices with their start and end apart: 21, of which 8 were waited for; matrix products, arithmetic and copies ran while one was open for 6% of the time, Pallas kernels for 17%

profile of v3, /device:TPU:8, one launch (start us, length us, event | category | flops | bytes accessed | tf_op | source)
XLA Modules:
  0.0 167.2 jit_solution(10919324741229060361)
XLA Ops:
  0.6 6.7 %collective-permute-start = (f32[2,2560]{1,0:T(2,128)}, f32[2,2560]{1,0:T(2,128)S(1)}, u32[]{:S(2)}, u32[]{:S(2)}) collective-permute-start(f32[2,2560]{1,0:T(2,128)} %bitcast.31), channel_id=1, source_target_pairs={{64,0},{128,64},{192,128},{0,192},{65,1},{129,65},{193,129},{1,193... | collective-permute-start | bytes 61448 | tf_op jit(solution)/shard_map/ppermute | solution.py:271
  10.7 2.1 %shard_map.123 = bf16[16,160,128]{2,1,0:T(8,128)(2,1)} custom-call(bf16[3,160,2560]{2,1,0:T(8,128)(2,1)} %bitcast.22), custom_call_target="tpu_custom_call" | custom-call | tf_op jit(solution)/shard_map/pallas_call | solution.py:89
  12.8 5.8 %all-to-all-start.1 = ((bf16[16,160,128]{2,1,0:T(8,128)(2,1)}), bf16[16,160,128]{2,1,0:T(8,128)(2,1)S(1)}, u32[]{:S(2)}, u32[]{:S(2)}) async-start(bf16[16,160,128]{2,1,0:T(8,128)(2,1)} %shard_map.123), calls=%async_computation.1 | async-start | bytes 1310720 | tf_op jit(solution)/shard_map/all_to_all | solution.py:282
  18.6 4.3 %shard_map.122 = (bf16[16,2,160,128]{3,2,1,0:T(8,128)(2,1)}, bf16[3,160,128]{2,1,0:T(8,128)(2,1)}, bf16[3,160,128]{2,1,0:T(8,128)(2,1)}, bf16[3,160,128]{2,1,0:T(8,128)(2,1)}, bf16[3,160,128]{2,1,0:T(8,128)(2,1)}) custom-call(s32[1]{0:T(128)} %bitcast.z_ref, bf16[3,160,2560]{2,1,0:T(8,128)(2,1)} %bitcast.23, f32[2,2560]{1,0:T(2,128)} %copy-done.7, ...), custom_call_target="tpu_custom_call" | custom-call | tf_op jit(solution)/shard_map/pallas_call | solution.py:89
  22.9 2.2 %shard_map.124 = (bf16[160,640]{1,0:T(8,128)(2,1)}, bf16[160,640]{1,0:T(8,128)(2,1)}, bf16[160,640]{1,0:T(8,128)(2,1)}, bf16[160,640]{1,0:T(8,128)(2,1)}) custom-call(s32[1]{0:T(128)} %bitcast.z_ref, bf16[160,2560]{1,0:T(8,128)(2,1)} %bitcast.25), custom_call_target="tpu_custom_call" | custom-call | tf_op jit(solution)/shard_map/pallas_call | solution.py:89
  25.1 3.7 %collective-permute-start.4 = (bf16[160,640]{1,0:T(8,128)(2,1)}, bf16[160,640]{1,0:T(8,128)(2,1)}, u32[]{:S(2)}, u32[]{:S(2)}) collective-permute-start(bf16[160,640]{1,0:T(8,128)(2,1)} %get-tuple-element.133), channel_id=1, source_target_pairs={{0,12},{4,0},{8,4},{12,8},{16,28},{20,16},{24,20},{28,24},{32,44},... | collective-permute-start | bytes 614408 | tf_op jit(solution)/shard_map/ppermute | solution.py:30
  29.9 2.7 %collective-permute-start.3 = (bf16[3,160,128]{2,1,0:T(8,128)(2,1)}, bf16[3,160,128]{2,1,0:T(8,128)(2,1)S(1)}, u32[]{:S(2)}, u32[]{:S(2)}) collective-permute-start(bf16[3,160,128]{2,1,0:T(8,128)(2,1)} %get-tuple-element.131), channel_id=1, source_target_pairs={{0,12},{4,0},{8,4},{12,8},{16,28},{20,16},{24,20},{28,24},{32,44},... | collective-permute-start | bytes 368648 | tf_op jit(solution)/shard_map/ppermute | solution.py:30
  32.6 8.3 %collective-permute-done.1.q1 = bf16[3,160,128]{2,1,0:T(8,128)(2,1)S(1)} collective-permute-done((bf16[3,160,128]{2,1,0:T(8,128)(2,1)}, bf16[3,160,128]{2,1,0:T(8,128)(2,1)S(1)}, u32[]{:S(2)}, u32[]{:S(2)}) %collective-permute-start.1) | collective-permute-done | bytes 122912 | tf_op jit(solution)/shard_map/ppermute | solution.py:30
  40.9 6.4 %collective-permute-done.2.q2 = bf16[3,160,128]{2,1,0:T(8,128)(2,1)S(1)} collective-permute-done((bf16[3,160,128]{2,1,0:T(8,128)(2,1)}, bf16[3,160,128]{2,1,0:T(8,128)(2,1)S(1)}, u32[]{:S(2)}, u32[]{:S(2)}) %collective-permute-start.2) | collective-permute-done | bytes 122912 | tf_op jit(solution)/shard_map/ppermute | solution.py:30
  48.6 6.7 %all-to-all-start.2 = ((bf16[16,2,160,128]{3,2,1,0:T(8,128)(2,1)}), bf16[16,2,160,128]{3,2,1,0:T(8,128)(2,1)}, u32[]{:S(2)}, u32[]{:S(2)}) async-start(bf16[16,2,160,128]{3,2,1,0:T(8,128)(2,1)} %get-tuple-element.134), calls=%async_computation.2 | async-start | bytes 2621440 | tf_op jit(solution)/shard_map/all_to_all | solution.py:297
  58.6 1.9 %collective-permute-start.11 = (bf16[2,640,128]{2,1,0:T(8,128)(2,1)}, bf16[2,640,128]{2,1,0:T(8,128)(2,1)}, u32[]{:S(2)}, u32[]{:S(2)}) collective-permute-start(bf16[2,640,128]{2,1,0:T(8,128)(2,1)} %pad_maximum_fusion.s0), channel_id=1, source_target_pairs={{0,16},{4,20},{8,24},{12,28},{16,32},{20,36},{24,40},{28,44},{32,4... | collective-permute-start | bytes 983048 | tf_op jit(solution)/shard_map/ppermute | solution.py:35
  60.5 2.7 %collective-permute-start.12 = (bf16[2,640,128]{2,1,0:T(8,128)(2,1)}, bf16[2,640,128]{2,1,0:T(8,128)(2,1)}, u32[]{:S(2)}, u32[]{:S(2)}) collective-permute-start(bf16[2,640,128]{2,1,0:T(8,128)(2,1)} %pad_maximum_fusion.s0), channel_id=1, source_target_pairs={{0,32},{4,36},{8,40},{12,44},{16,48},{20,52},{24,56},{28,60},{32,0... | collective-permute-start | bytes 983048 | tf_op jit(solution)/shard_map/ppermute | solution.py:35
  63.1 1.5 collective-permute-start.13
  64.7 1.5 collective-permute-start.9
  66.2 2.4 %collective-permute-start.10 = (bf16[160,640]{1,0:T(8,128)(2,1)}, bf16[160,640]{1,0:T(8,128)(2,1)}, u32[]{:S(2)}, u32[]{:S(2)}) collective-permute-start(bf16[160,640]{1,0:T(8,128)(2,1)} %get-tuple-element.141), channel_id=1, source_target_pairs={{0,8},{4,12},{8,0},{12,4},{16,24},{20,28},{24,16},{28,20},{32,40},... | collective-permute-start | bytes 614408 | tf_op jit(solution)/shard_map/ppermute | solution.py:30
  68.5 1.9 %fusion.2.gate_ref = f32[1,2560]{1,0:T(1,128)} fusion(f32[256,1]{0,1:T(1,128)S(1)} %bitcast.27, f32[1,256,2560]{2,1,0:T(8,128)S(1)} %copy-done), kind=kOutput, calls=%fused_computation.1 | convolution fusion | flops 7864320 | bytes 2632704 | tf_op jit(solution)/shard_map/dot_general | solution.py:300
  70.5 27.1 %all-to-all-done.2.r_ref = bf16[16,2,160,128]{3,2,1,0:T(8,128)(2,1)} async-done(((bf16[16,2,160,128]{3,2,1,0:T(8,128)(2,1)}), bf16[16,2,160,128]{3,2,1,0:T(8,128)(2,1)}, u32[]{:S(2)}, u32[]{:S(2)}) %all-to-all-start.2) | async-done | bytes 1310752 | tf_op jit(solution)/shard_map/all_to_all | solution.py:297
  97.7 11.7 %shard_map.125 = (bf16[640,128]{1,0:T(8,128)(2,1)}, bf16[640,128]{1,0:T(8,128)(2,1)}, bf16[640,128]{1,0:T(8,128)(2,1)}, bf16[640,128]{1,0:T(8,128)(2,1)}) custom-call(s32[1]{0:T(128)} %bitcast.1.x_ref, bf16[16,2,160,128]{3,2,1,0:T(8,128)(2,1)} %all-to-all-done.2.r_ref, bf16[16,160,128]{2,1,0:T(8,128)(2,1)} %copy-done.2), custom_call_target="tpu_custom_call" | custom-call | tf_op jit(solution)/shard_map/pallas_call | solution.py:89
  109.4 6.3 %collective-permute-start.7 = (bf16[640,128]{1,0:T(8,128)(2,1)}, bf16[640,128]{1,0:T(8,128)(2,1)S(1)}, u32[]{:S(2)}, u32[]{:S(2)}) collective-permute-start(bf16[640,128]{1,0:T(8,128)(2,1)} %get-tuple-element.138), channel_id=1, source_target_pairs={{0,96},{4,100},{8,104},{12,108},{16,112},{20,116},{24,120},{28,124... | collective-permute-start | bytes 491528 | tf_op jit(solution)/shard_map/ppermute | solution.py:56
  117.1 4.7 %shard_map.126 = bf16[640,128]{1,0:T(8,128)(2,1)} custom-call(bf16[3,160,128]{2,1,0:T(8,128)(2,1)} %get-tuple-element.142.q0, bf16[3,160,128]{2,1,0:T(8,128)(2,1)} %copy-done.4, bf16[3,160,128]{2,1,0:T(8,128)(2,1)} %copy-done.5, bf16[3,160,128]{2,1,0:T(8,128)(2,1)} %copy-done.6, bf16[2,640,128]{2,1,0:T(8,128)(2,1)} %pad_maximum_fusion.s0, ...), custom_call_target="tpu_custom_call" | custom-call | tf_op jit(solution)/shard_map/pallas_call | solution.py:89
  122.4 3.1 %collective-permute-done.6.refs_1_ = bf16[640,128]{1,0:T(8,128)(2,1)S(1)} collective-permute-done((bf16[640,128]{1,0:T(8,128)(2,1)}, bf16[640,128]{1,0:T(8,128)(2,1)S(1)}, u32[]{:S(2)}, u32[]{:S(2)}) %collective-permute-start.6) | collective-permute-done | bytes 163872 | tf_op jit(solution)/shard_map/ppermute | solution.py:56
  125.5 6.4 %collective-permute-done.8.refs_3_ = bf16[640,128]{1,0:T(8,128)(2,1)S(1)} collective-permute-done((bf16[640,128]{1,0:T(8,128)(2,1)}, bf16[640,128]{1,0:T(8,128)(2,1)S(1)}, u32[]{:S(2)}, u32[]{:S(2)}) %collective-permute-start.8) | collective-permute-done | bytes 163872 | tf_op jit(solution)/shard_map/ppermute | solution.py:56
  131.9 2.3 %collective-permute-done.14.refs_4_ = bf16[640,128]{1,0:T(8,128)(2,1)} collective-permute-done((bf16[640,128]{1,0:T(8,128)(2,1)}, bf16[640,128]{1,0:T(8,128)(2,1)}, u32[]{:S(2)}, u32[]{:S(2)}) %collective-permute-start.14) | collective-permute-done | bytes 163872 | tf_op jit(solution)/shard_map/ppermute | solution.py:56
  134.2 2.0 %shard_map.127 = (bf16[160,640]{1,0:T(8,128)(2,1)}, bf16[160,640]{1,0:T(8,128)(2,1)}, bf16[160,640]{1,0:T(8,128)(2,1)}, bf16[160,640]{1,0:T(8,128)(2,1)}) custom-call(s32[2]{0:T(128)S(1)} %pad_add_fusion.place_ref, bf16[640,128]{1,0:T(8,128)(2,1)S(1)} %collective-permute-done.5.refs_0_, bf16[640,128]{1,0:T(8,128)(2,1)S(1)} %collective-permute-done.6.refs_1_, ...), custom_call_target="tpu_custom_call" | custom-call | tf_op jit(solution)/shard_map/pallas_call | solution.py:89
  136.2 1.2 collective-permute-start.16
  137.4 2.0 %collective-permute-start.17 = (bf16[160,640]{1,0:T(8,128)(2,1)}, bf16[160,640]{1,0:T(8,128)(2,1)}, u32[]{:S(2)}, u32[]{:S(2)}) collective-permute-start(bf16[160,640]{1,0:T(8,128)(2,1)} %get-tuple-element.149), channel_id=1, source_target_pairs={{0,4},{4,8},{8,12},{12,0},{16,20},{20,24},{24,28},{28,16},{32,36},... | collective-permute-start | bytes 614408 | tf_op jit(solution)/shard_map/ppermute | solution.py:30
  140.1 24.8 %while.13 = (s32[]{:T(128)}, f32[4,2560]{1,0:T(4,128)}, f32[4,128]{1,0:T(4,128)S(1)}, s32[]{:T(128)}, s32[]{:T(128)}, /*index=5*/bf16[640,128]{1,0:T(8,128)(2,1)...) while((s32[]{:T(128)}, f32[4,2560]{1,0:T(4,128)}, ...), condition=%wide.region_1.2_spmd.clone, body=%wide.region_0.1_spmd.clone.sunk | while | flops 2 | bytes 1835749 | solution.py:345
  140.6 2.3 %body.2 = f32[64,8,128]{2,1,0:T(8,128)} custom-call(s32[2]{0:T(128)S(1)} %get-tuple-element.410.place_ref, f32[1,128]{1,0:T(1,128)} %broadcast_in_dim.122.time_ref, bf16[640,128]{1,0:T(8,128)(2,1)S(1)} %get-tuple-element.359.refs_0_, bf16[640,128]{1,0:T(8,128)(2,1)S(1)} %get-tuple-element.360.refs_1_, bf16[640,128]{1,0:T(8,128)(2,1)S(1)} %get-tuple-element.361.refs_2_, ...), custom_call_target="tpu_custom_call" | custom-call | tf_op jit(solution)/shard_map/while/body/pallas_call | solution.py:329
  142.8 9.0 %all-to-all-start = ((f32[64,8,128]{2,1,0:T(8,128)}), f32[64,8,128]{2,1,0:T(8,128)S(1)}, u32[]{:S(2)}, u32[]{:S(2)}) async-start(f32[64,8,128]{2,1,0:T(8,128)} %body.2), calls=%async_computation | async-start | bytes 524288 | tf_op jit(solution)/shard_map/while/body/all_to_all | solution.py:338
  151.9 10.6 %all-to-all-done.chan_ref = f32[64,8,128]{2,1,0:T(8,128)S(1)} async-done(((f32[64,8,128]{2,1,0:T(8,128)}), f32[64,8,128]{2,1,0:T(8,128)S(1)}, u32[]{:S(2)}, u32[]{:S(2)}) %all-to-all-start) | async-done | bytes 262176 | tf_op jit(solution)/shard_map/while/body/all_to_all | solution.py:338
  163.2 1.7 body.3
  164.9 2.3 %shard_map.128 = bf16[160,2560]{1,0:T(8,128)(2,1)} custom-call(s32[1]{0:T(128)} %bitcast.z_ref, bf16[160,640]{1,0:T(8,128)(2,1)} %get-tuple-element.153.a0, bf16[160,640]{1,0:T(8,128)(2,1)} %collective-permute-done.15.a1, bf16[160,640]{1,0:T(8,128)(2,1)} %collective-permute-done.16.a2, bf16[160,640]{1,0:T(8,128)(2,1)} %collective-permute-done.17.a3, ...), custom_call_target="tpu_custom_call" | custom-call | tf_op jit(solution)/shard_map/pallas_call | solution.py:89
  (59 shorter events, 12.4 us)
Async XLA Ops:
  0.6 67.9 %copy-start = (f32[1,256,2560]{2,1,0:T(8,128)S(1)}, f32[1,256,2560]{2,1,0:T(8,128)}, u32[]{:S(2)}) copy-start(f32[1,256,2560]{2,1,0:T(8,128)} %param.15) | copy-start | bytes 7864324
  0.6 12.1 %collective-permute-start = (f32[2,2560]{1,0:T(2,128)}, f32[2,2560]{1,0:T(2,128)S(1)}, u32[]{:S(2)}, u32[]{:S(2)}) collective-permute-start(f32[2,2560]{1,0:T(2,128)} %bitcast.31), channel_id=1, source_target_pairs={{64,0},{128,64},{192,128},{0,192},{65,1},{129,65},{193,129},{1,193... | collective-permute-start | bytes 61448 | tf_op jit(solution)/shard_map/ppermute | solution.py:271
  12.8 5.8 %copy-start.7 = (f32[2,2560]{1,0:T(2,128)}, f32[2,2560]{1,0:T(2,128)S(1)}, u32[]{:S(2)}) copy-start(f32[2,2560]{1,0:T(2,128)S(1)} %collective-permute-done.gain_ref) | copy-start | bytes 61444
  12.8 35.9 %all-to-all-start.1 = ((bf16[16,160,128]{2,1,0:T(8,128)(2,1)}), bf16[16,160,128]{2,1,0:T(8,128)(2,1)S(1)}, u32[]{:S(2)}, u32[]{:S(2)}) async-start(bf16[16,160,128]{2,1,0:T(8,128)(2,1)} %shard_map.123), calls=%async_computation.1 | async-start | bytes 1310720 | tf_op jit(solution)/shard_map/all_to_all | solution.py:282
  18.6 37.4 %copy-start.8 = (f32[128]{0:T(128)S(1)}, f32[128]{0:T(128)}, u32[]{:S(2)}) copy-start(f32[128]{0:T(128)} %constant.96.clone) | copy-start | bytes 1540
  22.9 33.1 %copy-start.3 = (bf16[3,160,128]{2,1,0:T(8,128)(2,1)S(1)}, bf16[3,160,128]{2,1,0:T(8,128)(2,1)}, u32[]{:S(2)}) copy-start(bf16[3,160,128]{2,1,0:T(8,128)(2,1)} %get-tuple-element.142.q0) | copy-start | bytes 368644
  22.9 41.7 %copy-start.9 = (f32[256]{0:T(256)S(1)}, f32[256]{0:T(256)}, u32[]{:S(2)}) copy-start(f32[256]{0:T(256)} %constant.97.clone) | copy-start | bytes 3076
  25.1 23.5 %collective-permute-start.4 = (bf16[160,640]{1,0:T(8,128)(2,1)}, bf16[160,640]{1,0:T(8,128)(2,1)}, u32[]{:S(2)}, u32[]{:S(2)}) collective-permute-start(bf16[160,640]{1,0:T(8,128)(2,1)} %get-tuple-element.133), channel_id=1, source_target_pairs={{0,12},{4,0},{8,4},{12,8},{16,28},{20,16},{24,20},{28,24},{32,44},... | collective-permute-start | bytes 614408 | tf_op jit(solution)/shard_map/ppermute | solution.py:30
  28.8 12.1 %collective-permute-start.1 = (bf16[3,160,128]{2,1,0:T(8,128)(2,1)}, bf16[3,160,128]{2,1,0:T(8,128)(2,1)S(1)}, u32[]{:S(2)}, u32[]{:S(2)}) collective-permute-start(bf16[3,160,128]{2,1,0:T(8,128)(2,1)} %get-tuple-element.129), channel_id=1, source_target_pairs={{0,4},{4,8},{8,12},{12,0},{16,20},{20,24},{24,28},{28,16},{32,36},... | collective-permute-start | bytes 368648 | tf_op jit(solution)/shard_map/ppermute | solution.py:30
  28.8 18.5 %collective-permute-start.2 = (bf16[3,160,128]{2,1,0:T(8,128)(2,1)}, bf16[3,160,128]{2,1,0:T(8,128)(2,1)S(1)}, u32[]{:S(2)}, u32[]{:S(2)}) collective-permute-start(bf16[3,160,128]{2,1,0:T(8,128)(2,1)} %get-tuple-element.130), channel_id=1, source_target_pairs={{0,8},{4,12},{8,0},{12,4},{16,24},{20,28},{24,16},{28,20},{32,40},... | collective-permute-start | bytes 368648 | tf_op jit(solution)/shard_map/ppermute | solution.py:30
  29.9 17.4 %collective-permute-start.3 = (bf16[3,160,128]{2,1,0:T(8,128)(2,1)}, bf16[3,160,128]{2,1,0:T(8,128)(2,1)S(1)}, u32[]{:S(2)}, u32[]{:S(2)}) collective-permute-start(bf16[3,160,128]{2,1,0:T(8,128)(2,1)} %get-tuple-element.131), channel_id=1, source_target_pairs={{0,12},{4,0},{8,4},{12,8},{16,28},{20,16},{24,20},{28,24},{32,44},... | collective-permute-start | bytes 368648 | tf_op jit(solution)/shard_map/ppermute | solution.py:30
  40.9 29.6 %copy-start.4 = (bf16[3,160,128]{2,1,0:T(8,128)(2,1)}, bf16[3,160,128]{2,1,0:T(8,128)(2,1)S(1)}, u32[]{:S(2)}) copy-start(bf16[3,160,128]{2,1,0:T(8,128)(2,1)S(1)} %collective-permute-done.1.q1) | copy-start | bytes 368644
  47.3 0.7 copy-start.5
  48.0 0.6 copy-start.6
  48.6 21.9 %copy-start.2 = (bf16[16,160,128]{2,1,0:T(8,128)(2,1)}, bf16[16,160,128]{2,1,0:T(8,128)(2,1)S(1)}, u32[]{:S(2)}) copy-start(bf16[16,160,128]{2,1,0:T(8,128)(2,1)S(1)} %all-to-all-done.1.v_ref) | copy-start | bytes 1966084
  48.6 49.0 %all-to-all-start.2 = ((bf16[16,2,160,128]{3,2,1,0:T(8,128)(2,1)}), bf16[16,2,160,128]{3,2,1,0:T(8,128)(2,1)}, u32[]{:S(2)}, u32[]{:S(2)}) async-start(bf16[16,2,160,128]{3,2,1,0:T(8,128)(2,1)} %get-tuple-element.134), calls=%async_computation.2 | async-start | bytes 2621440 | tf_op jit(solution)/shard_map/all_to_all | solution.py:297
  58.6 57.1 %collective-permute-start.11 = (bf16[2,640,128]{2,1,0:T(8,128)(2,1)}, bf16[2,640,128]{2,1,0:T(8,128)(2,1)}, u32[]{:S(2)}, u32[]{:S(2)}) collective-permute-start(bf16[2,640,128]{2,1,0:T(8,128)(2,1)} %pad_maximum_fusion.s0), channel_id=1, source_target_pairs={{0,16},{4,20},{8,24},{12,28},{16,32},{20,36},{24,40},{28,44},{32,4... | collective-permute-start | bytes 983048 | tf_op jit(solution)/shard_map/ppermute | solution.py:35
  60.5 56.1 %collective-permute-start.12 = (bf16[2,640,128]{2,1,0:T(8,128)(2,1)}, bf16[2,640,128]{2,1,0:T(8,128)(2,1)}, u32[]{:S(2)}, u32[]{:S(2)}) collective-permute-start(bf16[2,640,128]{2,1,0:T(8,128)(2,1)} %pad_maximum_fusion.s0), channel_id=1, source_target_pairs={{0,32},{4,36},{8,40},{12,44},{16,48},{20,52},{24,56},{28,60},{32,0... | collective-permute-start | bytes 983048 | tf_op jit(solution)/shard_map/ppermute | solution.py:35
  63.1 54.0 %collective-permute-start.13 = (bf16[2,640,128]{2,1,0:T(8,128)(2,1)}, bf16[2,640,128]{2,1,0:T(8,128)(2,1)}, u32[]{:S(2)}, u32[]{:S(2)}) collective-permute-start(bf16[2,640,128]{2,1,0:T(8,128)(2,1)} %pad_maximum_fusion.s0), channel_id=1, source_target_pairs={{0,48},{4,52},{8,56},{12,60},{16,0},{20,4},{24,8},{28,12},{32,16},... | collective-permute-start | bytes 983048 | tf_op jit(solution)/shard_map/ppermute | solution.py:35
  64.7 44.7 %collective-permute-start.9 = (bf16[160,640]{1,0:T(8,128)(2,1)}, bf16[160,640]{1,0:T(8,128)(2,1)}, u32[]{:S(2)}, u32[]{:S(2)}) collective-permute-start(bf16[160,640]{1,0:T(8,128)(2,1)} %get-tuple-element.140), channel_id=1, source_target_pairs={{0,4},{4,8},{8,12},{12,0},{16,20},{20,24},{24,28},{28,16},{32,36},... | collective-permute-start | bytes 614408 | tf_op jit(solution)/shard_map/ppermute | solution.py:30
  66.2 43.2 %collective-permute-start.10 = (bf16[160,640]{1,0:T(8,128)(2,1)}, bf16[160,640]{1,0:T(8,128)(2,1)}, u32[]{:S(2)}, u32[]{:S(2)}) collective-permute-start(bf16[160,640]{1,0:T(8,128)(2,1)} %get-tuple-element.141), channel_id=1, source_target_pairs={{0,8},{4,12},{8,0},{12,4},{16,24},{20,28},{24,16},{28,20},{32,40},... | collective-permute-start | bytes 614408 | tf_op jit(solution)/shard_map/ppermute | solution.py:30
  109.4 13.0 %collective-permute-start.5 = (bf16[640,128]{1,0:T(8,128)(2,1)}, bf16[640,128]{1,0:T(8,128)(2,1)S(1)}, u32[]{:S(2)}, u32[]{:S(2)}) collective-permute-start(bf16[640,128]{1,0:T(8,128)(2,1)} %get-tuple-element.136), channel_id=1, source_target_pairs={{0,64},{4,68},{8,72},{12,76},{16,80},{20,84},{24,88},{28,92},{32,9... | collective-permute-start | bytes 491528 | tf_op jit(solution)/shard_map/ppermute | solution.py:56
  109.4 16.1 %collective-permute-start.7 = (bf16[640,128]{1,0:T(8,128)(2,1)}, bf16[640,128]{1,0:T(8,128)(2,1)S(1)}, u32[]{:S(2)}, u32[]{:S(2)}) collective-permute-start(bf16[640,128]{1,0:T(8,128)(2,1)} %get-tuple-element.138), channel_id=1, source_target_pairs={{0,96},{4,100},{8,104},{12,108},{16,112},{20,116},{24,120},{28,124... | collective-permute-start | bytes 491528 | tf_op jit(solution)/shard_map/ppermute | solution.py:56
  115.7 9.9 %collective-permute-start.6 = (bf16[640,128]{1,0:T(8,128)(2,1)}, bf16[640,128]{1,0:T(8,128)(2,1)S(1)}, u32[]{:S(2)}, u32[]{:S(2)}) collective-permute-start(bf16[640,128]{1,0:T(8,128)(2,1)} %get-tuple-element.137), channel_id=1, source_target_pairs={{0,112},{4,116},{8,120},{12,124},{16,64},{20,68},{24,72},{28,76},{... | collective-permute-start | bytes 491528 | tf_op jit(solution)/shard_map/ppermute | solution.py:56
  116.6 15.4 %collective-permute-start.8 = (bf16[640,128]{1,0:T(8,128)(2,1)}, bf16[640,128]{1,0:T(8,128)(2,1)S(1)}, u32[]{:S(2)}, u32[]{:S(2)}) collective-permute-start(bf16[640,128]{1,0:T(8,128)(2,1)} %get-tuple-element.139), channel_id=1, source_target_pairs={{0,80},{4,84},{8,88},{12,92},{16,96},{20,100},{24,104},{28,108},{3... | collective-permute-start | bytes 491528 | tf_op jit(solution)/shard_map/ppermute | solution.py:56
  121.8 12.4 %collective-permute-start.14 = (bf16[640,128]{1,0:T(8,128)(2,1)}, bf16[640,128]{1,0:T(8,128)(2,1)}, u32[]{:S(2)}, u32[]{:S(2)}) collective-permute-start(bf16[640,128]{1,0:T(8,128)(2,1)} %shard_map.126), channel_id=1, source_target_pairs={{0,64},{4,68},{8,72},{12,76},{16,80},{20,84},{24,88},{28,92},{32,9... | collective-permute-start | bytes 491528 | tf_op jit(solution)/shard_map/ppermute | solution.py:56
  136.2 28.6 %collective-permute-start.15 = (bf16[160,640]{1,0:T(8,128)(2,1)}, bf16[160,640]{1,0:T(8,128)(2,1)}, u32[]{:S(2)}, u32[]{:S(2)}) collective-permute-start(bf16[160,640]{1,0:T(8,128)(2,1)} %get-tuple-element.147), channel_id=1, source_target_pairs={{0,12},{4,0},{8,4},{12,8},{16,28},{20,16},{24,20},{28,24},{32,44},... | collective-permute-start | bytes 614408 | tf_op jit(solution)/shard_map/ppermute | solution.py:30
  136.2 28.6 %collective-permute-start.16 = (bf16[160,640]{1,0:T(8,128)(2,1)}, bf16[160,640]{1,0:T(8,128)(2,1)}, u32[]{:S(2)}, u32[]{:S(2)}) collective-permute-start(bf16[160,640]{1,0:T(8,128)(2,1)} %get-tuple-element.148), channel_id=1, source_target_pairs={{0,8},{4,12},{8,0},{12,4},{16,24},{20,28},{24,16},{28,20},{32,40},... | collective-permute-start | bytes 614408 | tf_op jit(solution)/shard_map/ppermute | solution.py:30
  137.4 27.5 %collective-permute-start.17 = (bf16[160,640]{1,0:T(8,128)(2,1)}, bf16[160,640]{1,0:T(8,128)(2,1)}, u32[]{:S(2)}, u32[]{:S(2)}) collective-permute-start(bf16[160,640]{1,0:T(8,128)(2,1)} %get-tuple-element.149), channel_id=1, source_target_pairs={{0,4},{4,8},{8,12},{12,0},{16,20},{20,24},{24,28},{28,16},{32,36},... | collective-permute-start | bytes 614408 | tf_op jit(solution)/shard_map/ppermute | solution.py:30
  142.8 19.7 %all-to-all-start = ((f32[64,8,128]{2,1,0:T(8,128)}), f32[64,8,128]{2,1,0:T(8,128)S(1)}, u32[]{:S(2)}, u32[]{:S(2)}) async-start(f32[64,8,128]{2,1,0:T(8,128)} %body.2), calls=%async_computation | async-start | bytes 524288 | tf_op jit(solution)/shard_map/while/body/all_to_all | solution.py:338
  162.5 0.7 copy-start.1

commit v4 on v1

--- a/solution.py
+++ b/solution.py
@@ -166,6 +166,12 @@
     return (accum / total).astype(jnp.bfloat16)
 
 
+def pack_kernel(s0, s1, s2, s3, out_ref):
+    for j, s in enumerate((s0, s1, s2, s3)):
+        for part in range(2):
+            out_ref[part, j * TOK : (j + 1) * TOK] = s[part + 1]
+
+
 def shared_kernel(q0, q1, q2, q3, s0, s1, s2, s3, out_ref):
     blocks = (s0, s1, s2, s3)
     for pair in ((q0, q1), (q2, q3)):
@@ -275,8 +281,6 @@
     parts = qkv[0, 0].transpose(1, 0, 2)
     cots = call(cut_cotangent_kernel, [flat] * SIDE, 0, 1_600_000, z, cotangent[0, 0])
     cots_z = [None] * SIDE
-    for k in (2, 1):
-        cots_z[k] = away(cots[k], k)
     cosine, sine = rope_tables(positions[0])
     main, *shared = call(
         prep_kernel,
@@ -290,17 +294,12 @@
         sine,
     )
     shared_z = exchanged(along_z, shared)
-    main = lax.all_to_all(after(main, shared_z), "ctx", 0, 0)
-    pair = jnp.concatenate([b[1:] for b in shared_z], axis=1)
-    pairs = [pair] + [along_x(pair, k) for k in steps]
+    main = lax.all_to_all(main, "ctx", 0, 0)
     gate = jnp.dot(embed(step), mod_weight[0], precision=lax.Precision.HIGHEST)[None]
     rows = FREQS // (SIDE * SIDE * SIDE)
     index = (ctx * SIDE + lax.axis_index("dp").astype(jnp.int32)) * rows
     freq = lax.dynamic_slice_in_dim(np.tile(frequencies(), 2), index, rows)
     freq = jnp.broadcast_to(freq[:, None], (rows, HEAD_DIM))
-    shared_out = call(
-        shared_kernel, single, 840_000_000, 1_600_000, *shared_z, *pairs, smem=0
-    )
     main, gate, freq = lax.optimization_barrier((main, gate, freq))
     back = [None] * SIDE
     back[2], back[1], back[3] = call(
@@ -308,6 +307,20 @@
     )
     (back[0],) = call(
         functools.partial(main_kernel, (0,)), [single], 840_000_000, 2_000_000, x, main
+    )
+    for k in (2, 1):
+        cots_z[k] = away(after(cots[k], shared_z), k)
+    pair = call(
+        pack_kernel,
+        shape((2, ROWS, HEAD_DIM)),
+        0,
+        1_300_000,
+        *shared_z,
+        smem=0,
+    )
+    pairs = [pair] + [along_x(pair, k) for k in steps]
+    shared_out = call(
+        shared_kernel, single, 840_000_000, 1_600_000, *shared_z, *pairs, smem=0
     )
     for k in (3, 0):
         cots_z[k] = away(after(cots[k], back[2]), k)

time: 162 us -> 164 us (1.012)
  starting transfers between devices: 48.8 us -> 51.2 us
  Pallas kernels: 32.5 us -> 34.4 us
    all_to_all x1, waiting for transfers between devices: 41.1 us -> 0.01 us  [local(): main = lax.all_to_all(main, 'ctx', 0, 0)]
    ppermute x3, waiting for transfers between devices: 7.4 us -> 46.3 us  [along_z(): return lax.ppermute(value, 'ctx', pairs)]
    pallas_call x8 -> x9, Pallas kernels: 30.3 us -> 32.1 us  [call(): pl.pallas_call(kernel, grid=grid, out_shape=out_shape, in_specs=specs, ou...]
    ppermute x4, starting transfers between devices: 5.54 us -> 7.28 us  [away(): return lax.ppermute(value, ('segment', 'ctx'), section_pairs(SIDE - 1, by))]
  transfers between devices with their start and end apart: 21 -> 21, of which waited for: 5 -> 4; matrix products, arithmetic and copies ran while one was open for 4% -> 4% of each run, Pallas kernels for 16% -> 17%
where the time goes in v4:
time: 164 us
  waiting for transfers between devices  67.7 us (41%)
  starting transfers between devices  51.2 us (31%)
  Pallas kernels  34.4 us (21%)
  local copies, waits for them, and re-layouts  3.55 us (2%)
  other arithmetic  3.43 us (2%)
  matrix products  1.94 us (1%)
    ppermute x3, waiting for transfers between devices, along_z(): return lax.ppermute(value, 'ctx', pairs)  46.3 us
    pallas_call x9, Pallas kernels, call(): pl.pallas_call(kernel, grid=grid, out_shape=out_shape, in_specs=specs, ou...  32.1 us
    all_to_all x1, waiting for transfers between devices, gradient(): chans = lax.all_to_all(chans, ('ctx', 'dp'), 0, 0)  13.9 us
    all_to_all x1, starting transfers between devices, gradient(): chans = lax.all_to_all(chans, ('ctx', 'dp'), 0, 0)  11.3 us
    ppermute x6, starting transfers between devices, along_x(): return lax.ppermute(value, 'ctx', pairs)  8.48 us
    ppermute x1, waiting for transfers between devices, local(): lax.ppermute(grad, 'segment', [(i, (i + 1) % SIDE) for i in range(SIDE)])  7.43 us
    ppermute x4, starting transfers between devices, away(): return lax.ppermute(value, ('segment', 'ctx'), section_pairs(SIDE - 1, by))  7.28 us
    ppermute x1, starting transfers between devices, local(): lax.ppermute(gains, 'segment', [((i + 1) % SIDE, i) for i in range(SIDE)])  6.7 us
  transfers between devices with their start and end apart: 21, of which 4 were waited for; matrix products, arithmetic and copies ran while one was open for 4% of the time, Pallas kernels for 17%

profile of v4, /device:TPU:8, one launch (start us, length us, event | category | flops | bytes accessed | tf_op | source)
XLA Modules:
  0.0 163.8 jit_solution(8332633904156620572)
XLA Ops:
  2.2 6.7 %collective-permute-start = (f32[3,2560]{1,0:T(4,128)S(1)}, f32[3,2560]{1,0:T(4,128)}, u32[]{:S(2)}, u32[]{:S(2)}) collective-permute-start(f32[3,2560]{1,0:T(4,128)S(1)} %concatenate.16), channel_id=1, source_target_pairs={{64,0},{128,64},{192,128},{0,192},{65,1},{129,65},{193,129},{1,193... | collective-permute-start | bytes 92168 | tf_op jit(solution)/shard_map/ppermute | solution.py:280
  10.3 1.1 fusion.4
  12.2 4.5 %shard_map.122 = (bf16[16,3,160,128]{3,2,1,0:T(8,128)(2,1)}, bf16[3,160,128]{2,1,0:T(8,128)(2,1)}, bf16[3,160,128]{2,1,0:T(8,128)(2,1)}, bf16[3,160,128]{2,1,0:T(8,128)(2,1)}, bf16[3,160,128]{2,1,0:T(8,128)(2,1)}) custom-call(s32[1]{0:T(128)} %bitcast.1.z_ref, bf16[3,160,2560]{2,1,0:T(8,128)(2,1)} %bitcast.22, f32[3,2560]{1,0:T(4,128)} %collective-permute-done.gain_ref, ...), custom_call_target="tpu_custom_call" | custom-call | tf_op jit(solution)/shard_map/pallas_call | solution.py:97
  16.8 6.0 %all-to-all-start.1 = ((bf16[16,3,160,128]{3,2,1,0:T(8,128)(2,1)}), bf16[16,3,160,128]{3,2,1,0:T(8,128)(2,1)}, u32[]{:S(2)}, u32[]{:S(2)}) async-start(bf16[16,3,160,128]{3,2,1,0:T(8,128)(2,1)} %get-tuple-element.119), calls=%async_computation.1 | async-start | bytes 3932160 | tf_op jit(solution)/shard_map/all_to_all | solution.py:297
  22.7 2.0 %collective-permute-start.4 = (bf16[3,160,128]{2,1,0:T(8,128)(2,1)S(1)}, bf16[3,160,128]{2,1,0:T(8,128)(2,1)S(1)}, u32[]{:S(2)}, u32[]{:S(2)}) collective-permute-start(bf16[3,160,128]{2,1,0:T(8,128)(2,1)S(1)} %copy-done.9), channel_id=1, source_target_pairs={{0,4},{4,8},{8,12},{12,0},{16,20},{20,24},{24,28},{28,16},{32,36},... | collective-permute-start | bytes 368648 | tf_op jit(solution)/shard_map/ppermute | solution.py:30
  24.7 2.4 %collective-permute-start.5 = (bf16[3,160,128]{2,1,0:T(8,128)(2,1)S(1)}, bf16[3,160,128]{2,1,0:T(8,128)(2,1)S(1)}, u32[]{:S(2)}, u32[]{:S(2)}) collective-permute-start(bf16[3,160,128]{2,1,0:T(8,128)(2,1)S(1)} %copy-done.8), channel_id=1, source_target_pairs={{0,8},{4,12},{8,0},{12,4},{16,24},{20,28},{24,16},{28,20},{32,40},... | collective-permute-start | bytes 368648 | tf_op jit(solution)/shard_map/ppermute | solution.py:30
  27.1 1.5 collective-permute-start.6
  28.6 2.1 %shard_map.127 = (bf16[160,640]{1,0:T(8,128)(2,1)}, bf16[160,640]{1,0:T(8,128)(2,1)}, bf16[160,640]{1,0:T(8,128)(2,1)}, bf16[160,640]{1,0:T(8,128)(2,1)}) custom-call(s32[1]{0:T(128)} %bitcast.1.z_ref, bf16[160,2560]{1,0:T(8,128)(2,1)} %bitcast.24), custom_call_target="tpu_custom_call" | custom-call | tf_op jit(solution)/shard_map/pallas_call | solution.py:97
  30.8 31.6 %collective-permute-done.4.s1.q1 = bf16[3,160,128]{2,1,0:T(8,128)(2,1)S(1)} collective-permute-done((bf16[3,160,128]{2,1,0:T(8,128)(2,1)S(1)}, bf16[3,160,128]{2,1,0:T(8,128)(2,1)S(1)}, u32[]{:S(2)}, u32[]{:S(2)}) %collective-permute-start.4) | collective-permute-done | bytes 122912 | tf_op jit(solution)/shard_map/ppermute | solution.py:30
  62.4 14.7 %collective-permute-done.5.s2.q2 = bf16[3,160,128]{2,1,0:T(8,128)(2,1)S(1)} collective-permute-done((bf16[3,160,128]{2,1,0:T(8,128)(2,1)S(1)}, bf16[3,160,128]{2,1,0:T(8,128)(2,1)S(1)}, u32[]{:S(2)}, u32[]{:S(2)}) %collective-permute-start.5) | collective-permute-done | bytes 122912 | tf_op jit(solution)/shard_map/ppermute | solution.py:30
  77.8 1.8 %shard_map.125.s0 = bf16[2,640,128]{2,1,0:T(8,128)(2,1)} custom-call(bf16[3,160,128]{2,1,0:T(8,128)(2,1)} %get-tuple-element.124.s0.q0, bf16[3,160,128]{2,1,0:T(8,128)(2,1)} %copy-done.2, bf16[3,160,128]{2,1,0:T(8,128)(2,1)} %copy-done.3, bf16[3,160,128]{2,1,0:T(8,128)(2,1)} %copy-done.4), custom_call_target="tpu_custom_call" | custom-call | tf_op jit(solution)/shard_map/pallas_call | solution.py:97
  79.6 1.5 collective-permute-start.7
  81.1 2.7 %collective-permute-start.8 = (bf16[2,640,128]{2,1,0:T(8,128)(2,1)}, bf16[2,640,128]{2,1,0:T(8,128)(2,1)}, u32[]{:S(2)}, u32[]{:S(2)}) collective-permute-start(bf16[2,640,128]{2,1,0:T(8,128)(2,1)} %shard_map.125.s0), channel_id=1, source_target_pairs={{0,32},{4,36},{8,40},{12,44},{16,48},{20,52},{24,56},{28,60},{32,0... | collective-permute-start | bytes 983048 | tf_op jit(solution)/shard_map/ppermute | solution.py:35
  83.8 1.5 collective-permute-start.9
  85.2 1.9 %collective-permute-start.10 = (bf16[160,640]{1,0:T(8,128)(2,1)}, bf16[160,640]{1,0:T(8,128)(2,1)}, u32[]{:S(2)}, u32[]{:S(2)}) collective-permute-start(bf16[160,640]{1,0:T(8,128)(2,1)} %get-tuple-element.129), channel_id=1, source_target_pairs={{0,196},{4,200},{8,204},{12,192},{16,212},{20,216},{24,220},{28,20... | collective-permute-start | bytes 614408 | tf_op jit(solution)/shard_map/ppermute | solution.py:64
  87.2 2.2 %collective-permute-start.11 = (bf16[160,640]{1,0:T(8,128)(2,1)}, bf16[160,640]{1,0:T(8,128)(2,1)}, u32[]{:S(2)}, u32[]{:S(2)}) collective-permute-start(bf16[160,640]{1,0:T(8,128)(2,1)} %get-tuple-element.131), channel_id=1, source_target_pairs={{0,200},{4,204},{8,192},{12,196},{16,216},{20,220},{24,208},{28,21... | collective-permute-start | bytes 614408 | tf_op jit(solution)/shard_map/ppermute | solution.py:64
  89.4 1.9 %fusion.gate_ref = f32[1,2560]{1,0:T(1,128)} fusion(f32[256,1]{0,1:T(1,128)S(1)} %bitcast.27, f32[1,256,2560]{2,1,0:T(8,128)S(1)} %copy-done), kind=kOutput, calls=%fused_computation | convolution fusion | flops 7864320 | bytes 2632704 | tf_op jit(solution)/shard_map/dot_general | solution.py:298
  91.4 9.5 %shard_map.124 = (bf16[640,128]{1,0:T(8,128)(2,1)}, bf16[640,128]{1,0:T(8,128)(2,1)}, bf16[640,128]{1,0:T(8,128)(2,1)}) custom-call(s32[1]{0:T(128)} %bitcast.2.x_ref, bf16[16,3,160,128]{3,2,1,0:T(8,128)(2,1)} %all-to-all-done.1.r_ref), custom_call_target="tpu_custom_call" | custom-call | tf_op jit(solution)/shard_map/pallas_call | solution.py:97
  100.8 3.0 %collective-permute-start.16 = (bf16[160,640]{1,0:T(8,128)(2,1)}, bf16[160,640]{1,0:T(8,128)(2,1)}, u32[]{:S(2)}, u32[]{:S(2)}) collective-permute-start(bf16[160,640]{1,0:T(8,128)(2,1)} %get-tuple-element.139), channel_id=1, source_target_pairs={{0,192},{4,196},{8,200},{12,204},{16,208},{20,212},{24,216},{28,22... | collective-permute-start | bytes 614408 | tf_op jit(solution)/shard_map/ppermute | solution.py:64
  104.8 1.8 %collective-permute-start.1 = (bf16[640,128]{1,0:T(8,128)(2,1)}, bf16[640,128]{1,0:T(8,128)(2,1)S(1)}, u32[]{:S(2)}, u32[]{:S(2)}) collective-permute-start(bf16[640,128]{1,0:T(8,128)(2,1)} %get-tuple-element.121), channel_id=1, source_target_pairs={{0,48},{4,52},{8,56},{12,60},{16,0},{20,4},{24,8},{28,12},{32,16},... | collective-permute-start | bytes 491528 | tf_op jit(solution)/shard_map/ppermute | solution.py:35
  107.0 4.1 %shard_map.126.refs_4_ = bf16[640,128]{1,0:T(8,128)(2,1)S(1)} custom-call(bf16[3,160,128]{2,1,0:T(8,128)(2,1)} %get-tuple-element.124.s0.q0, bf16[3,160,128]{2,1,0:T(8,128)(2,1)} %copy-done.2, bf16[3,160,128]{2,1,0:T(8,128)(2,1)} %copy-done.3, bf16[3,160,128]{2,1,0:T(8,128)(2,1)} %copy-done.4, bf16[2,640,128]{2,1,0:T(8,128)(2,1)} %shard_map.125.s0, ...), custom_call_target="tpu_custom_call" | custom-call | tf_op jit(solution)/shard_map/pallas_call | solution.py:97
  111.1 4.1 %shard_map.123.refs_0_ = bf16[640,128]{1,0:T(8,128)(2,1)S(1)} custom-call(s32[1]{0:T(128)} %bitcast.2.x_ref, bf16[16,3,160,128]{3,2,1,0:T(8,128)(2,1)} %all-to-all-done.1.r_ref), custom_call_target="tpu_custom_call" | custom-call | tf_op jit(solution)/shard_map/pallas_call | solution.py:97
  115.2 2.0 %shard_map.128 = (bf16[160,640]{1,0:T(8,128)(2,1)}, bf16[160,640]{1,0:T(8,128)(2,1)}, bf16[160,640]{1,0:T(8,128)(2,1)}, bf16[160,640]{1,0:T(8,128)(2,1)}) custom-call(s32[2]{0:T(128)S(1)} %pad_add_fusion.place_ref, bf16[640,128]{1,0:T(8,128)(2,1)S(1)} %shard_map.123.refs_0_, bf16[640,128]{1,0:T(8,128)(2,1)S(1)} %collective-permute-done.1.refs_1_, ...), custom_call_target="tpu_custom_call" | custom-call | tf_op jit(solution)/shard_map/pallas_call | solution.py:97
  117.2 3.2 %collective-permute-start.12 = (bf16[160,640]{1,0:T(8,128)(2,1)}, bf16[160,640]{1,0:T(8,128)(2,1)}, u32[]{:S(2)}, u32[]{:S(2)}) collective-permute-start(bf16[160,640]{1,0:T(8,128)(2,1)} %get-tuple-element.133), channel_id=1, source_target_pairs={{0,64},{4,68},{8,72},{12,76},{16,80},{20,84},{24,88},{28,92},{32,9... | collective-permute-start | bytes 614408 | tf_op jit(solution)/shard_map/ppermute | solution.py:60
  121.7 1.1 collective-permute-start.15
  123.5 29.9 %while.12 = (s32[]{:T(128)}, f32[4,2560]{1,0:T(4,128)}, f32[4,128]{1,0:T(4,128)S(1)}, s32[]{:T(128)}, s32[]{:T(128)}, /*index=5*/bf16[640,128]{1,0:T(8,128)(2,1)...) while((s32[]{:T(128)}, f32[4,2560]{1,0:T(4,128)}, ...), condition=%wide.region_1.2_spmd, body=%wide.region_0.1_spmd.sunk | while | flops 2 | bytes 1835233 | solution.py:353
  123.5 2.3 %body.2 = f32[64,8,128]{2,1,0:T(8,128)} custom-call(s32[2]{0:T(128)S(1)} %get-tuple-element.353.place_ref, f32[3,2560]{1,0:T(4,128)} %get-tuple-element.354.time_ref, bf16[640,128]{1,0:T(8,128)(2,1)S(1)} %get-tuple-element.302.refs_0_, bf16[640,128]{1,0:T(8,128)(2,1)S(1)} %get-tuple-element.303.refs_1_, bf16[640,128]{1,0:T(8,128)(2,1)S(1)} %get-tuple-element.304.refs_2_, ...), custom_call_target="tpu_custom_call" | custom-call | tf_op jit(solution)/shard_map/while/body/pallas_call | solution.py:337
  125.8 11.3 %all-to-all-start = ((f32[64,8,128]{2,1,0:T(8,128)}), f32[64,8,128]{2,1,0:T(8,128)S(1)}, u32[]{:S(2)}, u32[]{:S(2)}) async-start(f32[64,8,128]{2,1,0:T(8,128)} %body.2), calls=%async_computation | async-start | bytes 524288 | tf_op jit(solution)/shard_map/while/body/all_to_all | solution.py:346
  137.1 13.9 %all-to-all-done.chan_ref = f32[64,8,128]{2,1,0:T(8,128)S(1)} async-done(((f32[64,8,128]{2,1,0:T(8,128)}), f32[64,8,128]{2,1,0:T(8,128)S(1)}, u32[]{:S(2)}, u32[]{:S(2)}) %all-to-all-start) | async-done | bytes 262176 | tf_op jit(solution)/shard_map/while/body/all_to_all | solution.py:346
  151.7 1.7 %body.3 = f32[4,2560]{1,0:T(4,128)} custom-call(s32[1]{0:T(128)} %bitcast.21.index_ref, f32[4,128]{1,0:T(4,128)S(1)} %get-tuple-element.359.freq_ref, f32[4,128]{1,0:T(4,128)S(1)} %get-tuple-element.345.before_ref, f32[64,8,128]{2,1,0:T(8,128)} %copy-done.1), custom_call_target="tpu_custom_call" | custom-call | tf_op jit(solution)/shard_map/while/body/pallas_call | solution.py:97
  153.5 7.4 %collective-permute-done.18 = f32[4,2560]{1,0:T(4,128)S(1)} collective-permute-done((f32[4,2560]{1,0:T(4,128)}, f32[4,2560]{1,0:T(4,128)S(1)}, u32[]{:S(2)}, u32[]{:S(2)}) %collective-permute-start.18) | collective-permute-done | bytes 40992 | tf_op jit(solution)/shard_map/ppermute | solution.py:354
  161.0 2.3 %shard_map.129 = bf16[160,2560]{1,0:T(8,128)(2,1)} custom-call(s32[1]{0:T(128)} %bitcast.1.z_ref, bf16[160,640]{1,0:T(8,128)(2,1)} %collective-permute-done.12.a0, bf16[160,640]{1,0:T(8,128)(2,1)} %collective-permute-done.13.a1, bf16[160,640]{1,0:T(8,128)(2,1)} %collective-permute-done.14.a2, bf16[160,640]{1,0:T(8,128)(2,1)} %collective-permute-done.15.a3, ...), custom_call_target="tpu_custom_call" | custom-call | tf_op jit(solution)/shard_map/pallas_call | solution.py:97
  (58 shorter events, 8.5 us)
Async XLA Ops:
  0.6 88.7 %copy-start = (f32[1,256,2560]{2,1,0:T(8,128)S(1)}, f32[1,256,2560]{2,1,0:T(8,128)}, u32[]{:S(2)}) copy-start(f32[1,256,2560]{2,1,0:T(8,128)} %param.15) | copy-start | bytes 7864324
  2.2 10.0 %collective-permute-start = (f32[3,2560]{1,0:T(4,128)S(1)}, f32[3,2560]{1,0:T(4,128)}, u32[]{:S(2)}, u32[]{:S(2)}) collective-permute-start(f32[3,2560]{1,0:T(4,128)S(1)} %concatenate.16), channel_id=1, source_target_pairs={{64,0},{128,64},{192,128},{0,192},{65,1},{129,65},{193,129},{1,193... | collective-permute-start | bytes 92168 | tf_op jit(solution)/shard_map/ppermute | solution.py:280
  16.7 6.0 %copy-start.9 = (bf16[3,160,128]{2,1,0:T(8,128)(2,1)S(1)}, bf16[3,160,128]{2,1,0:T(8,128)(2,1)}, u32[]{:S(2)}) copy-start(bf16[3,160,128]{2,1,0:T(8,128)(2,1)} %get-tuple-element.125) | copy-start | bytes 368644
  16.7 8.0 %copy-start.8 = (bf16[3,160,128]{2,1,0:T(8,128)(2,1)S(1)}, bf16[3,160,128]{2,1,0:T(8,128)(2,1)}, u32[]{:S(2)}) copy-start(bf16[3,160,128]{2,1,0:T(8,128)(2,1)} %get-tuple-element.126) | copy-start | bytes 368644
  16.7 10.3 %copy-start.7 = (bf16[3,160,128]{2,1,0:T(8,128)(2,1)S(1)}, bf16[3,160,128]{2,1,0:T(8,128)(2,1)}, u32[]{:S(2)}) copy-start(bf16[3,160,128]{2,1,0:T(8,128)(2,1)} %get-tuple-element.127) | copy-start | bytes 368644
  16.7 11.8 %copy-start.6 = (f32[128]{0:T(128)S(1)}, f32[128]{0:T(128)}, u32[]{:S(2)}) copy-start(f32[128]{0:T(128)} %constant.96.clone) | copy-start | bytes 1540
  16.7 14.0 %copy-start.10 = (f32[256]{0:T(256)S(1)}, f32[256]{0:T(256)}, u32[]{:S(2)}) copy-start(f32[256]{0:T(256)} %constant.97.clone) | copy-start | bytes 3076
  16.8 74.5 %all-to-all-start.1 = ((bf16[16,3,160,128]{3,2,1,0:T(8,128)(2,1)}), bf16[16,3,160,128]{3,2,1,0:T(8,128)(2,1)}, u32[]{:S(2)}, u32[]{:S(2)}) async-start(bf16[16,3,160,128]{3,2,1,0:T(8,128)(2,1)} %get-tuple-element.119), calls=%async_computation.1 | async-start | bytes 3932160 | tf_op jit(solution)/shard_map/all_to_all | solution.py:297
  22.7 39.7 %collective-permute-start.4 = (bf16[3,160,128]{2,1,0:T(8,128)(2,1)S(1)}, bf16[3,160,128]{2,1,0:T(8,128)(2,1)S(1)}, u32[]{:S(2)}, u32[]{:S(2)}) collective-permute-start(bf16[3,160,128]{2,1,0:T(8,128)(2,1)S(1)} %copy-done.9), channel_id=1, source_target_pairs={{0,4},{4,8},{8,12},{12,0},{16,20},{20,24},{24,28},{28,16},{32,36},... | collective-permute-start | bytes 368648 | tf_op jit(solution)/shard_map/ppermute | solution.py:30
  24.7 52.4 %collective-permute-start.5 = (bf16[3,160,128]{2,1,0:T(8,128)(2,1)S(1)}, bf16[3,160,128]{2,1,0:T(8,128)(2,1)S(1)}, u32[]{:S(2)}, u32[]{:S(2)}) collective-permute-start(bf16[3,160,128]{2,1,0:T(8,128)(2,1)S(1)} %copy-done.8), channel_id=1, source_target_pairs={{0,8},{4,12},{8,0},{12,4},{16,24},{20,28},{24,16},{28,20},{32,40},... | collective-permute-start | bytes 368648 | tf_op jit(solution)/shard_map/ppermute | solution.py:30
  27.1 50.1 %collective-permute-start.6 = (bf16[3,160,128]{2,1,0:T(8,128)(2,1)S(1)}, bf16[3,160,128]{2,1,0:T(8,128)(2,1)S(1)}, u32[]{:S(2)}, u32[]{:S(2)}) collective-permute-start(bf16[3,160,128]{2,1,0:T(8,128)(2,1)S(1)} %copy-done.7), channel_id=1, source_target_pairs={{0,12},{4,0},{8,4},{12,8},{16,28},{20,16},{24,20},{28,24},{32,44},... | collective-permute-start | bytes 368648 | tf_op jit(solution)/shard_map/ppermute | solution.py:30
  62.4 14.7 %copy-start.2 = (bf16[3,160,128]{2,1,0:T(8,128)(2,1)}, bf16[3,160,128]{2,1,0:T(8,128)(2,1)S(1)}, u32[]{:S(2)}) copy-start(bf16[3,160,128]{2,1,0:T(8,128)(2,1)S(1)} %collective-permute-done.4.s1.q1) | copy-start | bytes 368644
  77.1 0.6 copy-start.3
  77.1 0.7 copy-start.4
  79.6 25.1 %collective-permute-start.7 = (bf16[2,640,128]{2,1,0:T(8,128)(2,1)}, bf16[2,640,128]{2,1,0:T(8,128)(2,1)S(1)}, u32[]{:S(2)}, u32[]{:S(2)}) collective-permute-start(bf16[2,640,128]{2,1,0:T(8,128)(2,1)} %shard_map.125.s0), channel_id=1, source_target_pairs={{0,16},{4,20},{8,24},{12,28},{16,32},{20,36},{24,40},{28,44},{32,4... | collective-permute-start | bytes 983048 | tf_op jit(solution)/shard_map/ppermute | solution.py:35
  81.1 25.5 %collective-permute-start.8 = (bf16[2,640,128]{2,1,0:T(8,128)(2,1)}, bf16[2,640,128]{2,1,0:T(8,128)(2,1)}, u32[]{:S(2)}, u32[]{:S(2)}) collective-permute-start(bf16[2,640,128]{2,1,0:T(8,128)(2,1)} %shard_map.125.s0), channel_id=1, source_target_pairs={{0,32},{4,36},{8,40},{12,44},{16,48},{20,52},{24,56},{28,60},{32,0... | collective-permute-start | bytes 983048 | tf_op jit(solution)/shard_map/ppermute | solution.py:35
  83.8 23.0 %collective-permute-start.9 = (bf16[2,640,128]{2,1,0:T(8,128)(2,1)}, bf16[2,640,128]{2,1,0:T(8,128)(2,1)}, u32[]{:S(2)}, u32[]{:S(2)}) collective-permute-start(bf16[2,640,128]{2,1,0:T(8,128)(2,1)} %shard_map.125.s0), channel_id=1, source_target_pairs={{0,48},{4,52},{8,56},{12,60},{16,0},{20,4},{24,8},{28,12},{32,16},... | collective-permute-start | bytes 983048 | tf_op jit(solution)/shard_map/ppermute | solution.py:35
  85.2 15.6 %collective-permute-start.10 = (bf16[160,640]{1,0:T(8,128)(2,1)}, bf16[160,640]{1,0:T(8,128)(2,1)}, u32[]{:S(2)}, u32[]{:S(2)}) collective-permute-start(bf16[160,640]{1,0:T(8,128)(2,1)} %get-tuple-element.129), channel_id=1, source_target_pairs={{0,196},{4,200},{8,204},{12,192},{16,212},{20,216},{24,220},{28,20... | collective-permute-start | bytes 614408 | tf_op jit(solution)/shard_map/ppermute | solution.py:64
  87.2 16.7 %collective-permute-start.11 = (bf16[160,640]{1,0:T(8,128)(2,1)}, bf16[160,640]{1,0:T(8,128)(2,1)}, u32[]{:S(2)}, u32[]{:S(2)}) collective-permute-start(bf16[160,640]{1,0:T(8,128)(2,1)} %get-tuple-element.131), channel_id=1, source_target_pairs={{0,200},{4,204},{8,192},{12,196},{16,216},{20,220},{24,208},{28,21... | collective-permute-start | bytes 614408 | tf_op jit(solution)/shard_map/ppermute | solution.py:64
  100.8 20.9 %collective-permute-start.16 = (bf16[160,640]{1,0:T(8,128)(2,1)}, bf16[160,640]{1,0:T(8,128)(2,1)}, u32[]{:S(2)}, u32[]{:S(2)}) collective-permute-start(bf16[160,640]{1,0:T(8,128)(2,1)} %get-tuple-element.139), channel_id=1, source_target_pairs={{0,192},{4,196},{8,200},{12,204},{16,208},{20,212},{24,216},{28,22... | collective-permute-start | bytes 614408 | tf_op jit(solution)/shard_map/ppermute | solution.py:64
  103.9 11.3 %collective-permute-start.2 = (bf16[640,128]{1,0:T(8,128)(2,1)}, bf16[640,128]{1,0:T(8,128)(2,1)S(1)}, u32[]{:S(2)}, u32[]{:S(2)}) collective-permute-start(bf16[640,128]{1,0:T(8,128)(2,1)} %get-tuple-element.122), channel_id=1, source_target_pairs={{0,32},{4,36},{8,40},{12,44},{16,48},{20,52},{24,56},{28,60},{32,0... | collective-permute-start | bytes 491528 | tf_op jit(solution)/shard_map/ppermute | solution.py:35
  104.8 2.2 %copy-start.5 = (bf16[2,640,128]{2,1,0:T(8,128)(2,1)}, bf16[2,640,128]{2,1,0:T(8,128)(2,1)S(1)}, u32[]{:S(2)}) copy-start(bf16[2,640,128]{2,1,0:T(8,128)(2,1)S(1)} %collective-permute-done.7.s1) | copy-start | bytes 983044
  104.8 10.4 %collective-permute-start.1 = (bf16[640,128]{1,0:T(8,128)(2,1)}, bf16[640,128]{1,0:T(8,128)(2,1)S(1)}, u32[]{:S(2)}, u32[]{:S(2)}) collective-permute-start(bf16[640,128]{1,0:T(8,128)(2,1)} %get-tuple-element.121), channel_id=1, source_target_pairs={{0,48},{4,52},{8,56},{12,60},{16,0},{20,4},{24,8},{28,12},{32,16},... | collective-permute-start | bytes 491528 | tf_op jit(solution)/shard_map/ppermute | solution.py:35
  106.6 8.6 %collective-permute-start.3 = (bf16[640,128]{1,0:T(8,128)(2,1)}, bf16[640,128]{1,0:T(8,128)(2,1)}, u32[]{:S(2)}, u32[]{:S(2)}) collective-permute-start(bf16[640,128]{1,0:T(8,128)(2,1)} %get-tuple-element.123), channel_id=1, source_target_pairs={{0,16},{4,20},{8,24},{12,28},{16,32},{20,36},{24,40},{28,44},{32,4... | collective-permute-start | bytes 491528 | tf_op jit(solution)/shard_map/ppermute | solution.py:35
  106.8 16.1 %collective-permute-start.17 = (bf16[160,640]{1,0:T(8,128)(2,1)}, bf16[160,640]{1,0:T(8,128)(2,1)}, u32[]{:S(2)}, u32[]{:S(2)}) collective-permute-start(bf16[160,640]{1,0:T(8,128)(2,1)} %get-tuple-element.141), channel_id=1, source_target_pairs={{0,204},{4,192},{8,196},{12,200},{16,220},{20,208},{24,212},{28,21... | collective-permute-start | bytes 614408 | tf_op jit(solution)/shard_map/ppermute | solution.py:64
  117.2 43.7 %collective-permute-start.12 = (bf16[160,640]{1,0:T(8,128)(2,1)}, bf16[160,640]{1,0:T(8,128)(2,1)}, u32[]{:S(2)}, u32[]{:S(2)}) collective-permute-start(bf16[160,640]{1,0:T(8,128)(2,1)} %get-tuple-element.133), channel_id=1, source_target_pairs={{0,64},{4,68},{8,72},{12,76},{16,80},{20,84},{24,88},{28,92},{32,9... | collective-permute-start | bytes 614408 | tf_op jit(solution)/shard_map/ppermute | solution.py:60
  120.5 40.5 %collective-permute-start.13 = (bf16[160,640]{1,0:T(8,128)(2,1)}, bf16[160,640]{1,0:T(8,128)(2,1)}, u32[]{:S(2)}, u32[]{:S(2)}) collective-permute-start(bf16[160,640]{1,0:T(8,128)(2,1)} %get-tuple-element.134), channel_id=1, source_target_pairs={{0,76},{4,64},{8,68},{12,72},{16,92},{20,80},{24,84},{28,88},{32,1... | collective-permute-start | bytes 614408 | tf_op jit(solution)/shard_map/ppermute | solution.py:60
  121.3 39.6 %collective-permute-start.14 = (bf16[160,640]{1,0:T(8,128)(2,1)}, bf16[160,640]{1,0:T(8,128)(2,1)}, u32[]{:S(2)}, u32[]{:S(2)}) collective-permute-start(bf16[160,640]{1,0:T(8,128)(2,1)} %get-tuple-element.135), channel_id=1, source_target_pairs={{0,72},{4,76},{8,64},{12,68},{16,88},{20,92},{24,80},{28,84},{32,1... | collective-permute-start | bytes 614408 | tf_op jit(solution)/shard_map/ppermute | solution.py:60
  121.7 39.2 %collective-permute-start.15 = (bf16[160,640]{1,0:T(8,128)(2,1)}, bf16[160,640]{1,0:T(8,128)(2,1)}, u32[]{:S(2)}, u32[]{:S(2)}) collective-permute-start(bf16[160,640]{1,0:T(8,128)(2,1)} %get-tuple-element.136), channel_id=1, source_target_pairs={{0,68},{4,72},{8,76},{12,64},{16,84},{20,88},{24,92},{28,80},{32,1... | collective-permute-start | bytes 614408 | tf_op jit(solution)/shard_map/ppermute | solution.py:60
  125.8 25.2 %all-to-all-start = ((f32[64,8,128]{2,1,0:T(8,128)}), f32[64,8,128]{2,1,0:T(8,128)S(1)}, u32[]{:S(2)}, u32[]{:S(2)}) async-start(f32[64,8,128]{2,1,0:T(8,128)} %body.2), calls=%async_computation | async-start | bytes 524288 | tf_op jit(solution)/shard_map/while/body/all_to_all | solution.py:346
  151.0 0.7 copy-start.1
  153.4 7.5 %collective-permute-start.18 = (f32[4,2560]{1,0:T(4,128)}, f32[4,2560]{1,0:T(4,128)S(1)}, u32[]{:S(2)}, u32[]{:S(2)}) collective-permute-start(f32[4,2560]{1,0:T(4,128)} %get-tuple-element.143), channel_id=1, source_target_pairs={{0,64},{64,128},{128,192},{192,0},{1,65},{65,129},{129,193},{193,1... | collective-permute-start | bytes 122888 | tf_op jit(solution)/shard_map/ppermute | solution.py:354

commit v5 on v4

--- a/solution.py
+++ b/solution.py
@@ -281,6 +281,8 @@
     parts = qkv[0, 0].transpose(1, 0, 2)
     cots = call(cut_cotangent_kernel, [flat] * SIDE, 0, 1_600_000, z, cotangent[0, 0])
     cots_z = [None] * SIDE
+    for k in (2, 0):
+        cots_z[k] = away(cots[k], k)
     cosine, sine = rope_tables(positions[0])
     main, *shared = call(
         prep_kernel,
@@ -294,7 +296,8 @@
         sine,
     )
     shared_z = exchanged(along_z, shared)
-    main = lax.all_to_all(main, "ctx", 0, 0)
+    prepared = shared
+    main = lax.all_to_all(after(main, (cots_z[0], cots_z[2])), "ctx", 0, 0)
     gate = jnp.dot(embed(step), mod_weight[0], precision=lax.Precision.HIGHEST)[None]
     rows = FREQS // (SIDE * SIDE * SIDE)
     index = (ctx * SIDE + lax.axis_index("dp").astype(jnp.int32)) * rows
@@ -308,25 +311,23 @@
     (back[0],) = call(
         functools.partial(main_kernel, (0,)), [single], 840_000_000, 2_000_000, x, main
     )
-    for k in (2, 1):
-        cots_z[k] = away(after(cots[k], shared_z), k)
+    for k in (1, 3):
+        cots_z[k] = away(after(cots[k], prepared), k)
     pair = call(
         pack_kernel,
         shape((2, ROWS, HEAD_DIM)),
         0,
         1_300_000,
-        *shared_z,
+        *after(shared_z, (back[2], cots_z[1], cots_z[3])),
         smem=0,
     )
     pairs = [pair] + [along_x(pair, k) for k in steps]
     shared_out = call(
         shared_kernel, single, 840_000_000, 1_600_000, *shared_z, *pairs, smem=0
     )
-    for k in (3, 0):
-        cots_z[k] = away(after(cots[k], back[2]), k)
     back = [back[0]] + [along_x(back[m], SIDE - m) for m in steps]
     joined = call(
-        join_kernel, [flat] * SIDE, 0, 1_600_000, place, *back, after(shared_out, cots_z[1:3])
+        join_kernel, [flat] * SIDE, 0, 1_600_000, place, *back, shared_out
     )
     at_home = [None] * SIDE
     for k in (2, 1, 3, 0):

time: 164 us -> 173 us (1.055)
  waiting for transfers between devices: 67.7 us -> 81.9 us
  starting transfers between devices: 51.2 us -> 44.5 us
    all_to_all x1, waiting for transfers between devices: 0.01 us -> 48.1 us  [local(): main = lax.all_to_all(after(main, (cots_z[0], cots_z[2])), 'ctx', 0, 0)]
    ppermute x3, waiting for transfers between devices: 46.3 us -> 0.01 us  [along_z(): return lax.ppermute(value, 'ctx', pairs)]
    ppermute x6, waiting for transfers between devices: 0.02 us -> 11.4 us  [along_x(): return lax.ppermute(value, 'ctx', pairs)]
    ppermute x4, starting transfers between devices: 7.28 us -> 2.22 us  [away(): return lax.ppermute(value, ('segment', 'ctx'), section_pairs(SIDE - 1, by))]
    ppermute x4, waiting for transfers between devices: 0.01 us -> 3.25 us  [away(): return lax.ppermute(value, ('segment', 'ctx'), section_pairs(SIDE - 1, by))]
    all_to_all x1, waiting for transfers between devices: 13.9 us -> 11.7 us  [gradient(): chans = lax.all_to_all(chans, ('ctx', 'dp'), 0, 0)]
  transfers between devices with their start and end apart: 21 -> 21, of which waited for: 4 -> 5; matrix products, arithmetic and copies ran while one was open for 4% -> 4% of each run, Pallas kernels for 17% -> 16%
where the time goes in v5:
time: 173 us
  waiting for transfers between devices  81.9 us (47%)
  starting transfers between devices  44.5 us (26%)
  Pallas kernels  34.4 us (20%)
  local copies, waits for them, and re-layouts  4.98 us (3%)
  other arithmetic  3.43 us (2%)
  matrix products  1.93 us (1%)
    all_to_all x1, waiting for transfers between devices, local(): main = lax.all_to_all(after(main, (cots_z[0], cots_z[2])), 'ctx', 0, 0)  48.1 us
    pallas_call x9, Pallas kernels, call(): pl.pallas_call(kernel, grid=grid, out_shape=out_shape, in_specs=specs, ou...  32.1 us
    all_to_all x1, waiting for transfers between devices, gradient(): chans = lax.all_to_all(chans, ('ctx', 'dp'), 0, 0)  11.7 us
    ppermute x6, waiting for transfers between devices, along_x(): return lax.ppermute(value, 'ctx', pairs)  11.4 us
    all_to_all x1, starting transfers between devices, gradient(): chans = lax.all_to_all(chans, ('ctx', 'dp'), 0, 0)  9.61 us
    ppermute x1, waiting for transfers between devices, local(): lax.ppermute(grad, 'segment', [(i, (i + 1) % SIDE) for i in range(SIDE)])  7.54 us
    ppermute x6, starting transfers between devices, along_x(): return lax.ppermute(value, 'ctx', pairs)  7.02 us
    ppermute x1, starting transfers between devices, local(): lax.ppermute(gains, 'segment', [((i + 1) % SIDE, i) for i in range(SIDE)])  6.7 us
  transfers between devices with their start and end apart: 21, of which 5 were waited for; matrix products, arithmetic and copies ran while one was open for 4% of the time, Pallas kernels for 16%

profile of v5, /device:TPU:8, one launch (start us, length us, event | category | flops | bytes accessed | tf_op | source)
XLA Modules:
  0.0 172.8 jit_solution(14921881540250532284)
XLA Ops:
  2.2 6.7 %collective-permute-start = (f32[3,2560]{1,0:T(4,128)S(1)}, f32[3,2560]{1,0:T(4,128)}, u32[]{:S(2)}, u32[]{:S(2)}) collective-permute-start(f32[3,2560]{1,0:T(4,128)S(1)} %concatenate.16), channel_id=1, source_target_pairs={{64,0},{128,64},{192,128},{0,192},{65,1},{129,65},{193,129},{1,193... | collective-permute-start | bytes 92168 | tf_op jit(solution)/shard_map/ppermute | solution.py:280
  8.9 2.1 %shard_map.123 = (bf16[160,640]{1,0:T(8,128)(2,1)}, bf16[160,640]{1,0:T(8,128)(2,1)}, bf16[160,640]{1,0:T(8,128)(2,1)}, bf16[160,640]{1,0:T(8,128)(2,1)}) custom-call(s32[1]{0:T(128)} %bitcast.1.z_ref, bf16[160,2560]{1,0:T(8,128)(2,1)} %bitcast.24), custom_call_target="tpu_custom_call" | custom-call | tf_op jit(solution)/shard_map/pallas_call | solution.py:97
  13.1 1.1 fusion.4
  14.2 0.8 pad_maximum_fusion
  15.0 4.5 %shard_map.122 = (bf16[16,3,160,128]{3,2,1,0:T(8,128)(2,1)}, bf16[3,160,128]{2,1,0:T(8,128)(2,1)}, bf16[3,160,128]{2,1,0:T(8,128)(2,1)}, bf16[3,160,128]{2,1,0:T(8,128)(2,1)}, bf16[3,160,128]{2,1,0:T(8,128)(2,1)}) custom-call(s32[1]{0:T(128)} %bitcast.1.z_ref, bf16[3,160,2560]{2,1,0:T(8,128)(2,1)} %bitcast.22, f32[3,2560]{1,0:T(4,128)} %collective-permute-done.gain_ref, ...), custom_call_target="tpu_custom_call" | custom-call | tf_op jit(solution)/shard_map/pallas_call | solution.py:97
  19.5 3.2 %collective-permute-done.2 = bf16[160,640]{1,0:T(8,128)(2,1)} collective-permute-done((bf16[160,640]{1,0:T(8,128)(2,1)}, bf16[160,640]{1,0:T(8,128)(2,1)}, u32[]{:S(2)}, u32[]{:S(2)}) %collective-permute-start.2) | collective-permute-done | bytes 204832 | tf_op jit(solution)/shard_map/ppermute | solution.py:64
  22.8 6.5 %all-to-all-start.1 = ((bf16[16,3,160,128]{3,2,1,0:T(8,128)(2,1)}), bf16[16,3,160,128]{3,2,1,0:T(8,128)(2,1)}, u32[]{:S(2)}, u32[]{:S(2)}) async-start(bf16[16,3,160,128]{3,2,1,0:T(8,128)(2,1)} %get-tuple-element.124), calls=%async_computation.1 | async-start | bytes 3932160 | tf_op jit(solution)/shard_map/all_to_all | solution.py:300
  29.4 2.0 %collective-permute-start.6 = (bf16[3,160,128]{2,1,0:T(8,128)(2,1)}, bf16[3,160,128]{2,1,0:T(8,128)(2,1)S(1)}, u32[]{:S(2)}, u32[]{:S(2)}) collective-permute-start(bf16[3,160,128]{2,1,0:T(8,128)(2,1)} %get-tuple-element.130), channel_id=1, source_target_pairs={{0,4},{4,8},{8,12},{12,0},{16,20},{20,24},{24,28},{28,16},{32,36},... | collective-permute-start | bytes 368648 | tf_op jit(solution)/shard_map/ppermute | solution.py:30
  31.3 2.4 %collective-permute-start.7 = (bf16[3,160,128]{2,1,0:T(8,128)(2,1)}, bf16[3,160,128]{2,1,0:T(8,128)(2,1)S(1)}, u32[]{:S(2)}, u32[]{:S(2)}) collective-permute-start(bf16[3,160,128]{2,1,0:T(8,128)(2,1)} %get-tuple-element.131), channel_id=1, source_target_pairs={{0,8},{4,12},{8,0},{12,4},{16,24},{20,28},{24,16},{28,20},{32,40},... | collective-permute-start | bytes 368648 | tf_op jit(solution)/shard_map/ppermute | solution.py:30
  33.7 1.5 collective-permute-start.8
  35.1 1.2 collective-permute-start.9
  36.7 1.9 %fusion.gate_ref = f32[1,2560]{1,0:T(1,128)} fusion(f32[256,1]{0,1:T(1,128)S(1)} %bitcast.27, f32[1,256,2560]{2,1,0:T(8,128)S(1)} %copy-done), kind=kOutput, calls=%fused_computation | convolution fusion | flops 7864320 | bytes 2632704 | tf_op jit(solution)/shard_map/dot_general | solution.py:301
  38.7 48.1 %all-to-all-done.1.r_ref = bf16[16,3,160,128]{3,2,1,0:T(8,128)(2,1)} async-done(((bf16[16,3,160,128]{3,2,1,0:T(8,128)(2,1)}), bf16[16,3,160,128]{3,2,1,0:T(8,128)(2,1)}, u32[]{:S(2)}, u32[]{:S(2)}) %all-to-all-start.1) | async-done | bytes 1966112 | tf_op jit(solution)/shard_map/all_to_all | solution.py:300
  86.8 9.5 %shard_map.125 = (bf16[640,128]{1,0:T(8,128)(2,1)}, bf16[640,128]{1,0:T(8,128)(2,1)}, bf16[640,128]{1,0:T(8,128)(2,1)}) custom-call(s32[1]{0:T(128)} %bitcast.2.x_ref, bf16[16,3,160,128]{3,2,1,0:T(8,128)(2,1)} %all-to-all-done.1.r_ref), custom_call_target="tpu_custom_call" | custom-call | tf_op jit(solution)/shard_map/pallas_call | solution.py:97
  97.0 1.8 %shard_map.126.s0 = bf16[2,640,128]{2,1,0:T(8,128)(2,1)} custom-call(bf16[3,160,128]{2,1,0:T(8,128)(2,1)} %get-tuple-element.137.s0.q0, bf16[3,160,128]{2,1,0:T(8,128)(2,1)} %copy-done.2, bf16[3,160,128]{2,1,0:T(8,128)(2,1)} %copy-done.3, bf16[3,160,128]{2,1,0:T(8,128)(2,1)} %copy-done.4), custom_call_target="tpu_custom_call" | custom-call | tf_op jit(solution)/shard_map/pallas_call | solution.py:97
  98.9 2.3 %collective-permute-start.12 = (bf16[2,640,128]{2,1,0:T(8,128)(2,1)}, bf16[2,640,128]{2,1,0:T(8,128)(2,1)S(1)}, u32[]{:S(2)}, u32[]{:S(2)}) collective-permute-start(bf16[2,640,128]{2,1,0:T(8,128)(2,1)} %shard_map.126.s0), channel_id=1, source_target_pairs={{0,32},{4,36},{8,40},{12,44},{16,48},{20,52},{24,56},{28,60},{32,0... | collective-permute-start | bytes 983048 | tf_op jit(solution)/shard_map/ppermute | solution.py:35
  101.2 1.2 collective-permute-start.13
  102.4 2.7 %collective-permute-start.4 = (bf16[640,128]{1,0:T(8,128)(2,1)}, bf16[640,128]{1,0:T(8,128)(2,1)S(1)}, u32[]{:S(2)}, u32[]{:S(2)}) collective-permute-start(bf16[640,128]{1,0:T(8,128)(2,1)} %get-tuple-element.127), channel_id=1, source_target_pairs={{0,32},{4,36},{8,40},{12,44},{16,48},{20,52},{24,56},{28,60},{32,0... | collective-permute-start | bytes 491528 | tf_op jit(solution)/shard_map/ppermute | solution.py:35
  105.0 0.9 collective-permute-start.3
  105.9 11.4 %collective-permute-done.11.s1 = bf16[2,640,128]{2,1,0:T(8,128)(2,1)S(1)} collective-permute-done((bf16[2,640,128]{2,1,0:T(8,128)(2,1)}, bf16[2,640,128]{2,1,0:T(8,128)(2,1)S(1)}, u32[]{:S(2)}, u32[]{:S(2)}) %collective-permute-start.11) | collective-permute-done | bytes 327712 | tf_op jit(solution)/shard_map/ppermute | solution.py:35
  117.3 4.2 %shard_map.124.refs_0_ = bf16[640,128]{1,0:T(8,128)(2,1)S(1)} custom-call(s32[1]{0:T(128)} %bitcast.2.x_ref, bf16[16,3,160,128]{3,2,1,0:T(8,128)(2,1)} %all-to-all-done.1.r_ref), custom_call_target="tpu_custom_call" | custom-call | tf_op jit(solution)/shard_map/pallas_call | solution.py:97
  122.3 0.7 copy-done.7
  123.0 4.0 %shard_map.127.refs_4_ = bf16[640,128]{1,0:T(8,128)(2,1)S(1)} custom-call(bf16[3,160,128]{2,1,0:T(8,128)(2,1)} %get-tuple-element.137.s0.q0, bf16[3,160,128]{2,1,0:T(8,128)(2,1)} %copy-done.2, bf16[3,160,128]{2,1,0:T(8,128)(2,1)} %copy-done.3, bf16[3,160,128]{2,1,0:T(8,128)(2,1)} %copy-done.4, bf16[2,640,128]{2,1,0:T(8,128)(2,1)} %shard_map.126.s0, ...), custom_call_target="tpu_custom_call" | custom-call | tf_op jit(solution)/shard_map/pallas_call | solution.py:97
  127.1 2.0 %shard_map.128 = (bf16[160,640]{1,0:T(8,128)(2,1)}, bf16[160,640]{1,0:T(8,128)(2,1)}, bf16[160,640]{1,0:T(8,128)(2,1)}, bf16[160,640]{1,0:T(8,128)(2,1)}) custom-call(s32[2]{0:T(128)S(1)} %pad_add_fusion.place_ref, bf16[640,128]{1,0:T(8,128)(2,1)S(1)} %shard_map.124.refs_0_, bf16[640,128]{1,0:T(8,128)(2,1)S(1)} %collective-permute-done.3.refs_1_, ...), custom_call_target="tpu_custom_call" | custom-call | tf_op jit(solution)/shard_map/pallas_call | solution.py:97
  129.2 6.6 %collective-permute-start.17 = (bf16[160,640]{1,0:T(8,128)(2,1)}, bf16[160,640]{1,0:T(8,128)(2,1)}, u32[]{:S(2)}, u32[]{:S(2)}) collective-permute-start(bf16[160,640]{1,0:T(8,128)(2,1)} %get-tuple-element.144), channel_id=1, source_target_pairs={{0,68},{4,72},{8,76},{12,64},{16,84},{20,88},{24,92},{28,80},{32,1... | collective-permute-start | bytes 614408 | tf_op jit(solution)/shard_map/ppermute | solution.py:60
  136.4 26.0 %while.12 = (s32[]{:T(128)}, f32[4,2560]{1,0:T(4,128)}, f32[4,128]{1,0:T(4,128)S(1)}, s32[]{:T(128)}, s32[]{:T(128)}, /*index=5*/bf16[640,128]{1,0:T(8,128)(2,1)...) while((s32[]{:T(128)}, f32[4,2560]{1,0:T(4,128)}, ...), condition=%wide.region_1.2_spmd, body=%wide.region_0.1_spmd.sunk | while | flops 2 | bytes 1835233 | solution.py:354
  136.4 2.3 %body.2 = f32[64,8,128]{2,1,0:T(8,128)} custom-call(s32[2]{0:T(128)S(1)} %get-tuple-element.357.place_ref, f32[3,2560]{1,0:T(4,128)} %get-tuple-element.358.time_ref, bf16[640,128]{1,0:T(8,128)(2,1)S(1)} %get-tuple-element.306.refs_0_, bf16[640,128]{1,0:T(8,128)(2,1)S(1)} %get-tuple-element.307.refs_1_, bf16[640,128]{1,0:T(8,128)(2,1)S(1)} %get-tuple-element.308.refs_2_, ...), custom_call_target="tpu_custom_call" | custom-call | tf_op jit(solution)/shard_map/while/body/pallas_call | solution.py:338
  138.7 9.6 %all-to-all-start = ((f32[64,8,128]{2,1,0:T(8,128)}), f32[64,8,128]{2,1,0:T(8,128)S(1)}, u32[]{:S(2)}, u32[]{:S(2)}) async-start(f32[64,8,128]{2,1,0:T(8,128)} %body.2), calls=%async_computation | async-start | bytes 524288 | tf_op jit(solution)/shard_map/while/body/all_to_all | solution.py:347
  148.3 11.7 %all-to-all-done.chan_ref = f32[64,8,128]{2,1,0:T(8,128)S(1)} async-done(((f32[64,8,128]{2,1,0:T(8,128)}), f32[64,8,128]{2,1,0:T(8,128)S(1)}, u32[]{:S(2)}, u32[]{:S(2)}) %all-to-all-start) | async-done | bytes 262176 | tf_op jit(solution)/shard_map/while/body/all_to_all | solution.py:347
  160.7 1.7 body.3
  162.4 7.5 %collective-permute-done.18 = f32[4,2560]{1,0:T(4,128)S(1)} collective-permute-done((f32[4,2560]{1,0:T(4,128)}, f32[4,2560]{1,0:T(4,128)S(1)}, u32[]{:S(2)}, u32[]{:S(2)}) %collective-permute-start.18) | collective-permute-done | bytes 40992 | tf_op jit(solution)/shard_map/ppermute | solution.py:355
  169.9 2.3 %shard_map.129 = bf16[160,2560]{1,0:T(8,128)(2,1)} custom-call(s32[1]{0:T(128)} %bitcast.1.z_ref, bf16[160,640]{1,0:T(8,128)(2,1)} %collective-permute-done.14.a0, bf16[160,640]{1,0:T(8,128)(2,1)} %collective-permute-done.15.a1, bf16[160,640]{1,0:T(8,128)(2,1)} %collective-permute-done.16.a2, bf16[160,640]{1,0:T(8,128)(2,1)} %collective-permute-done.17.a3, ...), custom_call_target="tpu_custom_call" | custom-call | tf_op jit(solution)/shard_map/pallas_call | solution.py:97
  (62 shorter events, 7.0 us)
Async XLA Ops:
  0.6 36.1 %copy-start = (f32[1,256,2560]{2,1,0:T(8,128)S(1)}, f32[1,256,2560]{2,1,0:T(8,128)}, u32[]{:S(2)}) copy-start(f32[1,256,2560]{2,1,0:T(8,128)} %param.15) | copy-start | bytes 7864324
  2.2 12.8 %collective-permute-start = (f32[3,2560]{1,0:T(4,128)S(1)}, f32[3,2560]{1,0:T(4,128)}, u32[]{:S(2)}, u32[]{:S(2)}) collective-permute-start(f32[3,2560]{1,0:T(4,128)S(1)} %concatenate.16), channel_id=1, source_target_pairs={{64,0},{128,64},{192,128},{0,192},{65,1},{129,65},{193,129},{1,193... | collective-permute-start | bytes 92168 | tf_op jit(solution)/shard_map/ppermute | solution.py:280
  11.0 8.6 %collective-permute-start.1 = (bf16[160,640]{1,0:T(8,128)(2,1)}, bf16[160,640]{1,0:T(8,128)(2,1)}, u32[]{:S(2)}, u32[]{:S(2)}) collective-permute-start(bf16[160,640]{1,0:T(8,128)(2,1)} %get-tuple-element.122), channel_id=1, source_target_pairs={{0,192},{4,196},{8,200},{12,204},{16,208},{20,212},{24,216},{28,22... | collective-permute-start | bytes 614408 | tf_op jit(solution)/shard_map/ppermute | solution.py:64
  11.7 11.1 %collective-permute-start.2 = (bf16[160,640]{1,0:T(8,128)(2,1)}, bf16[160,640]{1,0:T(8,128)(2,1)}, u32[]{:S(2)}, u32[]{:S(2)}) collective-permute-start(bf16[160,640]{1,0:T(8,128)(2,1)} %get-tuple-element.123), channel_id=1, source_target_pairs={{0,200},{4,204},{8,192},{12,196},{16,216},{20,220},{24,208},{28,21... | collective-permute-start | bytes 614408 | tf_op jit(solution)/shard_map/ppermute | solution.py:64
  19.5 9.8 %copy-start.8 = (f32[128]{0:T(128)S(1)}, f32[128]{0:T(128)}, u32[]{:S(2)}) copy-start(f32[128]{0:T(128)} %constant.96.clone) | copy-start | bytes 1540
  19.5 14.2 %copy-start.11 = (bf16[3,160,128]{2,1,0:T(8,128)(2,1)S(1)}, bf16[3,160,128]{2,1,0:T(8,128)(2,1)}, u32[]{:S(2)}) copy-start(bf16[3,160,128]{2,1,0:T(8,128)(2,1)} %get-tuple-element.132) | copy-start | bytes 368644
  19.5 15.6 %copy-start.10 = (bf16[160,640]{1,0:T(8,128)(2,1)S(1)}, bf16[160,640]{1,0:T(8,128)(2,1)}, u32[]{:S(2)}) copy-start(bf16[160,640]{1,0:T(8,128)(2,1)} %get-tuple-element.134) | copy-start | bytes 614404
  19.5 16.8 %copy-start.9 = (bf16[160,640]{1,0:T(8,128)(2,1)S(1)}, bf16[160,640]{1,0:T(8,128)(2,1)}, u32[]{:S(2)}) copy-start(bf16[160,640]{1,0:T(8,128)(2,1)} %get-tuple-element.136) | copy-start | bytes 614404
  22.8 15.8 %copy-start.12 = (f32[256]{0:T(256)S(1)}, f32[256]{0:T(256)}, u32[]{:S(2)}) copy-start(f32[256]{0:T(256)} %constant.97.clone) | copy-start | bytes 3076
  22.8 64.0 %all-to-all-start.1 = ((bf16[16,3,160,128]{3,2,1,0:T(8,128)(2,1)}), bf16[16,3,160,128]{3,2,1,0:T(8,128)(2,1)}, u32[]{:S(2)}, u32[]{:S(2)}) async-start(bf16[16,3,160,128]{3,2,1,0:T(8,128)(2,1)} %get-tuple-element.124), calls=%async_computation.1 | async-start | bytes 3932160 | tf_op jit(solution)/shard_map/all_to_all | solution.py:300
  29.4 67.0 %collective-permute-start.6 = (bf16[3,160,128]{2,1,0:T(8,128)(2,1)}, bf16[3,160,128]{2,1,0:T(8,128)(2,1)S(1)}, u32[]{:S(2)}, u32[]{:S(2)}) collective-permute-start(bf16[3,160,128]{2,1,0:T(8,128)(2,1)} %get-tuple-element.130), channel_id=1, source_target_pairs={{0,4},{4,8},{8,12},{12,0},{16,20},{20,24},{24,28},{28,16},{32,36},... | collective-permute-start | bytes 368648 | tf_op jit(solution)/shard_map/ppermute | solution.py:30
  31.3 65.0 %collective-permute-start.7 = (bf16[3,160,128]{2,1,0:T(8,128)(2,1)}, bf16[3,160,128]{2,1,0:T(8,128)(2,1)S(1)}, u32[]{:S(2)}, u32[]{:S(2)}) collective-permute-start(bf16[3,160,128]{2,1,0:T(8,128)(2,1)} %get-tuple-element.131), channel_id=1, source_target_pairs={{0,8},{4,12},{8,0},{12,4},{16,24},{20,28},{24,16},{28,20},{32,40},... | collective-permute-start | bytes 368648 | tf_op jit(solution)/shard_map/ppermute | solution.py:30
  33.7 62.7 %collective-permute-start.8 = (bf16[3,160,128]{2,1,0:T(8,128)(2,1)S(1)}, bf16[3,160,128]{2,1,0:T(8,128)(2,1)S(1)}, u32[]{:S(2)}, u32[]{:S(2)}) collective-permute-start(bf16[3,160,128]{2,1,0:T(8,128)(2,1)S(1)} %copy-done.11), channel_id=1, source_target_pairs={{0,12},{4,0},{8,4},{12,8},{16,28},{20,16},{24,20},{28,24},{32,44},... | collective-permute-start | bytes 368648 | tf_op jit(solution)/shard_map/ppermute | solution.py:30
  35.1 61.2 %collective-permute-start.9 = (bf16[160,640]{1,0:T(8,128)(2,1)S(1)}, bf16[160,640]{1,0:T(8,128)(2,1)}, u32[]{:S(2)}, u32[]{:S(2)}) collective-permute-start(bf16[160,640]{1,0:T(8,128)(2,1)S(1)} %copy-done.10), channel_id=1, source_target_pairs={{0,196},{4,200},{8,204},{12,192},{16,212},{20,216},{24,220},{28,20... | collective-permute-start | bytes 614408 | tf_op jit(solution)/shard_map/ppermute | solution.py:64
  36.3 60.1 %collective-permute-start.10 = (bf16[160,640]{1,0:T(8,128)(2,1)S(1)}, bf16[160,640]{1,0:T(8,128)(2,1)}, u32[]{:S(2)}, u32[]{:S(2)}) collective-permute-start(bf16[160,640]{1,0:T(8,128)(2,1)S(1)} %copy-done.9), channel_id=1, source_target_pairs={{0,204},{4,192},{8,196},{12,200},{16,220},{20,208},{24,212},{28,21... | collective-permute-start | bytes 614408 | tf_op jit(solution)/shard_map/ppermute | solution.py:64
  96.3 0.7 copy-start.4
  98.9 18.4 %collective-permute-start.11 = (bf16[2,640,128]{2,1,0:T(8,128)(2,1)}, bf16[2,640,128]{2,1,0:T(8,128)(2,1)S(1)}, u32[]{:S(2)}, u32[]{:S(2)}) collective-permute-start(bf16[2,640,128]{2,1,0:T(8,128)(2,1)} %shard_map.126.s0), channel_id=1, source_target_pairs={{0,16},{4,20},{8,24},{12,28},{16,32},{20,36},{24,40},{28,44},{32,4... | collective-permute-start | bytes 983048 | tf_op jit(solution)/shard_map/ppermute | solution.py:35
  98.9 22.6 %collective-permute-start.12 = (bf16[2,640,128]{2,1,0:T(8,128)(2,1)}, bf16[2,640,128]{2,1,0:T(8,128)(2,1)S(1)}, u32[]{:S(2)}, u32[]{:S(2)}) collective-permute-start(bf16[2,640,128]{2,1,0:T(8,128)(2,1)} %shard_map.126.s0), channel_id=1, source_target_pairs={{0,32},{4,36},{8,40},{12,44},{16,48},{20,52},{24,56},{28,60},{32,0... | collective-permute-start | bytes 983048 | tf_op jit(solution)/shard_map/ppermute | solution.py:35
  101.2 20.3 %collective-permute-start.13 = (bf16[2,640,128]{2,1,0:T(8,128)(2,1)}, bf16[2,640,128]{2,1,0:T(8,128)(2,1)S(1)}, u32[]{:S(2)}, u32[]{:S(2)}) collective-permute-start(bf16[2,640,128]{2,1,0:T(8,128)(2,1)} %shard_map.126.s0), channel_id=1, source_target_pairs={{0,48},{4,52},{8,56},{12,60},{16,0},{20,4},{24,8},{28,12},{32,16},... | collective-permute-start | bytes 983048 | tf_op jit(solution)/shard_map/ppermute | solution.py:35
  102.4 24.7 %collective-permute-start.4 = (bf16[640,128]{1,0:T(8,128)(2,1)}, bf16[640,128]{1,0:T(8,128)(2,1)S(1)}, u32[]{:S(2)}, u32[]{:S(2)}) collective-permute-start(bf16[640,128]{1,0:T(8,128)(2,1)} %get-tuple-element.127), channel_id=1, source_target_pairs={{0,32},{4,36},{8,40},{12,44},{16,48},{20,52},{24,56},{28,60},{32,0... | collective-permute-start | bytes 491528 | tf_op jit(solution)/shard_map/ppermute | solution.py:35
  105.0 22.0 %collective-permute-start.3 = (bf16[640,128]{1,0:T(8,128)(2,1)}, bf16[640,128]{1,0:T(8,128)(2,1)S(1)}, u32[]{:S(2)}, u32[]{:S(2)}) collective-permute-start(bf16[640,128]{1,0:T(8,128)(2,1)} %get-tuple-element.126), channel_id=1, source_target_pairs={{0,48},{4,52},{8,56},{12,60},{16,0},{20,4},{24,8},{28,12},{32,16},... | collective-permute-start | bytes 491528 | tf_op jit(solution)/shard_map/ppermute | solution.py:35
  117.2 4.3 %copy-start.5 = (bf16[2,640,128]{2,1,0:T(8,128)(2,1)}, bf16[2,640,128]{2,1,0:T(8,128)(2,1)S(1)}, u32[]{:S(2)}) copy-start(bf16[2,640,128]{2,1,0:T(8,128)(2,1)S(1)} %collective-permute-done.11.s1) | copy-start | bytes 983044
  117.2 9.8 %collective-permute-start.5 = (bf16[640,128]{1,0:T(8,128)(2,1)}, bf16[640,128]{1,0:T(8,128)(2,1)}, u32[]{:S(2)}, u32[]{:S(2)}) collective-permute-start(bf16[640,128]{1,0:T(8,128)(2,1)} %get-tuple-element.128), channel_id=1, source_target_pairs={{0,16},{4,20},{8,24},{12,28},{16,32},{20,36},{24,40},{28,44},{32,4... | collective-permute-start | bytes 491528 | tf_op jit(solution)/shard_map/ppermute | solution.py:35
  121.5 0.7 copy-start.6
  122.2 0.7 copy-start.7
  129.1 40.8 %collective-permute-start.14 = (bf16[160,640]{1,0:T(8,128)(2,1)}, bf16[160,640]{1,0:T(8,128)(2,1)}, u32[]{:S(2)}, u32[]{:S(2)}) collective-permute-start(bf16[160,640]{1,0:T(8,128)(2,1)} %get-tuple-element.141), channel_id=1, source_target_pairs={{0,64},{4,68},{8,72},{12,76},{16,80},{20,84},{24,88},{28,92},{32,9... | collective-permute-start | bytes 614408 | tf_op jit(solution)/shard_map/ppermute | solution.py:60
  129.1 40.8 %collective-permute-start.15 = (bf16[160,640]{1,0:T(8,128)(2,1)}, bf16[160,640]{1,0:T(8,128)(2,1)}, u32[]{:S(2)}, u32[]{:S(2)}) collective-permute-start(bf16[160,640]{1,0:T(8,128)(2,1)} %get-tuple-element.142), channel_id=1, source_target_pairs={{0,76},{4,64},{8,68},{12,72},{16,92},{20,80},{24,84},{28,88},{32,1... | collective-permute-start | bytes 614408 | tf_op jit(solution)/shard_map/ppermute | solution.py:60
  129.1 40.8 %collective-permute-start.16 = (bf16[160,640]{1,0:T(8,128)(2,1)}, bf16[160,640]{1,0:T(8,128)(2,1)}, u32[]{:S(2)}, u32[]{:S(2)}) collective-permute-start(bf16[160,640]{1,0:T(8,128)(2,1)} %get-tuple-element.143), channel_id=1, source_target_pairs={{0,72},{4,76},{8,64},{12,68},{16,88},{20,92},{24,80},{28,84},{32,1... | collective-permute-start | bytes 614408 | tf_op jit(solution)/shard_map/ppermute | solution.py:60
  129.2 40.8 %collective-permute-start.17 = (bf16[160,640]{1,0:T(8,128)(2,1)}, bf16[160,640]{1,0:T(8,128)(2,1)}, u32[]{:S(2)}, u32[]{:S(2)}) collective-permute-start(bf16[160,640]{1,0:T(8,128)(2,1)} %get-tuple-element.144), channel_id=1, source_target_pairs={{0,68},{4,72},{8,76},{12,64},{16,84},{20,88},{24,92},{28,80},{32,1... | collective-permute-start | bytes 614408 | tf_op jit(solution)/shard_map/ppermute | solution.py:60
  138.7 21.3 %all-to-all-start = ((f32[64,8,128]{2,1,0:T(8,128)}), f32[64,8,128]{2,1,0:T(8,128)S(1)}, u32[]{:S(2)}, u32[]{:S(2)}) async-start(f32[64,8,128]{2,1,0:T(8,128)} %body.2), calls=%async_computation | async-start | bytes 524288 | tf_op jit(solution)/shard_map/while/body/all_to_all | solution.py:347
  160.0 0.7 copy-start.1
  162.4 7.5 %collective-permute-start.18 = (f32[4,2560]{1,0:T(4,128)}, f32[4,2560]{1,0:T(4,128)S(1)}, u32[]{:S(2)}, u32[]{:S(2)}) collective-permute-start(f32[4,2560]{1,0:T(4,128)} %get-tuple-element.147), channel_id=1, source_target_pairs={{0,64},{64,128},{128,192},{192,0},{1,65},{65,129},{129,193},{193,1... | collective-permute-start | bytes 122888 | tf_op jit(solution)/shard_map/ppermute | solution.py:355
  (2 other events, 1.3 us)

commit v6 on v1

--- a/solution.py
+++ b/solution.py
@@ -319,18 +319,20 @@
     for k in (2, 1, 3, 0):
         at_home[k] = home(joined[k], (SIDE - k) % SIDE)
 
+    sums = pl.pallas_call(
+        channels_kernel,
+        out_shape=shape((SIDE * count, 8, HEAD_DIM), jnp.float32),
+        in_specs=[SMEM_SPEC] + [VMEM_SPEC] * (1 + GROUP + SIDE),
+        out_specs=VMEM_SPEC,
+        scratch_shapes=[pltpu.VMEM((8, HEAD_DIM), jnp.float32)],
+        compiler_params=VMEM,
+        cost_estimate=pl.CostEstimate(flops=0, bytes_accessed=0, transcendentals=0),
+    )(place, gains, *back, shared_out, *cots_z)
+    sums = home(sums, 0)
+
     def gradient(_, state):
-        attn, before = lax.optimization_barrier(([*back, shared_out], state[1]))
-        chans = pl.pallas_call(
-            channels_kernel,
-            out_shape=shape((SIDE * count, 8, HEAD_DIM), jnp.float32),
-            in_specs=[SMEM_SPEC] + [VMEM_SPEC] * (1 + GROUP + SIDE),
-            out_specs=VMEM_SPEC,
-            scratch_shapes=[pltpu.VMEM((8, HEAD_DIM), jnp.float32)],
-            compiler_params=VMEM,
-            cost_estimate=pl.CostEstimate(flops=0, bytes_accessed=0, transcendentals=0),
-        )(place, gains, *attn, *cots_z)
-        chans = lax.all_to_all(chans, ("ctx", "dp"), 0, 0)
+        mine, before = lax.optimization_barrier((sums, state[1]))
+        chans = lax.all_to_all(mine, ("ctx", "dp"), 0, 0)
         grad = call(grad_kernel, zeros, 0, 200_000, index[None], freq, before, chans)
         return (grad, before)
 
@@ -338,10 +340,9 @@
     turns = jnp.where(step < 1000, 1, 2)
     start = (jnp.zeros((rows, WIDTH), jnp.float32), jnp.zeros((rows, HEAD_DIM), jnp.float32))
     grad, _ = lax.fori_loop(0, turns, gradient, start)
-    grad = lax.ppermute(grad, "segment", [(i, (i + 1) % SIDE) for i in range(SIDE)])
 
     attn_out = call(
-        finish_kernel, shape((TOK, WIDTH)), 500_000, 1_700_000, z, *at_home, gate
+        finish_kernel, shape((TOK, WIDTH)), 500_000, 1_700_000, z, *at_home, after(gate, grad)
     )
     return (attn_out[None, None], grad[None])
 

time: 162 us -> 166 us (1.025)
  Pallas kernels: 32.5 us -> 34.4 us
    ppermute x4 -> x5, waiting for transfers between devices: 0.01 us -> 11.5 us  [home(): return lax.ppermute(value, ('segment', 'ctx'), section_pairs(1, by))]
    ppermute x1 -> x0, waiting for transfers between devices: 7.75 us -> none  [local(): lax.ppermute(grad, 'segment', [(i, (i + 1) % SIDE) for i in range(SIDE)])]
    all_to_all x1, starting transfers between devices: 11.4 us -> 7.46 us  [gradient(): chans = lax.all_to_all(mine, ('ctx', 'dp'), 0, 0)]
    ppermute x4 -> x5, starting transfers between devices: 4.53 us -> 7.18 us  [home(): return lax.ppermute(value, ('segment', 'ctx'), section_pairs(1, by))]
    all_to_all x1, waiting for transfers between devices: 13 us -> 10.6 us  [gradient(): chans = lax.all_to_all(mine, ('ctx', 'dp'), 0, 0)]
  transfers between devices with their start and end apart: 21 -> 21, of which waited for: 5 -> 5; matrix products, arithmetic and copies ran while one was open for 4% -> 4% of each run, Pallas kernels for 16% -> 15%
where the time goes in v6:
time: 166 us
  waiting for transfers between devices  70.4 us (42%)
  starting transfers between devices  47.9 us (29%)
  Pallas kernels  34.4 us (21%)
  local copies, waits for them, and re-layouts  5.17 us (3%)
  other arithmetic  3.98 us (2%)
  matrix products  1.94 us (1%)
  between operations  1.68 us (1%)
    all_to_all x1, waiting for transfers between devices, local(): main = lax.all_to_all(after(main, shared_z), 'ctx', 0, 0)  40.9 us
    pallas_call x8, Pallas kernels, call(): pl.pallas_call(kernel, grid=grid, out_shape=out_shape, in_specs=specs, ou...  31.9 us
    ppermute x5, waiting for transfers between devices, home(): return lax.ppermute(value, ('segment', 'ctx'), section_pairs(1, by))  11.5 us
    all_to_all x1, waiting for transfers between devices, gradient(): chans = lax.all_to_all(mine, ('ctx', 'dp'), 0, 0)  10.6 us
    ppermute x6, starting transfers between devices, along_x(): return lax.ppermute(value, 'ctx', pairs)  8.86 us
    all_to_all x1, starting transfers between devices, local(): main = lax.all_to_all(after(main, shared_z), 'ctx', 0, 0)  7.57 us
    all_to_all x1, starting transfers between devices, gradient(): chans = lax.all_to_all(mine, ('ctx', 'dp'), 0, 0)  7.46 us
    ppermute x3, waiting for transfers between devices, along_z(): return lax.ppermute(value, 'ctx', pairs)  7.28 us
  transfers between devices with their start and end apart: 21, of which 5 were waited for; matrix products, arithmetic and copies ran while one was open for 4% of the time, Pallas kernels for 15%

profile of v6, /device:TPU:8, one launch (start us, length us, event | category | flops | bytes accessed | tf_op | source)
XLA Modules:
  0.0 165.5 jit_solution(15941861527733438886)
XLA Ops:
  2.2 6.7 %collective-permute-start = (f32[3,2560]{1,0:T(4,128)S(1)}, f32[3,2560]{1,0:T(4,128)S(1)}, u32[]{:S(2)}, u32[]{:S(2)}) collective-permute-start(f32[3,2560]{1,0:T(4,128)S(1)} %concatenate.19), channel_id=1, source_target_pairs={{64,0},{128,64},{192,128},{0,192},{65,1},{129,65},{193,129},{1,193... | collective-permute-start | bytes 92168 | tf_op jit(solution)/shard_map/ppermute | solution.py:274
  12.8 4.5 %shard_map.122 = (bf16[16,3,160,128]{3,2,1,0:T(8,128)(2,1)}, bf16[3,160,128]{2,1,0:T(8,128)(2,1)}, bf16[3,160,128]{2,1,0:T(8,128)(2,1)}, bf16[3,160,128]{2,1,0:T(8,128)(2,1)}, bf16[3,160,128]{2,1,0:T(8,128)(2,1)}) custom-call(s32[1]{0:T(128)} %bitcast.1.z_ref, bf16[3,160,2560]{2,1,0:T(8,128)(2,1)} %bitcast.22, f32[3,2560]{1,0:T(4,128)} %copy-done.17, ...), custom_call_target="tpu_custom_call" | custom-call | tf_op jit(solution)/shard_map/pallas_call | solution.py:97
  18.5 1.5 collective-permute-start.2
  19.9 1.9 %collective-permute-start.3 = (bf16[3,160,128]{2,1,0:T(8,128)(2,1)}, bf16[3,160,128]{2,1,0:T(8,128)(2,1)S(1)}, u32[]{:S(2)}, u32[]{:S(2)}) collective-permute-start(bf16[3,160,128]{2,1,0:T(8,128)(2,1)} %get-tuple-element.69), channel_id=1, source_target_pairs={{0,12},{4,0},{8,4},{12,8},{16,28},{20,16},{24,20},{28,24},{32,44},... | collective-permute-start | bytes 368648 | tf_op jit(solution)/shard_map/ppermute | solution.py:30
  21.8 3.9 %collective-permute-done.1.q1 = bf16[3,160,128]{2,1,0:T(8,128)(2,1)S(1)} collective-permute-done((bf16[3,160,128]{2,1,0:T(8,128)(2,1)}, bf16[3,160,128]{2,1,0:T(8,128)(2,1)S(1)}, u32[]{:S(2)}, u32[]{:S(2)}) %collective-permute-start.1) | collective-permute-done | bytes 122912 | tf_op jit(solution)/shard_map/ppermute | solution.py:30
  25.8 3.4 %collective-permute-done.2.q2 = bf16[3,160,128]{2,1,0:T(8,128)(2,1)S(1)} collective-permute-done((bf16[3,160,128]{2,1,0:T(8,128)(2,1)}, bf16[3,160,128]{2,1,0:T(8,128)(2,1)S(1)}, u32[]{:S(2)}, u32[]{:S(2)}) %collective-permute-start.2) | collective-permute-done | bytes 122912 | tf_op jit(solution)/shard_map/ppermute | solution.py:30
  29.1 7.6 %all-to-all-start.1 = ((bf16[16,3,160,128]{3,2,1,0:T(8,128)(2,1)}), bf16[16,3,160,128]{3,2,1,0:T(8,128)(2,1)}, u32[]{:S(2)}, u32[]{:S(2)}) async-start(bf16[16,3,160,128]{3,2,1,0:T(8,128)(2,1)} %get-tuple-element.70), calls=%async_computation.1 | async-start | bytes 3932160 | tf_op jit(solution)/shard_map/all_to_all | solution.py:293
  36.7 2.1 %shard_map.126 = (bf16[160,640]{1,0:T(8,128)(2,1)}, bf16[160,640]{1,0:T(8,128)(2,1)}, bf16[160,640]{1,0:T(8,128)(2,1)}, bf16[160,640]{1,0:T(8,128)(2,1)}) custom-call(s32[1]{0:T(128)} %bitcast.1.z_ref, bf16[160,2560]{1,0:T(8,128)(2,1)} %bitcast.24), custom_call_target="tpu_custom_call" | custom-call | tf_op jit(solution)/shard_map/pallas_call | solution.py:97
  38.8 2.2 %collective-permute-start.10 = (bf16[160,640]{1,0:T(8,128)(2,1)}, bf16[160,640]{1,0:T(8,128)(2,1)S(1)}, u32[]{:S(2)}, u32[]{:S(2)}) collective-permute-start(bf16[160,640]{1,0:T(8,128)(2,1)} %get-tuple-element.75), channel_id=1, source_target_pairs={{0,196},{4,200},{8,204},{12,192},{16,212},{20,216},{24,220},{28,20... | collective-permute-start | bytes 614408 | tf_op jit(solution)/shard_map/ppermute | solution.py:64
  41.0 1.2 collective-permute-start.11
  42.6 1.5 collective-permute-start.7
  44.1 2.7 %collective-permute-start.8 = (bf16[2,640,128]{2,1,0:T(8,128)(2,1)S(1)}, bf16[2,640,128]{2,1,0:T(8,128)(2,1)}, u32[]{:S(2)}, u32[]{:S(2)}) collective-permute-start(bf16[2,640,128]{2,1,0:T(8,128)(2,1)S(1)} %pad_maximum_fusion.s0), channel_id=1, source_target_pairs={{0,32},{4,36},{8,40},{12,44},{16,48},{20,52},{24,56},{28,60},{32,0... | collective-permute-start | bytes 983048 | tf_op jit(solution)/shard_map/ppermute | solution.py:35
  46.8 1.5 collective-permute-start.9
  48.3 1.9 %fusion.gate_ref = f32[1,2560]{1,0:T(1,128)} fusion(f32[256,1]{0,1:T(1,128)S(1)} %bitcast.27, f32[1,256,2560]{2,1,0:T(8,128)S(1)} %copy-done), kind=kOutput, calls=%fused_computation | convolution fusion | flops 7864320 | bytes 2632704 | tf_op jit(solution)/shard_map/dot_general | solution.py:296
  50.2 40.9 %all-to-all-done.1.r_ref = bf16[16,3,160,128]{3,2,1,0:T(8,128)(2,1)} async-done(((bf16[16,3,160,128]{3,2,1,0:T(8,128)(2,1)}), bf16[16,3,160,128]{3,2,1,0:T(8,128)(2,1)}, u32[]{:S(2)}, u32[]{:S(2)}) %all-to-all-start.1) | async-done | bytes 1966112 | tf_op jit(solution)/shard_map/all_to_all | solution.py:293
  91.2 9.5 %shard_map.124 = (bf16[640,128]{1,0:T(8,128)(2,1)}, bf16[640,128]{1,0:T(8,128)(2,1)}, bf16[640,128]{1,0:T(8,128)(2,1)}) custom-call(s32[1]{0:T(128)} %bitcast.2.x_ref, bf16[16,3,160,128]{3,2,1,0:T(8,128)(2,1)} %all-to-all-done.1.r_ref), custom_call_target="tpu_custom_call" | custom-call | tf_op jit(solution)/shard_map/pallas_call | solution.py:97
  100.7 2.2 %collective-permute-start.16 = (bf16[160,640]{1,0:T(8,128)(2,1)}, bf16[160,640]{1,0:T(8,128)(2,1)S(1)}, u32[]{:S(2)}, u32[]{:S(2)}) collective-permute-start(bf16[160,640]{1,0:T(8,128)(2,1)} %get-tuple-element.84), channel_id=1, source_target_pairs={{0,192},{4,196},{8,200},{12,204},{16,208},{20,212},{24,216},{28,22... | collective-permute-start | bytes 614408 | tf_op jit(solution)/shard_map/ppermute | solution.py:64
  102.9 1.2 collective-permute-start.5
  104.1 1.5 collective-permute-start.4
  106.7 4.7 %shard_map.125.refs_4_ = bf16[640,128]{1,0:T(8,128)(2,1)} custom-call(bf16[3,160,128]{2,1,0:T(8,128)(2,1)} %get-tuple-element.66.q0, bf16[3,160,128]{2,1,0:T(8,128)(2,1)} %copy-done.7, bf16[3,160,128]{2,1,0:T(8,128)(2,1)} %copy-done.8, bf16[3,160,128]{2,1,0:T(8,128)(2,1)} %copy-done.9, bf16[2,640,128]{2,1,0:T(8,128)(2,1)} %copy-done.2, ...), custom_call_target="tpu_custom_call" | custom-call | tf_op jit(solution)/shard_map/pallas_call | solution.py:97
  111.4 4.8 %shard_map.123.refs_0_ = bf16[640,128]{1,0:T(8,128)(2,1)} custom-call(s32[1]{0:T(128)} %bitcast.2.x_ref, bf16[16,3,160,128]{3,2,1,0:T(8,128)(2,1)} %all-to-all-done.1.r_ref), custom_call_target="tpu_custom_call" | custom-call | tf_op jit(solution)/shard_map/pallas_call | solution.py:97
  117.8 2.5 %shard_map.128 = f32[64,8,128]{2,1,0:T(8,128)} custom-call(s32[2]{0:T(128)} %pad_add_fusion.place_ref, f32[3,2560]{1,0:T(4,128)} %copy-done.17, bf16[640,128]{1,0:T(8,128)(2,1)} %shard_map.123.refs_0_, bf16[640,128]{1,0:T(8,128)(2,1)} %copy-done.4, bf16[640,128]{1,0:T(8,128)(2,1)} %copy-done.3, bf16[640,128]{1,0:T(8,128)(2,1)} %copy-done.5, ...), custom_call_target="tpu_custom_call" | custom-call | tf_op jit(solution)/shard_map/pallas_call | solution.py:322
  120.3 2.3 %shard_map.127 = (bf16[160,640]{1,0:T(8,128)(2,1)}, bf16[160,640]{1,0:T(8,128)(2,1)}, bf16[160,640]{1,0:T(8,128)(2,1)}, bf16[160,640]{1,0:T(8,128)(2,1)}) custom-call(s32[2]{0:T(128)} %pad_add_fusion.place_ref, bf16[640,128]{1,0:T(8,128)(2,1)} %shard_map.123.refs_0_, bf16[640,128]{1,0:T(8,128)(2,1)} %copy-done.4, bf16[640,128]{1,0:T(8,128)(2,1)} %copy-done.3, ...), custom_call_target="tpu_custom_call" | custom-call | tf_op jit(solution)/shard_map/pallas_call | solution.py:97
  122.6 1.2 collective-permute-start.12
  123.8 1.6 collective-permute-start.13
  125.4 4.4 %collective-permute-start.14 = (bf16[160,640]{1,0:T(8,128)(2,1)}, bf16[160,640]{1,0:T(8,128)(2,1)S(1)}, u32[]{:S(2)}, u32[]{:S(2)}) collective-permute-start(bf16[160,640]{1,0:T(8,128)(2,1)} %get-tuple-element.80), channel_id=1, source_target_pairs={{0,72},{4,76},{8,64},{12,68},{16,88},{20,92},{24,80},{28,84},{32,1... | collective-permute-start | bytes 614408 | tf_op jit(solution)/shard_map/ppermute | solution.py:60
  129.8 11.5 %collective-permute-done.18 = f32[64,8,128]{2,1,0:T(8,128)} collective-permute-done((f32[64,8,128]{2,1,0:T(8,128)}, f32[64,8,128]{2,1,0:T(8,128)}, u32[]{:S(2)}, u32[]{:S(2)}) %collective-permute-start.18) | collective-permute-done | bytes 262176 | tf_op jit(solution)/shard_map/ppermute | solution.py:60
  141.9 20.5 %while.12 = (s32[]{:T(128)}, f32[4,2560]{1,0:T(4,128)}, f32[4,128]{1,0:T(4,128)S(1)}, s32[]{:T(128)}, s32[]{:T(128)}, /*index=5*/f32[64,8,128]{2,1,0:T(8,128)}, f32[4,128]{1,0:T(4,128)S(1)}, s32[]{:T(128)}) while((s32[]{:T(128)}, f32[4,2560]{1,0:T(4,128)}, f32[4,128]{1,0:T(4,128)S(1)}, s32[]{:T(128)}, s32[]{:T(128)}, ...), condition=%wide.region_1.2_spmd, body=%wide.region_0.1_spmd.sunk | while | flops 2 | bytes 1835153 | solution.py:342
  141.9 7.5 %all-to-all-start = ((f32[64,8,128]{2,1,0:T(8,128)}), f32[64,8,128]{2,1,0:T(8,128)S(1)}, u32[]{:S(2)}, u32[]{:S(2)}) async-start(f32[64,8,128]{2,1,0:T(8,128)} %get-tuple-element.164), calls=%async_computation | async-start | bytes 524288 | tf_op jit(solution)/shard_map/while/body/all_to_all | solution.py:335
  149.4 10.6 %all-to-all-done.chan_ref = f32[64,8,128]{2,1,0:T(8,128)S(1)} async-done(((f32[64,8,128]{2,1,0:T(8,128)}), f32[64,8,128]{2,1,0:T(8,128)S(1)}, u32[]{:S(2)}, u32[]{:S(2)}) %all-to-all-start) | async-done | bytes 262176 | tf_op jit(solution)/shard_map/while/body/all_to_all | solution.py:335
  160.7 1.7 %body.1 = f32[4,2560]{1,0:T(4,128)} custom-call(s32[1]{0:T(128)} %bitcast.21.index_ref, f32[4,128]{1,0:T(4,128)S(1)} %get-tuple-element.187.freq_ref, f32[4,128]{1,0:T(4,128)S(1)} %get-tuple-element.183.before_ref, f32[64,8,128]{2,1,0:T(8,128)} %copy-done.1), custom_call_target="tpu_custom_call" | custom-call | tf_op jit(solution)/shard_map/while/body/pallas_call | solution.py:97
  163.2 2.3 %shard_map.129 = bf16[160,2560]{1,0:T(8,128)(2,1)} custom-call(s32[1]{0:T(128)} %bitcast.1.z_ref, bf16[160,640]{1,0:T(8,128)(2,1)} %copy-done.11, bf16[160,640]{1,0:T(8,128)(2,1)} %copy-done.12, bf16[160,640]{1,0:T(8,128)(2,1)} %copy-done.13, bf16[160,640]{1,0:T(8,128)(2,1)} %collective-permute-done.15.a3, f32[1,2560]{1,0:T(1,128)} %fusion.gate_ref), custom_call_target="tpu_custom_call" | custom-call | tf_op jit(solution)/shard_map/pallas_call | solution.py:97
  (79 shorter events, 10.9 us)
Async XLA Ops:
  0.6 47.6 %copy-start = (f32[1,256,2560]{2,1,0:T(8,128)S(1)}, f32[1,256,2560]{2,1,0:T(8,128)}, u32[]{:S(2)}) copy-start(f32[1,256,2560]{2,1,0:T(8,128)} %param.15) | copy-start | bytes 7864324
  2.2 10.0 %collective-permute-start = (f32[3,2560]{1,0:T(4,128)S(1)}, f32[3,2560]{1,0:T(4,128)S(1)}, u32[]{:S(2)}, u32[]{:S(2)}) collective-permute-start(f32[3,2560]{1,0:T(4,128)S(1)} %concatenate.19), channel_id=1, source_target_pairs={{64,0},{128,64},{192,128},{0,192},{65,1},{129,65},{193,129},{1,193... | collective-permute-start | bytes 92168 | tf_op jit(solution)/shard_map/ppermute | solution.py:274
  17.4 24.9 %copy-start.19 = (f32[256]{0:T(256)S(1)}, f32[256]{0:T(256)}, u32[]{:S(2)}) copy-start(f32[256]{0:T(256)} %constant.97.clone) | copy-start | bytes 3076
  17.4 25.0 %copy-start.18 = (f32[128]{0:T(128)S(1)}, f32[128]{0:T(128)}, u32[]{:S(2)}) copy-start(f32[128]{0:T(128)} %constant.96.clone) | copy-start | bytes 1540
  17.4 25.1 %copy-start.6 = (bf16[3,160,128]{2,1,0:T(8,128)(2,1)S(1)}, bf16[3,160,128]{2,1,0:T(8,128)(2,1)}, u32[]{:S(2)}) copy-start(bf16[3,160,128]{2,1,0:T(8,128)(2,1)} %get-tuple-element.66.q0) | copy-start | bytes 368644
  17.4 8.4 %collective-permute-start.1 = (bf16[3,160,128]{2,1,0:T(8,128)(2,1)}, bf16[3,160,128]{2,1,0:T(8,128)(2,1)S(1)}, u32[]{:S(2)}, u32[]{:S(2)}) collective-permute-start(bf16[3,160,128]{2,1,0:T(8,128)(2,1)} %get-tuple-element.67), channel_id=1, source_target_pairs={{0,4},{4,8},{8,12},{12,0},{16,20},{20,24},{24,28},{28,16},{32,36},... | collective-permute-start | bytes 368648 | tf_op jit(solution)/shard_map/ppermute | solution.py:30
  18.5 10.7 %collective-permute-start.2 = (bf16[3,160,128]{2,1,0:T(8,128)(2,1)}, bf16[3,160,128]{2,1,0:T(8,128)(2,1)S(1)}, u32[]{:S(2)}, u32[]{:S(2)}) collective-permute-start(bf16[3,160,128]{2,1,0:T(8,128)(2,1)} %get-tuple-element.68), channel_id=1, source_target_pairs={{0,8},{4,12},{8,0},{12,4},{16,24},{20,28},{24,16},{28,20},{32,40},... | collective-permute-start | bytes 368648 | tf_op jit(solution)/shard_map/ppermute | solution.py:30
  19.9 9.2 %collective-permute-start.3 = (bf16[3,160,128]{2,1,0:T(8,128)(2,1)}, bf16[3,160,128]{2,1,0:T(8,128)(2,1)S(1)}, u32[]{:S(2)}, u32[]{:S(2)}) collective-permute-start(bf16[3,160,128]{2,1,0:T(8,128)(2,1)} %get-tuple-element.69), channel_id=1, source_target_pairs={{0,12},{4,0},{8,4},{12,8},{16,28},{20,16},{24,20},{28,24},{32,44},... | collective-permute-start | bytes 368648 | tf_op jit(solution)/shard_map/ppermute | solution.py:30
  25.8 16.7 %copy-start.7 = (bf16[3,160,128]{2,1,0:T(8,128)(2,1)}, bf16[3,160,128]{2,1,0:T(8,128)(2,1)S(1)}, u32[]{:S(2)}) copy-start(bf16[3,160,128]{2,1,0:T(8,128)(2,1)S(1)} %collective-permute-done.1.q1) | copy-start | bytes 368644
  29.1 13.4 %copy-start.8 = (bf16[3,160,128]{2,1,0:T(8,128)(2,1)}, bf16[3,160,128]{2,1,0:T(8,128)(2,1)S(1)}, u32[]{:S(2)}) copy-start(bf16[3,160,128]{2,1,0:T(8,128)(2,1)S(1)} %collective-permute-done.2.q2) | copy-start | bytes 368644
  29.1 13.4 %copy-start.9 = (bf16[3,160,128]{2,1,0:T(8,128)(2,1)}, bf16[3,160,128]{2,1,0:T(8,128)(2,1)S(1)}, u32[]{:S(2)}) copy-start(bf16[3,160,128]{2,1,0:T(8,128)(2,1)S(1)} %collective-permute-done.3.q3) | copy-start | bytes 368644
  29.1 62.0 %all-to-all-start.1 = ((bf16[16,3,160,128]{3,2,1,0:T(8,128)(2,1)}), bf16[16,3,160,128]{3,2,1,0:T(8,128)(2,1)}, u32[]{:S(2)}, u32[]{:S(2)}) async-start(bf16[16,3,160,128]{3,2,1,0:T(8,128)(2,1)} %get-tuple-element.70), calls=%async_computation.1 | async-start | bytes 3932160 | tf_op jit(solution)/shard_map/all_to_all | solution.py:293
  38.8 61.8 %collective-permute-start.10 = (bf16[160,640]{1,0:T(8,128)(2,1)}, bf16[160,640]{1,0:T(8,128)(2,1)S(1)}, u32[]{:S(2)}, u32[]{:S(2)}) collective-permute-start(bf16[160,640]{1,0:T(8,128)(2,1)} %get-tuple-element.75), channel_id=1, source_target_pairs={{0,196},{4,200},{8,204},{12,192},{16,212},{20,216},{24,220},{28,20... | collective-permute-start | bytes 614408 | tf_op jit(solution)/shard_map/ppermute | solution.py:64
  41.0 61.9 %collective-permute-start.11 = (bf16[160,640]{1,0:T(8,128)(2,1)}, bf16[160,640]{1,0:T(8,128)(2,1)}, u32[]{:S(2)}, u32[]{:S(2)}) collective-permute-start(bf16[160,640]{1,0:T(8,128)(2,1)} %get-tuple-element.76), channel_id=1, source_target_pairs={{0,200},{4,204},{8,192},{12,196},{16,216},{20,220},{24,208},{28,21... | collective-permute-start | bytes 614408 | tf_op jit(solution)/shard_map/ppermute | solution.py:64
  42.6 64.1 %copy-start.2 = (bf16[2,640,128]{2,1,0:T(8,128)(2,1)}, bf16[2,640,128]{2,1,0:T(8,128)(2,1)S(1)}, u32[]{:S(2)}) copy-start(bf16[2,640,128]{2,1,0:T(8,128)(2,1)S(1)} %pad_maximum_fusion.s0) | copy-start | bytes 983044
  42.6 60.3 %collective-permute-start.7 = (bf16[2,640,128]{2,1,0:T(8,128)(2,1)S(1)}, bf16[2,640,128]{2,1,0:T(8,128)(2,1)S(1)}, u32[]{:S(2)}, u32[]{:S(2)}) collective-permute-start(bf16[2,640,128]{2,1,0:T(8,128)(2,1)S(1)} %pad_maximum_fusion.s0), channel_id=1, source_target_pairs={{0,16},{4,20},{8,24},{12,28},{16,32},{20,36},{24,40},{28,44},{32,4... | collective-permute-start | bytes 983048 | tf_op jit(solution)/shard_map/ppermute | solution.py:35
  44.1 60.0 %collective-permute-start.8 = (bf16[2,640,128]{2,1,0:T(8,128)(2,1)S(1)}, bf16[2,640,128]{2,1,0:T(8,128)(2,1)}, u32[]{:S(2)}, u32[]{:S(2)}) collective-permute-start(bf16[2,640,128]{2,1,0:T(8,128)(2,1)S(1)} %pad_maximum_fusion.s0), channel_id=1, source_target_pairs={{0,32},{4,36},{8,40},{12,44},{16,48},{20,52},{24,56},{28,60},{32,0... | collective-permute-start | bytes 983048 | tf_op jit(solution)/shard_map/ppermute | solution.py:35
  46.8 58.7 %collective-permute-start.9 = (bf16[2,640,128]{2,1,0:T(8,128)(2,1)S(1)}, bf16[2,640,128]{2,1,0:T(8,128)(2,1)}, u32[]{:S(2)}, u32[]{:S(2)}) collective-permute-start(bf16[2,640,128]{2,1,0:T(8,128)(2,1)S(1)} %pad_maximum_fusion.s0), channel_id=1, source_target_pairs={{0,48},{4,52},{8,56},{12,60},{16,0},{20,4},{24,8},{28,12},{32,16},... | collective-permute-start | bytes 983048 | tf_op jit(solution)/shard_map/ppermute | solution.py:35
  100.7 15.6 %copy-start.14 = (bf16[160,640]{1,0:T(8,128)(2,1)}, bf16[160,640]{1,0:T(8,128)(2,1)S(1)}, u32[]{:S(2)}) copy-start(bf16[160,640]{1,0:T(8,128)(2,1)S(1)} %collective-permute-done.10.refs_6_) | copy-start | bytes 614404
  100.7 15.6 %collective-permute-start.16 = (bf16[160,640]{1,0:T(8,128)(2,1)}, bf16[160,640]{1,0:T(8,128)(2,1)S(1)}, u32[]{:S(2)}, u32[]{:S(2)}) collective-permute-start(bf16[160,640]{1,0:T(8,128)(2,1)} %get-tuple-element.84), channel_id=1, source_target_pairs={{0,192},{4,196},{8,200},{12,204},{16,208},{20,212},{24,216},{28,22... | collective-permute-start | bytes 614408 | tf_op jit(solution)/shard_map/ppermute | solution.py:64
  102.9 13.4 %collective-permute-start.17 = (bf16[160,640]{1,0:T(8,128)(2,1)}, bf16[160,640]{1,0:T(8,128)(2,1)S(1)}, u32[]{:S(2)}, u32[]{:S(2)}) collective-permute-start(bf16[160,640]{1,0:T(8,128)(2,1)} %get-tuple-element.86), channel_id=1, source_target_pairs={{0,204},{4,192},{8,196},{12,200},{16,220},{20,208},{24,212},{28,21... | collective-permute-start | bytes 614408 | tf_op jit(solution)/shard_map/ppermute | solution.py:64
  102.9 3.8 %copy-start.10 = (bf16[2,640,128]{2,1,0:T(8,128)(2,1)}, bf16[2,640,128]{2,1,0:T(8,128)(2,1)S(1)}, u32[]{:S(2)}) copy-start(bf16[2,640,128]{2,1,0:T(8,128)(2,1)S(1)} %collective-permute-done.7.s1) | copy-start | bytes 983044
  102.9 13.3 %collective-permute-start.5 = (bf16[640,128]{1,0:T(8,128)(2,1)}, bf16[640,128]{1,0:T(8,128)(2,1)S(1)}, u32[]{:S(2)}, u32[]{:S(2)}) collective-permute-start(bf16[640,128]{1,0:T(8,128)(2,1)} %get-tuple-element.73), channel_id=1, source_target_pairs={{0,32},{4,36},{8,40},{12,44},{16,48},{20,52},{24,56},{28,60},{32,0... | collective-permute-start | bytes 491528 | tf_op jit(solution)/shard_map/ppermute | solution.py:35
  104.1 12.1 %collective-permute-start.4 = (bf16[640,128]{1,0:T(8,128)(2,1)}, bf16[640,128]{1,0:T(8,128)(2,1)S(1)}, u32[]{:S(2)}, u32[]{:S(2)}) collective-permute-start(bf16[640,128]{1,0:T(8,128)(2,1)} %get-tuple-element.72), channel_id=1, source_target_pairs={{0,48},{4,52},{8,56},{12,60},{16,0},{20,4},{24,8},{28,12},{32,16},... | collective-permute-start | bytes 491528 | tf_op jit(solution)/shard_map/ppermute | solution.py:35
  105.5 10.7 %collective-permute-start.6 = (bf16[640,128]{1,0:T(8,128)(2,1)}, bf16[640,128]{1,0:T(8,128)(2,1)S(1)}, u32[]{:S(2)}, u32[]{:S(2)}) collective-permute-start(bf16[640,128]{1,0:T(8,128)(2,1)} %get-tuple-element.74), channel_id=1, source_target_pairs={{0,16},{4,20},{8,24},{12,28},{16,32},{20,36},{24,40},{28,44},{32,4... | collective-permute-start | bytes 491528 | tf_op jit(solution)/shard_map/ppermute | solution.py:35
  116.3 0.8 copy-start.15
  120.3 21.0 %collective-permute-start.18 = (f32[64,8,128]{2,1,0:T(8,128)}, f32[64,8,128]{2,1,0:T(8,128)}, u32[]{:S(2)}, u32[]{:S(2)}) collective-permute-start(f32[64,8,128]{2,1,0:T(8,128)} %shard_map.128), channel_id=1, source_target_pairs={{0,64},{4,68},{8,72},{12,76},{16,80},{20,84},{24,88},{28,92},{32,9... | collective-permute-start | bytes 786440 | tf_op jit(solution)/shard_map/ppermute | solution.py:60
  122.6 39.8 %collective-permute-start.12 = (bf16[160,640]{1,0:T(8,128)(2,1)}, bf16[160,640]{1,0:T(8,128)(2,1)S(1)}, u32[]{:S(2)}, u32[]{:S(2)}) collective-permute-start(bf16[160,640]{1,0:T(8,128)(2,1)} %get-tuple-element.78), channel_id=1, source_target_pairs={{0,64},{4,68},{8,72},{12,76},{16,80},{20,84},{24,88},{28,92},{32,9... | collective-permute-start | bytes 614408 | tf_op jit(solution)/shard_map/ppermute | solution.py:60
  123.8 38.6 %collective-permute-start.13 = (bf16[160,640]{1,0:T(8,128)(2,1)}, bf16[160,640]{1,0:T(8,128)(2,1)S(1)}, u32[]{:S(2)}, u32[]{:S(2)}) collective-permute-start(bf16[160,640]{1,0:T(8,128)(2,1)} %get-tuple-element.79), channel_id=1, source_target_pairs={{0,76},{4,64},{8,68},{12,72},{16,92},{20,80},{24,84},{28,88},{32,1... | collective-permute-start | bytes 614408 | tf_op jit(solution)/shard_map/ppermute | solution.py:60
  125.4 37.0 %collective-permute-start.14 = (bf16[160,640]{1,0:T(8,128)(2,1)}, bf16[160,640]{1,0:T(8,128)(2,1)S(1)}, u32[]{:S(2)}, u32[]{:S(2)}) collective-permute-start(bf16[160,640]{1,0:T(8,128)(2,1)} %get-tuple-element.80), channel_id=1, source_target_pairs={{0,72},{4,76},{8,64},{12,68},{16,88},{20,92},{24,80},{28,84},{32,1... | collective-permute-start | bytes 614408 | tf_op jit(solution)/shard_map/ppermute | solution.py:60
  129.8 32.7 %collective-permute-start.15 = (bf16[160,640]{1,0:T(8,128)(2,1)}, bf16[160,640]{1,0:T(8,128)(2,1)}, u32[]{:S(2)}, u32[]{:S(2)}) collective-permute-start(bf16[160,640]{1,0:T(8,128)(2,1)} %get-tuple-element.81), channel_id=1, source_target_pairs={{0,68},{4,72},{8,76},{12,64},{16,84},{20,88},{24,92},{28,80},{32,1... | collective-permute-start | bytes 614408 | tf_op jit(solution)/shard_map/ppermute | solution.py:60
  141.9 18.1 %all-to-all-start = ((f32[64,8,128]{2,1,0:T(8,128)}), f32[64,8,128]{2,1,0:T(8,128)S(1)}, u32[]{:S(2)}, u32[]{:S(2)}) async-start(f32[64,8,128]{2,1,0:T(8,128)} %get-tuple-element.164), calls=%async_computation | async-start | bytes 524288 | tf_op jit(solution)/shard_map/while/body/all_to_all | solution.py:335
  (9 other events, 6.4 us)

commit v7 on v1

--- a/solution.py
+++ b/solution.py
@@ -204,10 +204,10 @@
             outs[step][:, column(place)] = refs[source][rows_of(z, source, step)]
 
 
-def channels_kernel(place_ref, time_ref, *refs):
+def channels_kernel(place_ref, *refs):
     x, z = place_ref[0], place_ref[1]
     cots = refs[GROUP : GROUP + SIDE]
-    out_ref, chan_ref = refs[GROUP + SIDE :]
+    chan_ref = refs[GROUP + SIDE]
     chan_ref[...] = jnp.zeros_like(chan_ref)
     for source in range(GROUP):
         place = lax.rem(x + source, SIDE) if source < SIDE else SIDE
@@ -216,9 +216,12 @@
             attn = refs[source][rows_of(z, source, step)].astype(jnp.float32)
             total = total + attn * cots[step][:, column(place)].astype(jnp.float32)
         chan_ref[pl.ds(place, 1)] = jnp.sum(total, axis=0, keepdims=True)
-    chan_ref[GROUP : GROUP + 1] = time_ref[2:3, :HEAD_DIM]
+
+
+def spread_kernel(chan_ref, time_ref, out_ref):
     for i in range(out_ref.shape[0]):
         out_ref[i] = chan_ref[...]
+        out_ref[i, GROUP : GROUP + 1] = time_ref[...]
 
 
 def finish_kernel(z_ref, a0, a1, a2, a3, gate_ref, out_ref):
@@ -269,9 +272,8 @@
     flat = shape((TOK, GROUP * HEAD_DIM))
 
     step = timesteps[0, 0]
-    when = jnp.full((1, WIDTH), step.astype(jnp.float32))
-    gains = jnp.concatenate([qk_gain[0], when])
-    gains = lax.ppermute(gains, "segment", [((i + 1) % SIDE, i) for i in range(SIDE)])
+    when = jnp.full((1, HEAD_DIM), step.astype(jnp.float32))
+    gains = lax.ppermute(qk_gain[0], "segment", [((i + 1) % SIDE, i) for i in range(SIDE)])
     parts = qkv[0, 0].transpose(1, 0, 2)
     cots = call(cut_cotangent_kernel, [flat] * SIDE, 0, 1_600_000, z, cotangent[0, 0])
     cots_z = [None] * SIDE
@@ -319,17 +321,16 @@
     for k in (2, 1, 3, 0):
         at_home[k] = home(joined[k], (SIDE - k) % SIDE)
 
+    chan = call(
+        channels_kernel, shape((8, HEAD_DIM), jnp.float32), 0, 0, place, *back, shared_out, *cots_z
+    )
+    chan = home(chan, 0)
+
     def gradient(_, state):
-        attn, before = lax.optimization_barrier(([*back, shared_out], state[1]))
-        chans = pl.pallas_call(
-            channels_kernel,
-            out_shape=shape((SIDE * count, 8, HEAD_DIM), jnp.float32),
-            in_specs=[SMEM_SPEC] + [VMEM_SPEC] * (1 + GROUP + SIDE),
-            out_specs=VMEM_SPEC,
-            scratch_shapes=[pltpu.VMEM((8, HEAD_DIM), jnp.float32)],
-            compiler_params=VMEM,
-            cost_estimate=pl.CostEstimate(flops=0, bytes_accessed=0, transcendentals=0),
-        )(place, gains, *attn, *cots_z)
+        mine, before = lax.optimization_barrier((chan, state[1]))
+        chans = call(
+            spread_kernel, shape((SIDE * count, 8, HEAD_DIM), jnp.float32), 0, 0, mine, when, smem=0
+        )
         chans = lax.all_to_all(chans, ("ctx", "dp"), 0, 0)
         grad = call(grad_kernel, zeros, 0, 200_000, index[None], freq, before, chans)
         return (grad, before)
@@ -338,10 +339,9 @@
     turns = jnp.where(step < 1000, 1, 2)
     start = (jnp.zeros((rows, WIDTH), jnp.float32), jnp.zeros((rows, HEAD_DIM), jnp.float32))
     grad, _ = lax.fori_loop(0, turns, gradient, start)
-    grad = lax.ppermute(grad, "segment", [(i, (i + 1) % SIDE) for i in range(SIDE)])
 
     attn_out = call(
-        finish_kernel, shape((TOK, WIDTH)), 500_000, 1_700_000, z, *at_home, gate
+        finish_kernel, shape((TOK, WIDTH)), 500_000, 1_700_000, z, *after(at_home, grad), gate
     )
     return (attn_out[None, None], grad[None])
 

time: 162 us -> 169 us (1.043)
  starting transfers between devices: 48.8 us -> 54.7 us
  waiting for transfers between devices: 69.3 us -> 65.3 us
  Pallas kernels: 32.5 us -> 35.6 us
  local copies, waits for them, and re-layouts: 3.62 us -> 5.53 us
    ppermute x2 -> x1, waiting for transfers between devices: 7.75 us -> 0.01 us  [local(): lax.ppermute(qk_gain[0], 'segment', [((i + 1) % SIDE, i) for i in range(S...]
    ppermute x4 -> x5, waiting for transfers between devices: 0.01 us -> 7.28 us  [home(): return lax.ppermute(value, ('segment', 'ctx'), section_pairs(1, by))]
    pallas_call x8 -> x10, Pallas kernels: 30.3 us -> 35.6 us  [call(): pl.pallas_call(kernel, grid=grid, out_shape=out_shape, in_specs=specs, ou...]
    all_to_all x1, starting transfers between devices: 11.4 us -> 15 us  [gradient(): chans = lax.all_to_all(chans, ('ctx', 'dp'), 0, 0)]
    all_to_all x1, waiting for transfers between devices: 13 us -> 10.6 us  [gradient(): chans = lax.all_to_all(chans, ('ctx', 'dp'), 0, 0)]
    pallas_call x1 -> x0, Pallas kernels: 2.29 us -> none  [gradient(): pl.pallas_call(channels_kernel, out_shape=shape((SIDE * count, 8, HEAD_DI...]
    unnamed x19 -> x38, local copies, waits for them, and re-layouts: 1.38 us -> 3.52 us
    ppermute x4 -> x5, starting transfers between devices: 4.53 us -> 6.52 us  [home(): return lax.ppermute(value, ('segment', 'ctx'), section_pairs(1, by))]
  transfers between devices with their start and end apart: 21 -> 21, of which waited for: 5 -> 5; matrix products, arithmetic and copies ran while one was open for 4% -> 4% of each run, Pallas kernels for 16% -> 17%
where the time goes in v7:
time: 169 us
  waiting for transfers between devices  65.3 us (39%)
  starting transfers between devices  54.7 us (32%)
  Pallas kernels  35.6 us (21%)
  local copies, waits for them, and re-layouts  5.53 us (3%)
  other arithmetic  3.98 us (2%)
  matrix products  1.94 us (1%)
    all_to_all x1, waiting for transfers between devices, local(): main = lax.all_to_all(after(main, shared_z), 'ctx', 0, 0)  40.1 us
    pallas_call x10, Pallas kernels, call(): pl.pallas_call(kernel, grid=grid, out_shape=out_shape, in_specs=specs, ou...  35.6 us
    all_to_all x1, starting transfers between devices, gradient(): chans = lax.all_to_all(chans, ('ctx', 'dp'), 0, 0)  15 us
    all_to_all x1, waiting for transfers between devices, gradient(): chans = lax.all_to_all(chans, ('ctx', 'dp'), 0, 0)  10.6 us
    ppermute x6, starting transfers between devices, along_x(): return lax.ppermute(value, 'ctx', pairs)  8.64 us
    all_to_all x1, starting transfers between devices, local(): main = lax.all_to_all(after(main, shared_z), 'ctx', 0, 0)  7.58 us
    ppermute x5, waiting for transfers between devices, home(): return lax.ppermute(value, ('segment', 'ctx'), section_pairs(1, by))  7.28 us
    ppermute x3, waiting for transfers between devices, along_z(): return lax.ppermute(value, 'ctx', pairs)  7.28 us
  transfers between devices with their start and end apart: 21, of which 5 were waited for; matrix products, arithmetic and copies ran while one was open for 4% of the time, Pallas kernels for 17%

profile of v7, /device:TPU:8, one launch (start us, length us, event | category | flops | bytes accessed | tf_op | source)
XLA Modules:
  0.0 168.7 jit_solution(6669088457228495280)
XLA Ops:
  0.6 6.7 %collective-permute-start = (f32[2,2560]{1,0:T(2,128)}, f32[2,2560]{1,0:T(2,128)S(1)}, u32[]{:S(2)}, u32[]{:S(2)}) collective-permute-start(f32[2,2560]{1,0:T(2,128)} %bitcast.30), channel_id=1, source_target_pairs={{64,0},{128,64},{192,128},{0,192},{65,1},{129,65},{193,129},{1,193... | collective-permute-start | bytes 61448 | tf_op jit(solution)/shard_map/ppermute | solution.py:276
  11.3 4.5 %shard_map.122 = (bf16[16,3,160,128]{3,2,1,0:T(8,128)(2,1)}, bf16[3,160,128]{2,1,0:T(8,128)(2,1)}, bf16[3,160,128]{2,1,0:T(8,128)(2,1)}, bf16[3,160,128]{2,1,0:T(8,128)(2,1)}, bf16[3,160,128]{2,1,0:T(8,128)(2,1)}) custom-call(s32[1]{0:T(128)} %bitcast.z_ref, bf16[3,160,2560]{2,1,0:T(8,128)(2,1)} %bitcast.22, f32[2,2560]{1,0:T(2,128)} %copy-done.16, ...), custom_call_target="tpu_custom_call" | custom-call | tf_op jit(solution)/shard_map/pallas_call | solution.py:97
  16.9 1.5 collective-permute-start.2
  18.4 1.9 %collective-permute-start.3 = (bf16[3,160,128]{2,1,0:T(8,128)(2,1)}, bf16[3,160,128]{2,1,0:T(8,128)(2,1)S(1)}, u32[]{:S(2)}, u32[]{:S(2)}) collective-permute-start(bf16[3,160,128]{2,1,0:T(8,128)(2,1)} %get-tuple-element.77), channel_id=1, source_target_pairs={{0,12},{4,0},{8,4},{12,8},{16,28},{20,16},{24,20},{28,24},{32,44},... | collective-permute-start | bytes 368648 | tf_op jit(solution)/shard_map/ppermute | solution.py:30
  20.3 3.9 %collective-permute-done.1.q1 = bf16[3,160,128]{2,1,0:T(8,128)(2,1)S(1)} collective-permute-done((bf16[3,160,128]{2,1,0:T(8,128)(2,1)}, bf16[3,160,128]{2,1,0:T(8,128)(2,1)S(1)}, u32[]{:S(2)}, u32[]{:S(2)}) %collective-permute-start.1) | collective-permute-done | bytes 122912 | tf_op jit(solution)/shard_map/ppermute | solution.py:30
  24.2 3.3 %collective-permute-done.2.q2 = bf16[3,160,128]{2,1,0:T(8,128)(2,1)S(1)} collective-permute-done((bf16[3,160,128]{2,1,0:T(8,128)(2,1)}, bf16[3,160,128]{2,1,0:T(8,128)(2,1)S(1)}, u32[]{:S(2)}, u32[]{:S(2)}) %collective-permute-start.2) | collective-permute-done | bytes 122912 | tf_op jit(solution)/shard_map/ppermute | solution.py:30
  27.6 7.6 %all-to-all-start.1 = ((bf16[16,3,160,128]{3,2,1,0:T(8,128)(2,1)}), bf16[16,3,160,128]{3,2,1,0:T(8,128)(2,1)}, u32[]{:S(2)}, u32[]{:S(2)}) async-start(bf16[16,3,160,128]{3,2,1,0:T(8,128)(2,1)} %get-tuple-element.78), calls=%async_computation.1 | async-start | bytes 3932160 | tf_op jit(solution)/shard_map/all_to_all | solution.py:295
  35.2 2.1 %shard_map.126 = (bf16[160,640]{1,0:T(8,128)(2,1)}, bf16[160,640]{1,0:T(8,128)(2,1)}, bf16[160,640]{1,0:T(8,128)(2,1)}, bf16[160,640]{1,0:T(8,128)(2,1)}) custom-call(s32[1]{0:T(128)} %bitcast.z_ref, bf16[160,2560]{1,0:T(8,128)(2,1)} %bitcast.24), custom_call_target="tpu_custom_call" | custom-call | tf_op jit(solution)/shard_map/pallas_call | solution.py:97
  37.3 2.4 %collective-permute-start.10 = (bf16[160,640]{1,0:T(8,128)(2,1)}, bf16[160,640]{1,0:T(8,128)(2,1)}, u32[]{:S(2)}, u32[]{:S(2)}) collective-permute-start(bf16[160,640]{1,0:T(8,128)(2,1)} %get-tuple-element.83), channel_id=1, source_target_pairs={{0,196},{4,200},{8,204},{12,192},{16,212},{20,216},{24,220},{28,20... | collective-permute-start | bytes 614408 | tf_op jit(solution)/shard_map/ppermute | solution.py:64
  39.7 1.2 collective-permute-start.11
  41.8 1.5 collective-permute-start.7
  43.4 2.7 %collective-permute-start.8 = (bf16[2,640,128]{2,1,0:T(8,128)(2,1)S(1)}, bf16[2,640,128]{2,1,0:T(8,128)(2,1)}, u32[]{:S(2)}, u32[]{:S(2)}) collective-permute-start(bf16[2,640,128]{2,1,0:T(8,128)(2,1)S(1)} %pad_maximum_fusion.s0), channel_id=1, source_target_pairs={{0,32},{4,36},{8,40},{12,44},{16,48},{20,52},{24,56},{28,60},{32,0... | collective-permute-start | bytes 983048 | tf_op jit(solution)/shard_map/ppermute | solution.py:35
  46.0 1.5 collective-permute-start.9
  47.5 1.9 %fusion.2.gate_ref = f32[1,2560]{1,0:T(1,128)} fusion(f32[256,1]{0,1:T(1,128)S(1)} %bitcast.26, f32[1,256,2560]{2,1,0:T(8,128)S(1)} %copy-done), kind=kOutput, calls=%fused_computation.1 | convolution fusion | flops 7864320 | bytes 2632704 | tf_op jit(solution)/shard_map/dot_general | solution.py:298
  49.5 40.1 %all-to-all-done.1.r_ref = bf16[16,3,160,128]{3,2,1,0:T(8,128)(2,1)} async-done(((bf16[16,3,160,128]{3,2,1,0:T(8,128)(2,1)}), bf16[16,3,160,128]{3,2,1,0:T(8,128)(2,1)}, u32[]{:S(2)}, u32[]{:S(2)}) %all-to-all-start.1) | async-done | bytes 1966112 | tf_op jit(solution)/shard_map/all_to_all | solution.py:295
  89.6 9.5 %shard_map.124 = (bf16[640,128]{1,0:T(8,128)(2,1)}, bf16[640,128]{1,0:T(8,128)(2,1)}, bf16[640,128]{1,0:T(8,128)(2,1)}) custom-call(s32[1]{0:T(128)} %bitcast.1.x_ref, bf16[16,3,160,128]{3,2,1,0:T(8,128)(2,1)} %all-to-all-done.1.r_ref), custom_call_target="tpu_custom_call" | custom-call | tf_op jit(solution)/shard_map/pallas_call | solution.py:97
  99.1 2.2 %collective-permute-start.16 = (bf16[160,640]{1,0:T(8,128)(2,1)}, bf16[160,640]{1,0:T(8,128)(2,1)S(1)}, u32[]{:S(2)}, u32[]{:S(2)}) collective-permute-start(bf16[160,640]{1,0:T(8,128)(2,1)} %get-tuple-element.91), channel_id=1, source_target_pairs={{0,192},{4,196},{8,200},{12,204},{16,208},{20,212},{24,216},{28,22... | collective-permute-start | bytes 614408 | tf_op jit(solution)/shard_map/ppermute | solution.py:64
  102.2 1.7 collective-permute-start.4
  104.9 4.7 %shard_map.125.refs_4_ = bf16[640,128]{1,0:T(8,128)(2,1)} custom-call(bf16[3,160,128]{2,1,0:T(8,128)(2,1)} %get-tuple-element.74.q0, bf16[3,160,128]{2,1,0:T(8,128)(2,1)} %copy-done.7, bf16[3,160,128]{2,1,0:T(8,128)(2,1)} %copy-done.8, bf16[3,160,128]{2,1,0:T(8,128)(2,1)} %copy-done.9, bf16[2,640,128]{2,1,0:T(8,128)(2,1)} %copy-done.2, ...), custom_call_target="tpu_custom_call" | custom-call | tf_op jit(solution)/shard_map/pallas_call | solution.py:97
  109.6 4.8 %shard_map.123.refs_0_ = bf16[640,128]{1,0:T(8,128)(2,1)} custom-call(s32[1]{0:T(128)} %bitcast.1.x_ref, bf16[16,3,160,128]{3,2,1,0:T(8,128)(2,1)} %all-to-all-done.1.r_ref), custom_call_target="tpu_custom_call" | custom-call | tf_op jit(solution)/shard_map/pallas_call | solution.py:97
  115.8 2.3 %shard_map.127 = (bf16[160,640]{1,0:T(8,128)(2,1)}, bf16[160,640]{1,0:T(8,128)(2,1)}, bf16[160,640]{1,0:T(8,128)(2,1)}, bf16[160,640]{1,0:T(8,128)(2,1)}) custom-call(s32[2]{0:T(128)} %pad_add_fusion.place_ref, bf16[640,128]{1,0:T(8,128)(2,1)} %shard_map.123.refs_0_, bf16[640,128]{1,0:T(8,128)(2,1)} %copy-done.4, bf16[640,128]{1,0:T(8,128)(2,1)} %copy-done.3, ...), custom_call_target="tpu_custom_call" | custom-call | tf_op jit(solution)/shard_map/pallas_call | solution.py:97
  118.1 2.2 %collective-permute-start.13 = (bf16[160,640]{1,0:T(8,128)(2,1)}, bf16[160,640]{1,0:T(8,128)(2,1)S(1)}, u32[]{:S(2)}, u32[]{:S(2)}) collective-permute-start(bf16[160,640]{1,0:T(8,128)(2,1)} %get-tuple-element.87), channel_id=1, source_target_pairs={{0,76},{4,64},{8,68},{12,72},{16,92},{20,80},{24,84},{28,88},{32,1... | collective-permute-start | bytes 614408 | tf_op jit(solution)/shard_map/ppermute | solution.py:60
  121.4 1.5 collective-permute-start.15
  123.5 2.3 %shard_map.128 = f32[8,128]{1,0:T(8,128)} custom-call(s32[2]{0:T(128)} %pad_add_fusion.place_ref, bf16[640,128]{1,0:T(8,128)(2,1)} %shard_map.123.refs_0_, bf16[640,128]{1,0:T(8,128)(2,1)} %copy-done.4, bf16[640,128]{1,0:T(8,128)(2,1)} %copy-done.3, bf16[640,128]{1,0:T(8,128)(2,1)} %copy-done.5, bf16[640,128]{1,0:T(8,128)(2,1)} %shard_map.125.refs_4_, ...), custom_call_target="tpu_custom_call" | custom-call | tf_op jit(solution)/shard_map/pallas_call | solution.py:97
  125.9 1.8 %collective-permute-start.18 = (f32[8,128]{1,0:T(8,128)}, f32[8,128]{1,0:T(8,128)S(1)}, u32[]{:S(2)}, u32[]{:S(2)}) collective-permute-start(f32[8,128]{1,0:T(8,128)} %shard_map.128), channel_id=1, source_target_pairs={{0,64},{4,68},{8,72},{12,76},{16,80},{20,84},{24,88},{28,92},{32,9... | collective-permute-start | bytes 12296 | tf_op jit(solution)/shard_map/ppermute | solution.py:60
  127.7 7.3 %collective-permute-done.18 = f32[8,128]{1,0:T(8,128)S(1)} collective-permute-done((f32[8,128]{1,0:T(8,128)}, f32[8,128]{1,0:T(8,128)S(1)}, u32[]{:S(2)}, u32[]{:S(2)}) %collective-permute-start.18) | collective-permute-done | bytes 4128 | tf_op jit(solution)/shard_map/ppermute | solution.py:60
  135.6 30.0 %while.13 = (s32[]{:T(128)}, f32[4,2560]{1,0:T(4,128)}, f32[4,128]{1,0:T(4,128)S(1)}, s32[]{:T(128)}, s32[]{:T(128)}, /*index=5*/f32[8,128]{1,0:T(8,128)S(1)}, f32[4,128]{1,0:T(4,128)S(1)}, f32[]{:T(128)}, s32[]{:T(128)}) while((s32[]{:T(128)}, f32[4,2560]{1,0:T(4,128)}, f32[4,128]{1,0:T(4,128)S(1)}, s32[]{:T(128)}, s32[]{:T(128)}, ...), condition=%wide.region_1.2_spmd.clone, body=%wide.region_0.1_spmd.clone.sunk | while | flops 2 | bytes 1835677 | solution.py:341
  136.1 1.4 body.2
  137.5 15.0 %all-to-all-start = ((f32[64,8,128]{2,1,0:T(8,128)}), f32[64,8,128]{2,1,0:T(8,128)S(1)}, u32[]{:S(2)}, u32[]{:S(2)}) async-start(f32[64,8,128]{2,1,0:T(8,128)} %body.2), calls=%async_computation | async-start | bytes 524288 | tf_op jit(solution)/shard_map/while/body/all_to_all | solution.py:334
  152.5 10.6 %all-to-all-done.chan_ref = f32[64,8,128]{2,1,0:T(8,128)S(1)} async-done(((f32[64,8,128]{2,1,0:T(8,128)}), f32[64,8,128]{2,1,0:T(8,128)S(1)}, u32[]{:S(2)}, u32[]{:S(2)}) %all-to-all-start) | async-done | bytes 262176 | tf_op jit(solution)/shard_map/while/body/all_to_all | solution.py:334
  163.9 1.7 body.3
  166.4 2.3 %shard_map.129 = bf16[160,2560]{1,0:T(8,128)(2,1)} custom-call(s32[1]{0:T(128)} %bitcast.z_ref, bf16[160,640]{1,0:T(8,128)(2,1)} %copy-done.11, bf16[160,640]{1,0:T(8,128)(2,1)} %copy-done.12, bf16[160,640]{1,0:T(8,128)(2,1)} %copy-done.13, bf16[160,640]{1,0:T(8,128)(2,1)} %collective-permute-done.15.a3, f32[1,2560]{1,0:T(1,128)} %fusion.2.gate_ref), custom_call_target="tpu_custom_call" | custom-call | tf_op jit(solution)/shard_map/pallas_call | solution.py:97
  (80 shorter events, 13.0 us)
Async XLA Ops:
  0.6 46.9 %copy-start = (f32[1,256,2560]{2,1,0:T(8,128)S(1)}, f32[1,256,2560]{2,1,0:T(8,128)}, u32[]{:S(2)}) copy-start(f32[1,256,2560]{2,1,0:T(8,128)} %param.15) | copy-start | bytes 7864324
  0.6 10.0 %collective-permute-start = (f32[2,2560]{1,0:T(2,128)}, f32[2,2560]{1,0:T(2,128)S(1)}, u32[]{:S(2)}, u32[]{:S(2)}) collective-permute-start(f32[2,2560]{1,0:T(2,128)} %bitcast.30), channel_id=1, source_target_pairs={{64,0},{128,64},{192,128},{0,192},{65,1},{129,65},{193,129},{1,193... | collective-permute-start | bytes 61448 | tf_op jit(solution)/shard_map/ppermute | solution.py:276
  15.8 25.7 %copy-start.19 = (f32[256]{0:T(256)S(1)}, f32[256]{0:T(256)}, u32[]{:S(2)}) copy-start(f32[256]{0:T(256)} %constant.97.clone) | copy-start | bytes 3076
  15.8 25.8 %copy-start.17 = (f32[128]{0:T(128)S(1)}, f32[128]{0:T(128)}, u32[]{:S(2)}) copy-start(f32[128]{0:T(128)} %constant.96.clone) | copy-start | bytes 1540
  15.8 25.9 %copy-start.6 = (bf16[3,160,128]{2,1,0:T(8,128)(2,1)S(1)}, bf16[3,160,128]{2,1,0:T(8,128)(2,1)}, u32[]{:S(2)}) copy-start(bf16[3,160,128]{2,1,0:T(8,128)(2,1)} %get-tuple-element.74.q0) | copy-start | bytes 368644
  15.8 8.4 %collective-permute-start.1 = (bf16[3,160,128]{2,1,0:T(8,128)(2,1)}, bf16[3,160,128]{2,1,0:T(8,128)(2,1)S(1)}, u32[]{:S(2)}, u32[]{:S(2)}) collective-permute-start(bf16[3,160,128]{2,1,0:T(8,128)(2,1)} %get-tuple-element.75), channel_id=1, source_target_pairs={{0,4},{4,8},{8,12},{12,0},{16,20},{20,24},{24,28},{28,16},{32,36},... | collective-permute-start | bytes 368648 | tf_op jit(solution)/shard_map/ppermute | solution.py:30
  16.9 10.7 %collective-permute-start.2 = (bf16[3,160,128]{2,1,0:T(8,128)(2,1)}, bf16[3,160,128]{2,1,0:T(8,128)(2,1)S(1)}, u32[]{:S(2)}, u32[]{:S(2)}) collective-permute-start(bf16[3,160,128]{2,1,0:T(8,128)(2,1)} %get-tuple-element.76), channel_id=1, source_target_pairs={{0,8},{4,12},{8,0},{12,4},{16,24},{20,28},{24,16},{28,20},{32,40},... | collective-permute-start | bytes 368648 | tf_op jit(solution)/shard_map/ppermute | solution.py:30
  18.4 9.2 %collective-permute-start.3 = (bf16[3,160,128]{2,1,0:T(8,128)(2,1)}, bf16[3,160,128]{2,1,0:T(8,128)(2,1)S(1)}, u32[]{:S(2)}, u32[]{:S(2)}) collective-permute-start(bf16[3,160,128]{2,1,0:T(8,128)(2,1)} %get-tuple-element.77), channel_id=1, source_target_pairs={{0,12},{4,0},{8,4},{12,8},{16,28},{20,16},{24,20},{28,24},{32,44},... | collective-permute-start | bytes 368648 | tf_op jit(solution)/shard_map/ppermute | solution.py:30
  24.2 17.5 %copy-start.7 = (bf16[3,160,128]{2,1,0:T(8,128)(2,1)}, bf16[3,160,128]{2,1,0:T(8,128)(2,1)S(1)}, u32[]{:S(2)}) copy-start(bf16[3,160,128]{2,1,0:T(8,128)(2,1)S(1)} %collective-permute-done.1.q1) | copy-start | bytes 368644
  27.6 14.2 %copy-start.8 = (bf16[3,160,128]{2,1,0:T(8,128)(2,1)}, bf16[3,160,128]{2,1,0:T(8,128)(2,1)S(1)}, u32[]{:S(2)}) copy-start(bf16[3,160,128]{2,1,0:T(8,128)(2,1)S(1)} %collective-permute-done.2.q2) | copy-start | bytes 368644
  27.6 14.2 %copy-start.9 = (bf16[3,160,128]{2,1,0:T(8,128)(2,1)}, bf16[3,160,128]{2,1,0:T(8,128)(2,1)S(1)}, u32[]{:S(2)}) copy-start(bf16[3,160,128]{2,1,0:T(8,128)(2,1)S(1)} %collective-permute-done.3.q3) | copy-start | bytes 368644
  27.6 62.0 %all-to-all-start.1 = ((bf16[16,3,160,128]{3,2,1,0:T(8,128)(2,1)}), bf16[16,3,160,128]{3,2,1,0:T(8,128)(2,1)}, u32[]{:S(2)}, u32[]{:S(2)}) async-start(bf16[16,3,160,128]{3,2,1,0:T(8,128)(2,1)} %get-tuple-element.78), calls=%async_computation.1 | async-start | bytes 3932160 | tf_op jit(solution)/shard_map/all_to_all | solution.py:295
  37.3 61.8 %collective-permute-start.10 = (bf16[160,640]{1,0:T(8,128)(2,1)}, bf16[160,640]{1,0:T(8,128)(2,1)}, u32[]{:S(2)}, u32[]{:S(2)}) collective-permute-start(bf16[160,640]{1,0:T(8,128)(2,1)} %get-tuple-element.83), channel_id=1, source_target_pairs={{0,196},{4,200},{8,204},{12,192},{16,212},{20,216},{24,220},{28,20... | collective-permute-start | bytes 614408 | tf_op jit(solution)/shard_map/ppermute | solution.py:64
  39.7 61.7 %collective-permute-start.11 = (bf16[160,640]{1,0:T(8,128)(2,1)}, bf16[160,640]{1,0:T(8,128)(2,1)}, u32[]{:S(2)}, u32[]{:S(2)}) collective-permute-start(bf16[160,640]{1,0:T(8,128)(2,1)} %get-tuple-element.84), channel_id=1, source_target_pairs={{0,200},{4,204},{8,192},{12,196},{16,216},{20,220},{24,208},{28,21... | collective-permute-start | bytes 614408 | tf_op jit(solution)/shard_map/ppermute | solution.py:64
  41.8 62.5 %copy-start.18 = (bf16[160,640]{1,0:T(8,128)(2,1)S(1)}, bf16[160,640]{1,0:T(8,128)(2,1)}, u32[]{:S(2)}) copy-start(bf16[160,640]{1,0:T(8,128)(2,1)} %get-tuple-element.93) | copy-start | bytes 614404
  41.8 63.1 %copy-start.2 = (bf16[2,640,128]{2,1,0:T(8,128)(2,1)}, bf16[2,640,128]{2,1,0:T(8,128)(2,1)S(1)}, u32[]{:S(2)}) copy-start(bf16[2,640,128]{2,1,0:T(8,128)(2,1)S(1)} %pad_maximum_fusion.s0) | copy-start | bytes 983044
  41.8 60.4 %collective-permute-start.7 = (bf16[2,640,128]{2,1,0:T(8,128)(2,1)S(1)}, bf16[2,640,128]{2,1,0:T(8,128)(2,1)S(1)}, u32[]{:S(2)}, u32[]{:S(2)}) collective-permute-start(bf16[2,640,128]{2,1,0:T(8,128)(2,1)S(1)} %pad_maximum_fusion.s0), channel_id=1, source_target_pairs={{0,16},{4,20},{8,24},{12,28},{16,32},{20,36},{24,40},{28,44},{32,4... | collective-permute-start | bytes 983048 | tf_op jit(solution)/shard_map/ppermute | solution.py:35
  43.4 60.5 %collective-permute-start.8 = (bf16[2,640,128]{2,1,0:T(8,128)(2,1)S(1)}, bf16[2,640,128]{2,1,0:T(8,128)(2,1)}, u32[]{:S(2)}, u32[]{:S(2)}) collective-permute-start(bf16[2,640,128]{2,1,0:T(8,128)(2,1)S(1)} %pad_maximum_fusion.s0), channel_id=1, source_target_pairs={{0,32},{4,36},{8,40},{12,44},{16,48},{20,52},{24,56},{28,60},{32,0... | collective-permute-start | bytes 983048 | tf_op jit(solution)/shard_map/ppermute | solution.py:35
  46.0 58.2 %collective-permute-start.9 = (bf16[2,640,128]{2,1,0:T(8,128)(2,1)S(1)}, bf16[2,640,128]{2,1,0:T(8,128)(2,1)}, u32[]{:S(2)}, u32[]{:S(2)}) collective-permute-start(bf16[2,640,128]{2,1,0:T(8,128)(2,1)S(1)} %pad_maximum_fusion.s0), channel_id=1, source_target_pairs={{0,48},{4,52},{8,56},{12,60},{16,0},{20,4},{24,8},{28,12},{32,16},... | collective-permute-start | bytes 983048 | tf_op jit(solution)/shard_map/ppermute | solution.py:35
  99.1 22.2 %collective-permute-start.16 = (bf16[160,640]{1,0:T(8,128)(2,1)}, bf16[160,640]{1,0:T(8,128)(2,1)S(1)}, u32[]{:S(2)}, u32[]{:S(2)}) collective-permute-start(bf16[160,640]{1,0:T(8,128)(2,1)} %get-tuple-element.91), channel_id=1, source_target_pairs={{0,192},{4,196},{8,200},{12,204},{16,208},{20,212},{24,216},{28,22... | collective-permute-start | bytes 614408 | tf_op jit(solution)/shard_map/ppermute | solution.py:64
  101.3 13.1 %collective-permute-start.5 = (bf16[640,128]{1,0:T(8,128)(2,1)}, bf16[640,128]{1,0:T(8,128)(2,1)S(1)}, u32[]{:S(2)}, u32[]{:S(2)}) collective-permute-start(bf16[640,128]{1,0:T(8,128)(2,1)} %get-tuple-element.81), channel_id=1, source_target_pairs={{0,32},{4,36},{8,40},{12,44},{16,48},{20,52},{24,56},{28,60},{32,0... | collective-permute-start | bytes 491528 | tf_op jit(solution)/shard_map/ppermute | solution.py:35
  102.2 2.7 %copy-start.10 = (bf16[2,640,128]{2,1,0:T(8,128)(2,1)}, bf16[2,640,128]{2,1,0:T(8,128)(2,1)S(1)}, u32[]{:S(2)}) copy-start(bf16[2,640,128]{2,1,0:T(8,128)(2,1)S(1)} %collective-permute-done.7.s1) | copy-start | bytes 983044
  102.2 12.2 %collective-permute-start.4 = (bf16[640,128]{1,0:T(8,128)(2,1)}, bf16[640,128]{1,0:T(8,128)(2,1)S(1)}, u32[]{:S(2)}, u32[]{:S(2)}) collective-permute-start(bf16[640,128]{1,0:T(8,128)(2,1)} %get-tuple-element.80), channel_id=1, source_target_pairs={{0,48},{4,52},{8,56},{12,60},{16,0},{20,4},{24,8},{28,12},{32,16},... | collective-permute-start | bytes 491528 | tf_op jit(solution)/shard_map/ppermute | solution.py:35
  103.9 10.5 %collective-permute-start.6 = (bf16[640,128]{1,0:T(8,128)(2,1)}, bf16[640,128]{1,0:T(8,128)(2,1)S(1)}, u32[]{:S(2)}, u32[]{:S(2)}) collective-permute-start(bf16[640,128]{1,0:T(8,128)(2,1)} %get-tuple-element.82), channel_id=1, source_target_pairs={{0,16},{4,20},{8,24},{12,28},{16,32},{20,36},{24,40},{28,44},{32,4... | collective-permute-start | bytes 491528 | tf_op jit(solution)/shard_map/ppermute | solution.py:35
  104.3 18.6 %collective-permute-start.17 = (bf16[160,640]{1,0:T(8,128)(2,1)S(1)}, bf16[160,640]{1,0:T(8,128)(2,1)S(1)}, u32[]{:S(2)}, u32[]{:S(2)}) collective-permute-start(bf16[160,640]{1,0:T(8,128)(2,1)S(1)} %copy-done.18), channel_id=1, source_target_pairs={{0,204},{4,192},{8,196},{12,200},{16,220},{20,208},{24,212},{28,21... | collective-permute-start | bytes 614408 | tf_op jit(solution)/shard_map/ppermute | solution.py:64
  118.1 47.4 %collective-permute-start.12 = (bf16[160,640]{1,0:T(8,128)(2,1)}, bf16[160,640]{1,0:T(8,128)(2,1)S(1)}, u32[]{:S(2)}, u32[]{:S(2)}) collective-permute-start(bf16[160,640]{1,0:T(8,128)(2,1)} %get-tuple-element.86), channel_id=1, source_target_pairs={{0,64},{4,68},{8,72},{12,76},{16,80},{20,84},{24,88},{28,92},{32,9... | collective-permute-start | bytes 614408 | tf_op jit(solution)/shard_map/ppermute | solution.py:60
  118.1 47.4 %collective-permute-start.13 = (bf16[160,640]{1,0:T(8,128)(2,1)}, bf16[160,640]{1,0:T(8,128)(2,1)S(1)}, u32[]{:S(2)}, u32[]{:S(2)}) collective-permute-start(bf16[160,640]{1,0:T(8,128)(2,1)} %get-tuple-element.87), channel_id=1, source_target_pairs={{0,76},{4,64},{8,68},{12,72},{16,92},{20,80},{24,84},{28,88},{32,1... | collective-permute-start | bytes 614408 | tf_op jit(solution)/shard_map/ppermute | solution.py:60
  120.3 45.2 %collective-permute-start.14 = (bf16[160,640]{1,0:T(8,128)(2,1)}, bf16[160,640]{1,0:T(8,128)(2,1)S(1)}, u32[]{:S(2)}, u32[]{:S(2)}) collective-permute-start(bf16[160,640]{1,0:T(8,128)(2,1)} %get-tuple-element.88), channel_id=1, source_target_pairs={{0,72},{4,76},{8,64},{12,68},{16,88},{20,92},{24,80},{28,84},{32,1... | collective-permute-start | bytes 614408 | tf_op jit(solution)/shard_map/ppermute | solution.py:60
  121.4 1.5 copy-start.14
  121.4 44.2 %collective-permute-start.15 = (bf16[160,640]{1,0:T(8,128)(2,1)}, bf16[160,640]{1,0:T(8,128)(2,1)}, u32[]{:S(2)}, u32[]{:S(2)}) collective-permute-start(bf16[160,640]{1,0:T(8,128)(2,1)} %get-tuple-element.89), channel_id=1, source_target_pairs={{0,68},{4,72},{8,76},{12,64},{16,84},{20,88},{24,92},{28,80},{32,1... | collective-permute-start | bytes 614408 | tf_op jit(solution)/shard_map/ppermute | solution.py:60
  125.9 9.1 %collective-permute-start.18 = (f32[8,128]{1,0:T(8,128)}, f32[8,128]{1,0:T(8,128)S(1)}, u32[]{:S(2)}, u32[]{:S(2)}) collective-permute-start(f32[8,128]{1,0:T(8,128)} %shard_map.128), channel_id=1, source_target_pairs={{0,64},{4,68},{8,72},{12,76},{16,80},{20,84},{24,88},{28,92},{32,9... | collective-permute-start | bytes 12296 | tf_op jit(solution)/shard_map/ppermute | solution.py:60
  137.5 25.7 %all-to-all-start = ((f32[64,8,128]{2,1,0:T(8,128)}), f32[64,8,128]{2,1,0:T(8,128)S(1)}, u32[]{:S(2)}, u32[]{:S(2)}) async-start(f32[64,8,128]{2,1,0:T(8,128)} %body.2), calls=%async_computation | async-start | bytes 524288 | tf_op jit(solution)/shard_map/while/body/all_to_all | solution.py:334
  (9 other events, 6.3 us)

commit v8 on v1

--- a/solution.py
+++ b/solution.py
@@ -335,9 +335,8 @@
         return (grad, before)
 
     zeros = shape((rows, WIDTH), jnp.float32)
-    turns = jnp.where(step < 1000, 1, 2)
     start = (jnp.zeros((rows, WIDTH), jnp.float32), jnp.zeros((rows, HEAD_DIM), jnp.float32))
-    grad, _ = lax.fori_loop(0, turns, gradient, start)
+    grad, _ = gradient(0, start)
     grad = lax.ppermute(grad, "segment", [(i, (i + 1) % SIDE) for i in range(SIDE)])
 
     attn_out = call(

time: 162 us -> 168 us (1.037)
  starting transfers between devices: 48.8 us -> 56.2 us
  waiting for transfers between devices: 69.3 us -> 63.6 us
  Pallas kernels: 32.5 us -> 34.4 us
    ppermute x4, waiting for transfers between devices: 0.01 us -> 14.2 us  [home(): return lax.ppermute(value, ('segment', 'ctx'), section_pairs(1, by))]
    all_to_all x1, waiting for transfers between devices: 13 us -> 1.15 us  [gradient(): chans = lax.all_to_all(chans, ('ctx', 'dp'), 0, 0)]
    ppermute x1, waiting for transfers between devices: 7.75 us -> 0.01 us  [local(): lax.ppermute(grad, 'segment', [(i, (i + 1) % SIDE) for i in range(SIDE)])]
    ppermute x4, starting transfers between devices: 5.54 us -> 9.62 us  [away(): return lax.ppermute(value, ('segment', 'ctx'), section_pairs(SIDE - 1, by))]
    ppermute x4, starting transfers between devices: 4.53 us -> 7.4 us  [home(): return lax.ppermute(value, ('segment', 'ctx'), section_pairs(1, by))]
    all_to_all x1, waiting for transfers between devices: 41.1 us -> 38.4 us  [local(): main = lax.all_to_all(after(main, shared_z), 'ctx', 0, 0)]
    ppermute x4, waiting for transfers between devices: 0.01 us -> 2.44 us  [away(): return lax.ppermute(value, ('segment', 'ctx'), section_pairs(SIDE - 1, by))]
  transfers between devices with their start and end apart: 21 -> 21, of which waited for: 5 -> 7; matrix products, arithmetic and copies ran while one was open for 4% -> 4% of each run, Pallas kernels for 16% -> 16%
where the time goes in v8:
time: 168 us; the launch traced here: 167 us
  waiting for transfers between devices  63.6 us (38%)
  starting transfers between devices  56.2 us (33%)
  Pallas kernels  34.4 us (20%)
  local copies, waits for them, and re-layouts  4.85 us (3%)
  other arithmetic  4.03 us (2%)
  matrix products  1.94 us (1%)
  between operations  1.69 us (1%)
    all_to_all x1, waiting for transfers between devices, local(): main = lax.all_to_all(after(main, shared_z), 'ctx', 0, 0)  38.4 us
    pallas_call x8, Pallas kernels, call(): pl.pallas_call(kernel, grid=grid, out_shape=out_shape, in_specs=specs, ou...  31.9 us
    ppermute x4, waiting for transfers between devices, home(): return lax.ppermute(value, ('segment', 'ctx'), section_pairs(1, by))  14.2 us
    all_to_all x1, starting transfers between devices, gradient(): chans = lax.all_to_all(chans, ('ctx', 'dp'), 0, 0)  11.5 us
    ppermute x4, starting transfers between devices, away(): return lax.ppermute(value, ('segment', 'ctx'), section_pairs(SIDE - 1, by))  9.62 us
    ppermute x6, starting transfers between devices, along_x(): return lax.ppermute(value, 'ctx', pairs)  8.91 us
    all_to_all x1, starting transfers between devices, local(): main = lax.all_to_all(after(main, shared_z), 'ctx', 0, 0)  7.57 us
    ppermute x4, starting transfers between devices, home(): return lax.ppermute(value, ('segment', 'ctx'), section_pairs(1, by))  7.4 us
  transfers between devices with their start and end apart: 21, of which 7 were waited for; matrix products, arithmetic and copies ran while one was open for 4% of the time, Pallas kernels for 16%

profile of v8, /device:TPU:8, one launch (start us, length us, event | category | flops | bytes accessed | tf_op | source)
XLA Modules:
  0.0 166.7 jit_solution(4179510493253853913)
XLA Ops:
  2.2 6.7 %collective-permute-start = (f32[3,2560]{1,0:T(4,128)S(1)}, f32[3,2560]{1,0:T(4,128)S(1)}, u32[]{:S(2)}, u32[]{:S(2)}) collective-permute-start(f32[3,2560]{1,0:T(4,128)S(1)} %concatenate.19), channel_id=1, source_target_pairs={{64,0},{128,64},{192,128},{0,192},{65,1},{129,65},{193,129},{1,193... | collective-permute-start | bytes 92168 | tf_op jit(solution)/shard_map/ppermute | solution.py:274
  10.3 1.1 fusion.4
  12.8 4.5 %shard_map.122 = (bf16[16,3,160,128]{3,2,1,0:T(8,128)(2,1)}, bf16[3,160,128]{2,1,0:T(8,128)(2,1)}, bf16[3,160,128]{2,1,0:T(8,128)(2,1)}, bf16[3,160,128]{2,1,0:T(8,128)(2,1)}, bf16[3,160,128]{2,1,0:T(8,128)(2,1)}) custom-call(s32[1]{0:T(128)} %bitcast.z_ref, bf16[3,160,2560]{2,1,0:T(8,128)(2,1)} %bitcast.19, f32[3,2560]{1,0:T(4,128)} %copy-done.17, ...), custom_call_target="tpu_custom_call" | custom-call | tf_op jit(solution)/shard_map/pallas_call | solution.py:97
  17.4 1.1 collective-permute-start.1
  18.4 1.5 collective-permute-start.2
  19.9 1.9 %collective-permute-start.3 = (bf16[3,160,128]{2,1,0:T(8,128)(2,1)}, bf16[3,160,128]{2,1,0:T(8,128)(2,1)S(1)}, u32[]{:S(2)}, u32[]{:S(2)}) collective-permute-start(bf16[3,160,128]{2,1,0:T(8,128)(2,1)} %get-tuple-element.35), channel_id=1, source_target_pairs={{0,12},{4,0},{8,4},{12,8},{16,28},{20,16},{24,20},{28,24},{32,44},... | collective-permute-start | bytes 368648 | tf_op jit(solution)/shard_map/ppermute | solution.py:30
  21.8 3.9 %collective-permute-done.1.q1 = bf16[3,160,128]{2,1,0:T(8,128)(2,1)S(1)} collective-permute-done((bf16[3,160,128]{2,1,0:T(8,128)(2,1)}, bf16[3,160,128]{2,1,0:T(8,128)(2,1)S(1)}, u32[]{:S(2)}, u32[]{:S(2)}) %collective-permute-start.1) | collective-permute-done | bytes 122912 | tf_op jit(solution)/shard_map/ppermute | solution.py:30
  25.8 3.4 %collective-permute-done.2.q2 = bf16[3,160,128]{2,1,0:T(8,128)(2,1)S(1)} collective-permute-done((bf16[3,160,128]{2,1,0:T(8,128)(2,1)}, bf16[3,160,128]{2,1,0:T(8,128)(2,1)S(1)}, u32[]{:S(2)}, u32[]{:S(2)}) %collective-permute-start.2) | collective-permute-done | bytes 122912 | tf_op jit(solution)/shard_map/ppermute | solution.py:30
  29.1 7.6 %all-to-all-start = ((bf16[16,3,160,128]{3,2,1,0:T(8,128)(2,1)}), bf16[16,3,160,128]{3,2,1,0:T(8,128)(2,1)}, u32[]{:S(2)}, u32[]{:S(2)}) async-start(bf16[16,3,160,128]{3,2,1,0:T(8,128)(2,1)} %get-tuple-element.36), calls=%async_computation | async-start | bytes 3932160 | tf_op jit(solution)/shard_map/all_to_all | solution.py:293
  37.0 1.9 %collective-permute-start.7 = (bf16[2,640,128]{2,1,0:T(8,128)(2,1)S(1)}, bf16[2,640,128]{2,1,0:T(8,128)(2,1)}, u32[]{:S(2)}, u32[]{:S(2)}) collective-permute-start(bf16[2,640,128]{2,1,0:T(8,128)(2,1)S(1)} %pad_maximum_fusion.s0), channel_id=1, source_target_pairs={{0,16},{4,20},{8,24},{12,28},{16,32},{20,36},{24,40},{28,44},{32,4... | collective-permute-start | bytes 983048 | tf_op jit(solution)/shard_map/ppermute | solution.py:35
  38.9 2.7 %collective-permute-start.8 = (bf16[2,640,128]{2,1,0:T(8,128)(2,1)S(1)}, bf16[2,640,128]{2,1,0:T(8,128)(2,1)}, u32[]{:S(2)}, u32[]{:S(2)}) collective-permute-start(bf16[2,640,128]{2,1,0:T(8,128)(2,1)S(1)} %pad_maximum_fusion.s0), channel_id=1, source_target_pairs={{0,32},{4,36},{8,40},{12,44},{16,48},{20,52},{24,56},{28,60},{32,0... | collective-permute-start | bytes 983048 | tf_op jit(solution)/shard_map/ppermute | solution.py:35
  41.6 1.5 collective-permute-start.9
  43.1 1.9 %fusion.gate_ref = f32[1,2560]{1,0:T(1,128)} fusion(f32[256,1]{0,1:T(1,128)S(1)} %bitcast.24, f32[1,256,2560]{2,1,0:T(8,128)S(1)} %copy-done), kind=kOutput, calls=%fused_computation | convolution fusion | flops 7864320 | bytes 2632704 | tf_op jit(solution)/shard_map/dot_general | solution.py:296
  45.0 38.4 %all-to-all-done.r_ref = bf16[16,3,160,128]{3,2,1,0:T(8,128)(2,1)} async-done(((bf16[16,3,160,128]{3,2,1,0:T(8,128)(2,1)}), bf16[16,3,160,128]{3,2,1,0:T(8,128)(2,1)}, u32[]{:S(2)}, u32[]{:S(2)}) %all-to-all-start) | async-done | bytes 1966112 | tf_op jit(solution)/shard_map/all_to_all | solution.py:293
  84.1 9.5 %shard_map.124 = (bf16[640,128]{1,0:T(8,128)(2,1)}, bf16[640,128]{1,0:T(8,128)(2,1)}, bf16[640,128]{1,0:T(8,128)(2,1)}) custom-call(s32[1]{0:T(128)} %bitcast.1.x_ref, bf16[16,3,160,128]{3,2,1,0:T(8,128)(2,1)} %all-to-all-done.r_ref), custom_call_target="tpu_custom_call" | custom-call | tf_op jit(solution)/shard_map/pallas_call | solution.py:97
  95.0 2.1 %shard_map.126 = (bf16[160,640]{1,0:T(8,128)(2,1)}, bf16[160,640]{1,0:T(8,128)(2,1)}, bf16[160,640]{1,0:T(8,128)(2,1)}, bf16[160,640]{1,0:T(8,128)(2,1)}) custom-call(s32[1]{0:T(128)} %bitcast.z_ref, bf16[160,2560]{1,0:T(8,128)(2,1)} %bitcast.21), custom_call_target="tpu_custom_call" | custom-call | tf_op jit(solution)/shard_map/pallas_call | solution.py:97
  97.1 4.8 %collective-permute-start.10 = (bf16[160,640]{1,0:T(8,128)(2,1)}, bf16[160,640]{1,0:T(8,128)(2,1)S(1)}, u32[]{:S(2)}, u32[]{:S(2)}) collective-permute-start(bf16[160,640]{1,0:T(8,128)(2,1)} %get-tuple-element.41), channel_id=1, source_target_pairs={{0,196},{4,200},{8,204},{12,192},{16,212},{20,216},{24,220},{28,20... | collective-permute-start | bytes 614408 | tf_op jit(solution)/shard_map/ppermute | solution.py:64
  102.8 3.2 %collective-permute-start.16 = (bf16[160,640]{1,0:T(8,128)(2,1)}, bf16[160,640]{1,0:T(8,128)(2,1)S(1)}, u32[]{:S(2)}, u32[]{:S(2)}) collective-permute-start(bf16[160,640]{1,0:T(8,128)(2,1)} %get-tuple-element.57), channel_id=1, source_target_pairs={{0,192},{4,196},{8,200},{12,204},{16,208},{20,212},{24,216},{28,22... | collective-permute-start | bytes 614408 | tf_op jit(solution)/shard_map/ppermute | solution.py:64
  106.8 1.4 collective-permute-start.6
  108.9 4.7 %shard_map.125.refs_4_ = bf16[640,128]{1,0:T(8,128)(2,1)} custom-call(bf16[3,160,128]{2,1,0:T(8,128)(2,1)} %get-tuple-element.32.q0, bf16[3,160,128]{2,1,0:T(8,128)(2,1)} %copy-done.7, bf16[3,160,128]{2,1,0:T(8,128)(2,1)} %copy-done.8, bf16[3,160,128]{2,1,0:T(8,128)(2,1)} %copy-done.9, bf16[2,640,128]{2,1,0:T(8,128)(2,1)} %copy-done.1, ...), custom_call_target="tpu_custom_call" | custom-call | tf_op jit(solution)/shard_map/pallas_call | solution.py:97
  113.6 4.8 %shard_map.123.refs_0_ = bf16[640,128]{1,0:T(8,128)(2,1)} custom-call(s32[1]{0:T(128)} %bitcast.1.x_ref, bf16[16,3,160,128]{3,2,1,0:T(8,128)(2,1)} %all-to-all-done.r_ref), custom_call_target="tpu_custom_call" | custom-call | tf_op jit(solution)/shard_map/pallas_call | solution.py:97
  118.4 2.4 %collective-permute-done.17.refs_8_ = bf16[160,640]{1,0:T(8,128)(2,1)S(1)} collective-permute-done((bf16[160,640]{1,0:T(8,128)(2,1)}, bf16[160,640]{1,0:T(8,128)(2,1)S(1)}, u32[]{:S(2)}, u32[]{:S(2)}) %collective-permute-start.17) | collective-permute-done | bytes 204832 | tf_op jit(solution)/shard_map/ppermute | solution.py:64
  121.6 2.5 %shard_map.129 = f32[64,8,128]{2,1,0:T(8,128)} custom-call(s32[2]{0:T(128)} %pad_add_fusion.place_ref, f32[3,2560]{1,0:T(4,128)} %copy-done.17, bf16[640,128]{1,0:T(8,128)(2,1)} %shard_map.123.refs_0_, bf16[640,128]{1,0:T(8,128)(2,1)} %copy-done.3, bf16[640,128]{1,0:T(8,128)(2,1)} %copy-done.4, bf16[640,128]{1,0:T(8,128)(2,1)} %copy-done.5, ...), custom_call_target="tpu_custom_call" | custom-call | tf_op jit(solution)/shard_map/pallas_call | solution.py:324
  124.1 11.5 %all-to-all-start.1 = ((f32[64,8,128]{2,1,0:T(8,128)}), f32[64,8,128]{2,1,0:T(8,128)S(1)}, u32[]{:S(2)}, u32[]{:S(2)}) async-start(f32[64,8,128]{2,1,0:T(8,128)} %shard_map.129), calls=%async_computation.1 | async-start | bytes 524288 | tf_op jit(solution)/shard_map/all_to_all | solution.py:333
  135.6 2.3 %shard_map.127 = (bf16[160,640]{1,0:T(8,128)(2,1)}, bf16[160,640]{1,0:T(8,128)(2,1)}, bf16[160,640]{1,0:T(8,128)(2,1)}, bf16[160,640]{1,0:T(8,128)(2,1)}) custom-call(s32[2]{0:T(128)} %pad_add_fusion.place_ref, bf16[640,128]{1,0:T(8,128)(2,1)} %shard_map.123.refs_0_, bf16[640,128]{1,0:T(8,128)(2,1)} %copy-done.3, bf16[640,128]{1,0:T(8,128)(2,1)} %copy-done.4, ...), custom_call_target="tpu_custom_call" | custom-call | tf_op jit(solution)/shard_map/pallas_call | solution.py:97
  137.9 5.6 %collective-permute-start.13 = (bf16[160,640]{1,0:T(8,128)(2,1)}, bf16[160,640]{1,0:T(8,128)(2,1)S(1)}, u32[]{:S(2)}, u32[]{:S(2)}) collective-permute-start(bf16[160,640]{1,0:T(8,128)(2,1)} %get-tuple-element.45), channel_id=1, source_target_pairs={{0,76},{4,64},{8,68},{12,72},{16,92},{20,80},{24,84},{28,88},{32,1... | collective-permute-start | bytes 614408 | tf_op jit(solution)/shard_map/ppermute | solution.py:60
  143.7 1.6 collective-permute-start.15
  145.3 1.1 all-to-all-done.1.chan_ref
  147.2 1.7 %shard_map.130 = f32[4,2560]{1,0:T(4,128)} custom-call(s32[1]{0:T(128)} %bitcast.13.index_ref, f32[4,128]{1,0:T(4,128)} %broadcast_in_dim.85.freq_ref, f32[4,128]{1,0:T(4,128)} %broadcast_in_dim.88.before_ref, f32[64,8,128]{2,1,0:T(8,128)} %copy-done.2), custom_call_target="tpu_custom_call" | custom-call | tf_op jit(solution)/shard_map/pallas_call | solution.py:97
  148.9 11.8 %collective-permute-done.13.a1 = bf16[160,640]{1,0:T(8,128)(2,1)S(1)} collective-permute-done((bf16[160,640]{1,0:T(8,128)(2,1)}, bf16[160,640]{1,0:T(8,128)(2,1)S(1)}, u32[]{:S(2)}, u32[]{:S(2)}) %collective-permute-start.13) | collective-permute-done | bytes 204832 | tf_op jit(solution)/shard_map/ppermute | solution.py:60
  160.7 2.4 %collective-permute-done.14.a2 = bf16[160,640]{1,0:T(8,128)(2,1)S(1)} collective-permute-done((bf16[160,640]{1,0:T(8,128)(2,1)}, bf16[160,640]{1,0:T(8,128)(2,1)S(1)}, u32[]{:S(2)}, u32[]{:S(2)}) %collective-permute-start.14) | collective-permute-done | bytes 204832 | tf_op jit(solution)/shard_map/ppermute | solution.py:60
  163.8 2.3 %shard_map.128 = bf16[160,2560]{1,0:T(8,128)(2,1)} custom-call(s32[1]{0:T(128)} %bitcast.z_ref, bf16[160,640]{1,0:T(8,128)(2,1)} %copy-done.10, bf16[160,640]{1,0:T(8,128)(2,1)} %copy-done.11, bf16[160,640]{1,0:T(8,128)(2,1)} %copy-done.12, bf16[160,640]{1,0:T(8,128)(2,1)} %collective-permute-done.15.a3, f32[1,2560]{1,0:T(1,128)} %fusion.gate_ref), custom_call_target="tpu_custom_call" | custom-call | tf_op jit(solution)/shard_map/pallas_call | solution.py:97
  (78 shorter events, 11.0 us)
Async XLA Ops:
  0.6 42.5 %copy-start = (f32[1,256,2560]{2,1,0:T(8,128)S(1)}, f32[1,256,2560]{2,1,0:T(8,128)}, u32[]{:S(2)}) copy-start(f32[1,256,2560]{2,1,0:T(8,128)} %param.13) | copy-start | bytes 7864324
  2.2 10.0 %collective-permute-start = (f32[3,2560]{1,0:T(4,128)S(1)}, f32[3,2560]{1,0:T(4,128)S(1)}, u32[]{:S(2)}, u32[]{:S(2)}) collective-permute-start(f32[3,2560]{1,0:T(4,128)S(1)} %concatenate.19), channel_id=1, source_target_pairs={{64,0},{128,64},{192,128},{0,192},{65,1},{129,65},{193,129},{1,193... | collective-permute-start | bytes 92168 | tf_op jit(solution)/shard_map/ppermute | solution.py:274
  17.3 19.4 %copy-start.19 = (f32[256]{0:T(256)S(1)}, f32[256]{0:T(256)}, u32[]{:S(2)}) copy-start(f32[256]{0:T(256)} %constant.85.clone) | copy-start | bytes 3076
  17.3 19.5 %copy-start.18 = (f32[128]{0:T(128)S(1)}, f32[128]{0:T(128)}, u32[]{:S(2)}) copy-start(f32[128]{0:T(128)} %constant.84.clone) | copy-start | bytes 1540
  17.3 19.5 %copy-start.6 = (bf16[3,160,128]{2,1,0:T(8,128)(2,1)S(1)}, bf16[3,160,128]{2,1,0:T(8,128)(2,1)}, u32[]{:S(2)}) copy-start(bf16[3,160,128]{2,1,0:T(8,128)(2,1)} %get-tuple-element.32.q0) | copy-start | bytes 368644
  17.4 8.4 %collective-permute-start.1 = (bf16[3,160,128]{2,1,0:T(8,128)(2,1)}, bf16[3,160,128]{2,1,0:T(8,128)(2,1)S(1)}, u32[]{:S(2)}, u32[]{:S(2)}) collective-permute-start(bf16[3,160,128]{2,1,0:T(8,128)(2,1)} %get-tuple-element.33), channel_id=1, source_target_pairs={{0,4},{4,8},{8,12},{12,0},{16,20},{20,24},{24,28},{28,16},{32,36},... | collective-permute-start | bytes 368648 | tf_op jit(solution)/shard_map/ppermute | solution.py:30
  18.4 10.7 %collective-permute-start.2 = (bf16[3,160,128]{2,1,0:T(8,128)(2,1)}, bf16[3,160,128]{2,1,0:T(8,128)(2,1)S(1)}, u32[]{:S(2)}, u32[]{:S(2)}) collective-permute-start(bf16[3,160,128]{2,1,0:T(8,128)(2,1)} %get-tuple-element.34), channel_id=1, source_target_pairs={{0,8},{4,12},{8,0},{12,4},{16,24},{20,28},{24,16},{28,20},{32,40},... | collective-permute-start | bytes 368648 | tf_op jit(solution)/shard_map/ppermute | solution.py:30
  19.9 9.2 %collective-permute-start.3 = (bf16[3,160,128]{2,1,0:T(8,128)(2,1)}, bf16[3,160,128]{2,1,0:T(8,128)(2,1)S(1)}, u32[]{:S(2)}, u32[]{:S(2)}) collective-permute-start(bf16[3,160,128]{2,1,0:T(8,128)(2,1)} %get-tuple-element.35), channel_id=1, source_target_pairs={{0,12},{4,0},{8,4},{12,8},{16,28},{20,16},{24,20},{28,24},{32,44},... | collective-permute-start | bytes 368648 | tf_op jit(solution)/shard_map/ppermute | solution.py:30
  25.8 11.2 %copy-start.7 = (bf16[3,160,128]{2,1,0:T(8,128)(2,1)}, bf16[3,160,128]{2,1,0:T(8,128)(2,1)S(1)}, u32[]{:S(2)}) copy-start(bf16[3,160,128]{2,1,0:T(8,128)(2,1)S(1)} %collective-permute-done.1.q1) | copy-start | bytes 368644
  29.1 7.8 %copy-start.8 = (bf16[3,160,128]{2,1,0:T(8,128)(2,1)}, bf16[3,160,128]{2,1,0:T(8,128)(2,1)S(1)}, u32[]{:S(2)}) copy-start(bf16[3,160,128]{2,1,0:T(8,128)(2,1)S(1)} %collective-permute-done.2.q2) | copy-start | bytes 368644
  29.1 7.9 %copy-start.9 = (bf16[3,160,128]{2,1,0:T(8,128)(2,1)}, bf16[3,160,128]{2,1,0:T(8,128)(2,1)S(1)}, u32[]{:S(2)}) copy-start(bf16[3,160,128]{2,1,0:T(8,128)(2,1)S(1)} %collective-permute-done.3.q3) | copy-start | bytes 368644
  29.1 54.4 %all-to-all-start = ((bf16[16,3,160,128]{3,2,1,0:T(8,128)(2,1)}), bf16[16,3,160,128]{3,2,1,0:T(8,128)(2,1)}, u32[]{:S(2)}, u32[]{:S(2)}) async-start(bf16[16,3,160,128]{3,2,1,0:T(8,128)(2,1)} %get-tuple-element.36), calls=%async_computation | async-start | bytes 3932160 | tf_op jit(solution)/shard_map/all_to_all | solution.py:293
  37.0 60.1 %copy-start.1 = (bf16[2,640,128]{2,1,0:T(8,128)(2,1)}, bf16[2,640,128]{2,1,0:T(8,128)(2,1)S(1)}, u32[]{:S(2)}) copy-start(bf16[2,640,128]{2,1,0:T(8,128)(2,1)S(1)} %pad_maximum_fusion.s0) | copy-start | bytes 983044
  37.0 60.1 %collective-permute-start.7 = (bf16[2,640,128]{2,1,0:T(8,128)(2,1)S(1)}, bf16[2,640,128]{2,1,0:T(8,128)(2,1)}, u32[]{:S(2)}, u32[]{:S(2)}) collective-permute-start(bf16[2,640,128]{2,1,0:T(8,128)(2,1)S(1)} %pad_maximum_fusion.s0), channel_id=1, source_target_pairs={{0,16},{4,20},{8,24},{12,28},{16,32},{20,36},{24,40},{28,44},{32,4... | collective-permute-start | bytes 983048 | tf_op jit(solution)/shard_map/ppermute | solution.py:35
  38.9 63.0 %collective-permute-start.8 = (bf16[2,640,128]{2,1,0:T(8,128)(2,1)S(1)}, bf16[2,640,128]{2,1,0:T(8,128)(2,1)}, u32[]{:S(2)}, u32[]{:S(2)}) collective-permute-start(bf16[2,640,128]{2,1,0:T(8,128)(2,1)S(1)} %pad_maximum_fusion.s0), channel_id=1, source_target_pairs={{0,32},{4,36},{8,40},{12,44},{16,48},{20,52},{24,56},{28,60},{32,0... | collective-permute-start | bytes 983048 | tf_op jit(solution)/shard_map/ppermute | solution.py:35
  41.6 61.2 %collective-permute-start.9 = (bf16[2,640,128]{2,1,0:T(8,128)(2,1)S(1)}, bf16[2,640,128]{2,1,0:T(8,128)(2,1)}, u32[]{:S(2)}, u32[]{:S(2)}) collective-permute-start(bf16[2,640,128]{2,1,0:T(8,128)(2,1)S(1)} %pad_maximum_fusion.s0), channel_id=1, source_target_pairs={{0,48},{4,52},{8,56},{12,60},{16,0},{20,4},{24,8},{28,12},{32,16},... | collective-permute-start | bytes 983048 | tf_op jit(solution)/shard_map/ppermute | solution.py:35
  93.6 12.4 %collective-permute-start.4 = (bf16[640,128]{1,0:T(8,128)(2,1)}, bf16[640,128]{1,0:T(8,128)(2,1)S(1)}, u32[]{:S(2)}, u32[]{:S(2)}) collective-permute-start(bf16[640,128]{1,0:T(8,128)(2,1)} %get-tuple-element.38), channel_id=1, source_target_pairs={{0,48},{4,52},{8,56},{12,60},{16,0},{20,4},{24,8},{28,12},{32,16},... | collective-permute-start | bytes 491528 | tf_op jit(solution)/shard_map/ppermute | solution.py:35
  94.5 12.3 %collective-permute-start.5 = (bf16[640,128]{1,0:T(8,128)(2,1)}, bf16[640,128]{1,0:T(8,128)(2,1)S(1)}, u32[]{:S(2)}, u32[]{:S(2)}) collective-permute-start(bf16[640,128]{1,0:T(8,128)(2,1)} %get-tuple-element.39), channel_id=1, source_target_pairs={{0,32},{4,36},{8,40},{12,44},{16,48},{20,52},{24,56},{28,60},{32,0... | collective-permute-start | bytes 491528 | tf_op jit(solution)/shard_map/ppermute | solution.py:35
  97.1 21.2 %collective-permute-start.10 = (bf16[160,640]{1,0:T(8,128)(2,1)}, bf16[160,640]{1,0:T(8,128)(2,1)S(1)}, u32[]{:S(2)}, u32[]{:S(2)}) collective-permute-start(bf16[160,640]{1,0:T(8,128)(2,1)} %get-tuple-element.41), channel_id=1, source_target_pairs={{0,196},{4,200},{8,204},{12,192},{16,212},{20,216},{24,220},{28,20... | collective-permute-start | bytes 614408 | tf_op jit(solution)/shard_map/ppermute | solution.py:64
  102.0 16.4 %collective-permute-start.11 = (bf16[160,640]{1,0:T(8,128)(2,1)}, bf16[160,640]{1,0:T(8,128)(2,1)S(1)}, u32[]{:S(2)}, u32[]{:S(2)}) collective-permute-start(bf16[160,640]{1,0:T(8,128)(2,1)} %get-tuple-element.42), channel_id=1, source_target_pairs={{0,200},{4,204},{8,192},{12,196},{16,216},{20,220},{24,208},{28,21... | collective-permute-start | bytes 614408 | tf_op jit(solution)/shard_map/ppermute | solution.py:64
  102.8 15.6 %collective-permute-start.16 = (bf16[160,640]{1,0:T(8,128)(2,1)}, bf16[160,640]{1,0:T(8,128)(2,1)S(1)}, u32[]{:S(2)}, u32[]{:S(2)}) collective-permute-start(bf16[160,640]{1,0:T(8,128)(2,1)} %get-tuple-element.57), channel_id=1, source_target_pairs={{0,192},{4,196},{8,200},{12,204},{16,208},{20,212},{24,216},{28,22... | collective-permute-start | bytes 614408 | tf_op jit(solution)/shard_map/ppermute | solution.py:64
  106.0 14.8 %copy-start.3 = (bf16[640,128]{1,0:T(8,128)(2,1)}, bf16[640,128]{1,0:T(8,128)(2,1)S(1)}, u32[]{:S(2)}) copy-start(bf16[640,128]{1,0:T(8,128)(2,1)S(1)} %collective-permute-done.4.refs_1_) | copy-start | bytes 491524
  106.0 14.8 %collective-permute-start.17 = (bf16[160,640]{1,0:T(8,128)(2,1)}, bf16[160,640]{1,0:T(8,128)(2,1)S(1)}, u32[]{:S(2)}, u32[]{:S(2)}) collective-permute-start(bf16[160,640]{1,0:T(8,128)(2,1)} %get-tuple-element.59), channel_id=1, source_target_pairs={{0,204},{4,192},{8,196},{12,200},{16,220},{20,208},{24,212},{28,21... | collective-permute-start | bytes 614408 | tf_op jit(solution)/shard_map/ppermute | solution.py:64
  106.8 14.1 %copy-start.4 = (bf16[640,128]{1,0:T(8,128)(2,1)}, bf16[640,128]{1,0:T(8,128)(2,1)S(1)}, u32[]{:S(2)}) copy-start(bf16[640,128]{1,0:T(8,128)(2,1)S(1)} %collective-permute-done.5.refs_2_) | copy-start | bytes 491524
  106.8 11.6 %collective-permute-start.6 = (bf16[640,128]{1,0:T(8,128)(2,1)}, bf16[640,128]{1,0:T(8,128)(2,1)S(1)}, u32[]{:S(2)}, u32[]{:S(2)}) collective-permute-start(bf16[640,128]{1,0:T(8,128)(2,1)} %get-tuple-element.40), channel_id=1, source_target_pairs={{0,16},{4,20},{8,24},{12,28},{16,32},{20,36},{24,40},{28,44},{32,4... | collective-permute-start | bytes 491528 | tf_op jit(solution)/shard_map/ppermute | solution.py:35
  124.1 22.4 %all-to-all-start.1 = ((f32[64,8,128]{2,1,0:T(8,128)}), f32[64,8,128]{2,1,0:T(8,128)S(1)}, u32[]{:S(2)}, u32[]{:S(2)}) async-start(f32[64,8,128]{2,1,0:T(8,128)} %shard_map.129), calls=%async_computation.1 | async-start | bytes 524288 | tf_op jit(solution)/shard_map/all_to_all | solution.py:333
  137.9 10.9 %collective-permute-start.12 = (bf16[160,640]{1,0:T(8,128)(2,1)}, bf16[160,640]{1,0:T(8,128)(2,1)S(1)}, u32[]{:S(2)}, u32[]{:S(2)}) collective-permute-start(bf16[160,640]{1,0:T(8,128)(2,1)} %get-tuple-element.44), channel_id=1, source_target_pairs={{0,64},{4,68},{8,72},{12,76},{16,80},{20,84},{24,88},{28,92},{32,9... | collective-permute-start | bytes 614408 | tf_op jit(solution)/shard_map/ppermute | solution.py:60
  137.9 22.8 %collective-permute-start.13 = (bf16[160,640]{1,0:T(8,128)(2,1)}, bf16[160,640]{1,0:T(8,128)(2,1)S(1)}, u32[]{:S(2)}, u32[]{:S(2)}) collective-permute-start(bf16[160,640]{1,0:T(8,128)(2,1)} %get-tuple-element.45), channel_id=1, source_target_pairs={{0,76},{4,64},{8,68},{12,72},{16,92},{20,80},{24,84},{28,88},{32,1... | collective-permute-start | bytes 614408 | tf_op jit(solution)/shard_map/ppermute | solution.py:60
  143.5 19.6 %collective-permute-start.14 = (bf16[160,640]{1,0:T(8,128)(2,1)}, bf16[160,640]{1,0:T(8,128)(2,1)S(1)}, u32[]{:S(2)}, u32[]{:S(2)}) collective-permute-start(bf16[160,640]{1,0:T(8,128)(2,1)} %get-tuple-element.46), channel_id=1, source_target_pairs={{0,72},{4,76},{8,64},{12,68},{16,88},{20,92},{24,80},{28,84},{32,1... | collective-permute-start | bytes 614408 | tf_op jit(solution)/shard_map/ppermute | solution.py:60
  143.7 19.4 %collective-permute-start.15 = (bf16[160,640]{1,0:T(8,128)(2,1)}, bf16[160,640]{1,0:T(8,128)(2,1)}, u32[]{:S(2)}, u32[]{:S(2)}) collective-permute-start(bf16[160,640]{1,0:T(8,128)(2,1)} %get-tuple-element.47), channel_id=1, source_target_pairs={{0,68},{4,72},{8,76},{12,64},{16,84},{20,88},{24,92},{28,80},{32,1... | collective-permute-start | bytes 614408 | tf_op jit(solution)/shard_map/ppermute | solution.py:60
  148.9 17.2 %collective-permute-start.18 = (f32[4,2560]{1,0:T(4,128)}, f32[4,2560]{1,0:T(4,128)S(1)}, u32[]{:S(2)}, u32[]{:S(2)}) collective-permute-start(f32[4,2560]{1,0:T(4,128)} %shard_map.130), channel_id=1, source_target_pairs={{0,64},{64,128},{128,192},{192,0},{1,65},{65,129},{129,193},{193,1... | collective-permute-start | bytes 122888 | tf_op jit(solution)/shard_map/ppermute | solution.py:340
  148.9 14.3 %copy-start.10 = (bf16[160,640]{1,0:T(8,128)(2,1)}, bf16[160,640]{1,0:T(8,128)(2,1)S(1)}, u32[]{:S(2)}) copy-start(bf16[160,640]{1,0:T(8,128)(2,1)S(1)} %collective-permute-done.12.a0) | copy-start | bytes 614404
  (9 other events, 15.1 us)
